TPU v7x, 32 devices: a whole 2x2x4 slice. The times are simulated.
32 devices in a mesh: own: 16 (over z, y, core), dp: 2 (over x).
Axes of the slice: x: 2, y: 2, z: 4, core: 2. Of those that a mesh axis runs over, the one named last changes fastest.
Arguments:
- tokens: bfloat16 [16, 1024, 768], P('own', 'dp'), may hold values from -6 to 6
- tie_vector: int32 [3], replicated, may hold values from 0 to 1, as said below
- qkv_weight: bfloat16 [2, 768, 2304], P(None, 'own'), may hold values from -0.21875 to 0.21875
- out_weight: bfloat16 [2, 768, 768], P(None, 'own'), may hold values from -0.875 to 0.875
- fc_weight: bfloat16 [2, 768, 3072], P(None, 'own'), may hold values from -0.21875 to 0.21875
- proj_weight: bfloat16 [2, 3072, 768], P(None, 'own'), may hold values from -0.109375 to 0.109375
- norm_gains: bfloat16 [2, 2, 768], P(None, None, 'own'), may hold values from 0.25 to 1.75
- norm_shifts: bfloat16 [2, 2, 768], P(None, None, 'own'), may hold values from -1.5 to 1.5
- bias_model: bfloat16 [2, 4, 768], P(None, None, 'own'), may hold values from -1.5 to 1.5
- bias_hidden: bfloat16 [2, 3072], P(None, 'own'), may hold values from -2.5 to 2.5
- cotangent: bfloat16 [16, 1024, 768], P('own', 'dp'), may hold values from -6 to 6
Outputs:
- output: bfloat16 [16, 1024, 768], P('own', 'dp')
- input_grad: bfloat16 [16, 1024, 768], P('own', 'dp')
- qkv_grad: float32 [2, 768, 2304], P(None, 'own')
- out_grad: float32 [2, 768, 768], P(None, 'own')
- fc_grad: float32 [2, 768, 3072], P(None, 'own')
- proj_grad: float32 [2, 3072, 768], P(None, 'own')
- gains_grad: float32 [2, 2, 768], P(None, None, 'own')
- shifts_grad: float32 [2, 2, 768], P(None, None, 'own')
- bias_model_grad: float32 [2, 4, 768], P(None, None, 'own')
- bias_hidden_grad: float32 [2, 3072], P(None, 'own')
Inputs may be any that keep to these rules, and one draw needn't show every extreme that they name: `tie_vector`: each of the 2 sources is read by at least one of the 3 layers.
All inputs are finite; a program needn't handle non-finite values.
Results may differ from a plain program's by a relative error of at most 0.018.
Values may be sent and summed in bfloat16 or wider, within the bound.
No kernel may reach another device: no remote copies, remote signals or barrier semaphores. Data moves between devices by JAX's collectives and lax.ppermute only.
A program may use at most 448 MiB of HBM per device.

v0:
```python
import jax
import jax.numpy as jnp
from jax import lax
from jax.sharding import PartitionSpec as P

D = 768
HEADS = 12
USES = 3


NORM_EPS = 1e-05


def norm_apply(values_in, gain_vec, shift_vec):
    centre = jnp.mean(values_in, -1, keepdims=True)
    centred = values_in - centre
    spread = jnp.mean(centred * centred, -1, keepdims=True)
    return centred * lax.rsqrt(spread + NORM_EPS) * gain_vec + shift_vec


def gelu_apply(pre_act):
    return (
        0.5
        * pre_act
        * (1.0 + jnp.tanh(0.7978845608028654 * (pre_act + 0.044715 * pre_act * pre_act * pre_act)))
    )


def pick_source(tables, source):
    return tuple((lax.dynamic_index_in_dim(table, source, 0, keepdims=False) for table in tables))


def fetch_forward(tables, source):
    qkv_w, out_w, fc_w, proj_w, gains, shifts, bias_m, bias_h = pick_source(tables, source)
    return (
        lax.all_gather(qkv_w, "own", axis=0, tiled=True),
        lax.all_gather(out_w, "own", axis=0, tiled=True),
        lax.all_gather(fc_w, "own", axis=0, tiled=True),
        lax.all_gather(proj_w, "own", axis=0, tiled=True),
        lax.all_gather(gains, "own", axis=1, tiled=True),
        lax.all_gather(shifts, "own", axis=1, tiled=True),
        lax.all_gather(bias_m, "own", axis=1, tiled=True),
        lax.all_gather(bias_h, "own", axis=0, tiled=True),
    )


def fetch_backward(tables, source):
    qkv_w, out_w, fc_w, proj_w, gains, shifts, bias_m, bias_h = pick_source(tables, source)
    return (
        lax.all_gather(qkv_w, "own", axis=0, tiled=True),
        lax.all_gather(out_w, "own", axis=0, tiled=True),
        lax.all_gather(fc_w, "own", axis=0, tiled=True),
        lax.all_gather(proj_w, "own", axis=0, tiled=True),
        lax.all_gather(gains, "own", axis=1, tiled=True),
        lax.all_gather(shifts, "own", axis=1, tiled=True),
        lax.all_gather(bias_m, "own", axis=1, tiled=True),
        lax.all_gather(bias_h, "own", axis=0, tiled=True),
    )


def reduce_grads(grads):
    g_qkv, g_out, g_fc, g_proj, g_gain, g_shift, g_bmodel, g_bhidden = grads
    shares = (
        lax.psum_scatter(g_qkv.astype(jnp.bfloat16), "own", scatter_dimension=0, tiled=True).astype(
            jnp.float32
        ),
        lax.psum_scatter(g_out.astype(jnp.bfloat16), "own", scatter_dimension=0, tiled=True).astype(
            jnp.float32
        ),
        lax.psum_scatter(g_fc.astype(jnp.bfloat16), "own", scatter_dimension=0, tiled=True).astype(
            jnp.float32
        ),
        lax.psum_scatter(
            g_proj.astype(jnp.bfloat16), "own", scatter_dimension=0, tiled=True
        ).astype(jnp.float32),
        lax.psum_scatter(
            g_gain.astype(jnp.bfloat16), "own", scatter_dimension=1, tiled=True
        ).astype(jnp.float32),
        lax.psum_scatter(
            g_shift.astype(jnp.bfloat16), "own", scatter_dimension=1, tiled=True
        ).astype(jnp.float32),
        lax.psum_scatter(
            g_bmodel.astype(jnp.bfloat16), "own", scatter_dimension=1, tiled=True
        ).astype(jnp.float32),
        lax.psum_scatter(
            g_bhidden.astype(jnp.bfloat16), "own", scatter_dimension=0, tiled=True
        ).astype(jnp.float32),
    )
    s_qkv, s_out, s_fc, s_proj, s_gain, s_shift, s_bmodel, s_bhidden = shares
    return (
        lax.psum(s_qkv.astype(jnp.bfloat16), "dp").astype(jnp.float32),
        lax.psum(s_out.astype(jnp.bfloat16), "dp").astype(jnp.float32),
        lax.psum(s_fc.astype(jnp.bfloat16), "dp").astype(jnp.float32),
        lax.psum(s_proj.astype(jnp.bfloat16), "dp").astype(jnp.float32),
        lax.psum(s_gain.astype(jnp.bfloat16), "dp").astype(jnp.float32),
        lax.psum(s_shift.astype(jnp.bfloat16), "dp").astype(jnp.float32),
        lax.psum(s_bmodel.astype(jnp.bfloat16), "dp").astype(jnp.float32),
        lax.psum(s_bhidden.astype(jnp.bfloat16), "dp").astype(jnp.float32),
    )


def add_at(tables, additions, source):
    return tuple(
        (
            lax.dynamic_update_index_in_dim(
                table, lax.dynamic_index_in_dim(table, source, 0, keepdims=False) + extra, source, 0
            )
            for table, extra in zip(tables, additions)
        )
    )


def front_half(resid, weights):
    qkv_w, out_w, fc_w, proj_w, gains, shifts, bias_m, bias_h = weights
    normed = norm_apply(resid, gains[0].astype(jnp.float32), shifts[0].astype(jnp.float32)).astype(
        jnp.bfloat16
    )
    joined = jnp.dot(normed, qkv_w, preferred_element_type=jnp.float32)
    queries = (joined[:, :D] + bias_m[0].astype(jnp.float32)).astype(jnp.bfloat16)
    keys_local = joined[:, D : 2 * D].astype(jnp.bfloat16)
    values_local = (joined[:, 2 * D :] + bias_m[1].astype(jnp.float32)).astype(jnp.bfloat16)
    return (normed, queries, keys_local, values_local)


def attend(queries, both_full, query_pos):
    seq_count = both_full.shape[0]
    length = both_full.shape[1]
    head_dim = D // HEADS
    scale = float(head_dim) ** (-0.5)
    q_heads = queries.reshape(seq_count, -1, HEADS, head_dim)
    k_heads = both_full[..., :D].reshape(seq_count, length, HEADS, head_dim)
    v_heads = both_full[..., D:].reshape(seq_count, length, HEADS, head_dim)
    scores = (
        jnp.einsum("bqhd,bkhd->bhqk", q_heads, k_heads, preferred_element_type=jnp.float32) * scale
    )
    allowed = jnp.arange(length)[None, :] <= query_pos[:, None]
    row_top = jnp.max(jnp.where(allowed, scores, -1e30), -1, keepdims=True)
    expo_rows = jnp.where(allowed, jnp.exp(scores - row_top), 0.0)
    probs = expo_rows / jnp.sum(expo_rows, -1, keepdims=True)
    attn_probs = probs.astype(jnp.bfloat16)
    mixed = jnp.einsum("bhqk,bkhd->bqhd", attn_probs, v_heads, preferred_element_type=jnp.float32)
    mixed = mixed.reshape(queries.shape[0], D).astype(jnp.bfloat16)
    return (probs, attn_probs, mixed, q_heads, k_heads, v_heads)


def back_half(resid, mixed, weights):
    qkv_w, out_w, fc_w, proj_w, gains, shifts, bias_m, bias_h = weights
    middle = (
        resid
        + jnp.dot(mixed, out_w, preferred_element_type=jnp.float32)
        + bias_m[2].astype(jnp.float32)
    )
    normed_mlp = norm_apply(
        middle, gains[1].astype(jnp.float32), shifts[1].astype(jnp.float32)
    ).astype(jnp.bfloat16)
    pre_act = jnp.dot(normed_mlp, fc_w, preferred_element_type=jnp.float32) + bias_h.astype(
        jnp.float32
    )
    activated = gelu_apply(pre_act).astype(jnp.bfloat16)
    result = (
        middle
        + jnp.dot(activated, proj_w, preferred_element_type=jnp.float32)
        + bias_m[3].astype(jnp.float32)
    )
    return (middle, normed_mlp, pre_act, activated, result)


def per_device(
    tokens,
    tie_vector,
    qkv_weight,
    out_weight,
    fc_weight,
    proj_weight,
    norm_gains,
    norm_shifts,
    bias_model,
    bias_hidden,
    cotangent,
):
    seq_count, pos_dev, width = tokens.shape
    rows = seq_count * pos_dev
    scale = float(D // HEADS) ** (-0.5)
    tables = (
        qkv_weight,
        out_weight,
        fc_weight,
        proj_weight,
        norm_gains,
        norm_shifts,
        bias_model,
        bias_hidden,
    )
    query_pos = lax.axis_index("dp") * pos_dev + jnp.arange(pos_dev)
    resid = tokens.reshape(rows, width).astype(jnp.float32)
    saved = []
    for layer_index in range(USES):
        source = tie_vector[layer_index]
        weights = fetch_forward(tables, source)
        normed, queries, keys_local, values_local = front_half(resid, weights)
        both = jnp.concatenate([keys_local, values_local], -1).reshape(seq_count, pos_dev, 2 * D)
        both_full = lax.all_gather(both, "dp", axis=1, tiled=True)
        probs, attn_probs, mixed, q_heads, k_heads, v_heads = attend(queries, both_full, query_pos)
        saved.append(resid)
        resid = back_half(resid, mixed, weights)[4]
    output = resid.astype(jnp.bfloat16).reshape(tokens.shape)
    grads_out = tuple((jnp.zeros(table.shape, jnp.float32) for table in tables))
    dres = cotangent.reshape(rows, width).astype(jnp.float32)
    for layer_index in reversed(range(USES)):
        source = tie_vector[layer_index]
        weights = fetch_backward(tables, source)
        qkv_w, out_w, fc_w, proj_w, gains, shifts, bias_m, bias_h = weights
        resid_in = saved[layer_index]
        normed, queries, keys_local, values_local = front_half(resid_in, weights)
        both = jnp.concatenate([keys_local, values_local], -1).reshape(seq_count, pos_dev, 2 * D)
        both_full = lax.all_gather(both, "dp", axis=1, tiled=True)
        probs, attn_probs, mixed, q_heads, k_heads, v_heads = attend(queries, both_full, query_pos)
        middle, normed_mlp, pre_act, activated, result = back_half(resid_in, mixed, weights)
        d_branch = dres.astype(jnp.bfloat16)
        g_proj = jnp.dot(activated.T, d_branch, preferred_element_type=jnp.float32)
        g_bias3 = jnp.sum(d_branch.astype(jnp.float32), 0)
        d_act = jnp.dot(d_branch, proj_w.T, preferred_element_type=jnp.float32)
        _, gelu_pull = jax.vjp(gelu_apply, pre_act)
        d_pre = gelu_pull(d_act)[0].astype(jnp.bfloat16)
        g_fc = jnp.dot(normed_mlp.T, d_pre, preferred_element_type=jnp.float32)
        g_bhidden = jnp.sum(d_pre.astype(jnp.float32), 0)
        d_normed_mlp = jnp.dot(d_pre, fc_w.T, preferred_element_type=jnp.float32)
        _, norm_pull_mlp = jax.vjp(
            norm_apply, middle, gains[1].astype(jnp.float32), shifts[1].astype(jnp.float32)
        )
        d_mid_norm, g_gain2, g_shift2 = norm_pull_mlp(d_normed_mlp)
        d_middle = dres + d_mid_norm
        d_attn = d_middle.astype(jnp.bfloat16)
        g_out = jnp.dot(mixed.T, d_attn, preferred_element_type=jnp.float32)
        g_bias2 = jnp.sum(d_attn.astype(jnp.float32), 0)
        d_mixed = jnp.dot(d_attn, out_w.T, preferred_element_type=jnp.float32).astype(jnp.bfloat16)
        d_mixed = d_mixed.reshape(q_heads.shape)
        d_probs = jnp.einsum(
            "bqhd,bkhd->bhqk", d_mixed, v_heads, preferred_element_type=jnp.float32
        )
        d_scores = (probs * (d_probs - jnp.sum(d_probs * probs, -1, keepdims=True))).astype(
            jnp.bfloat16
        )
        d_queries = (
            (
                jnp.einsum("bhqk,bkhd->bqhd", d_scores, k_heads, preferred_element_type=jnp.float32)
                * scale
            )
            .reshape(rows, D)
            .astype(jnp.bfloat16)
        )
        d_keys_part = (
            jnp.einsum("bhqk,bqhd->bkhd", d_scores, q_heads, preferred_element_type=jnp.float32)
            * scale
        ).reshape(seq_count, -1, D)
        d_values_part = jnp.einsum(
            "bhqk,bqhd->bkhd", attn_probs, d_mixed, preferred_element_type=jnp.float32
        ).reshape(seq_count, -1, D)
        d_keys, d_values = (
            lax.psum_scatter(
                d_keys_part.astype(jnp.bfloat16), "dp", scatter_dimension=1, tiled=True
            ).astype(jnp.float32),
            lax.psum_scatter(
                d_values_part.astype(jnp.bfloat16), "dp", scatter_dimension=1, tiled=True
            ).astype(jnp.float32),
        )
        d_keys = d_keys.reshape(rows, D).astype(jnp.bfloat16)
        d_values = d_values.reshape(rows, D).astype(jnp.bfloat16)
        g_bias0 = jnp.sum(d_queries.astype(jnp.float32), 0)
        g_bias1 = jnp.sum(d_values.astype(jnp.float32), 0)
        d_joined = jnp.concatenate([d_queries, d_keys, d_values], -1)
        g_qkv = jnp.dot(normed.T, d_joined, preferred_element_type=jnp.float32)
        d_normed = jnp.dot(d_joined, qkv_w.T, preferred_element_type=jnp.float32)
        _, norm_pull_attn = jax.vjp(
            norm_apply, resid_in, gains[0].astype(jnp.float32), shifts[0].astype(jnp.float32)
        )
        d_in_norm, g_gain1, g_shift1 = norm_pull_attn(d_normed)
        dres = d_middle + d_in_norm
        local_grads = (
            g_qkv,
            g_out,
            g_fc,
            g_proj,
            jnp.stack([g_gain1, g_gain2]),
            jnp.stack([g_shift1, g_shift2]),
            jnp.stack([g_bias0, g_bias1, g_bias2, g_bias3]),
            g_bhidden,
        )
        grads_out = add_at(grads_out, reduce_grads(local_grads), source)
    input_grad = dres.astype(jnp.bfloat16).reshape(tokens.shape)
    return (
        output,
        input_grad,
        grads_out[0],
        grads_out[1],
        grads_out[2],
        grads_out[3],
        grads_out[4],
        grads_out[5],
        grads_out[6],
        grads_out[7],
    )


def solution(mesh):
    return jax.shard_map(
        per_device,
        mesh=mesh,
        in_specs=(
            P("own", "dp", None),
            P(),
            P(None, "own", None),
            P(None, "own", None),
            P(None, "own", None),
            P(None, "own", None),
            P(None, None, "own"),
            P(None, None, "own"),
            P(None, None, "own"),
            P(None, "own"),
            P("own", "dp", None),
        ),
        out_specs=(
            P("own", "dp", None),
            P("own", "dp", None),
            P(None, "own", None),
            P(None, "own", None),
            P(None, "own", None),
            P(None, "own", None),
            P(None, None, "own"),
            P(None, None, "own"),
            P(None, None, "own"),
            P(None, "own"),
        ),
        check_vma=False,
    )
```

profile of v0, /device:TPU:0, one launch (start us, length us, event | category | flops | bytes accessed | tf_op | source)
XLA Modules:
  0.0 2596.1 jit_solution(2012745115977519370)
XLA Ops:
  18.4 25.3 all-gather
  62.7 20.6 all-gather.3
  116.2 57.9 %all-reduce.7 = (bf16[3072]{0:T(1024)(128)(2,1)S(1)}, bf16[3072]{0:T(1024)(128)(2,1)S(1)}, bf16[3072]{0:T(1024)(128)(2,1)}) all-reduce(bf16[3072]{0:T(1024)(128)(2,1)S(1)} %dynamic-update-slice, bf16[3072]{0:T(1024)(128)(2,1)S(1)} %dynamic-update-slice.1, bf16[3072]{0:T(1024)(128)(2,1)S(1)} %dynamic-update-slice.2), channel_id=9, replica_groups=mesh['own'=16,'dp'=2] {'own'}, use_global_device_ids=true, to_apply=%add | all-reduce | flops 9216 | bytes 36864
  198.2 21.4 all-gather.10
  318.5 37.8 %all-gather.53.cloned.1.call-done = bf16[1,768,2304]{2,1,0:T(8,128)(2,1)} async-done(((bf16[1,48,2304]{2,1,0:T(8,128)(2,1)}), bf16[1,768,2304]{2,1,0:T(8,128)(2,1)}) %all-gather.53.cloned.1.call-update) | async-done | bytes 3538960 | tf_op jit(solution)/shard_map/all_gather | solution.py:36
  414.2 20.7 all-gather.21
  509.3 47.7 %all-gather.61.cloned.1.call-done = bf16[1,3072,768]{2,1,0:T(8,128)(2,1)} async-done(((bf16[1,192,768]{2,1,0:T(8,128)(2,1)}), bf16[1,3072,768]{2,1,0:T(8,128)(2,1)}) %all-gather.61.cloned.1.call-update) | async-done | bytes 4718608 | tf_op jit(solution)/shard_map/all_gather | solution.py:39
  566.1 39.0 %all-gather.63.cloned.1.call-done = bf16[1,768,2304]{2,1,0:T(8,128)(2,1)} async-done(((bf16[1,48,2304]{2,1,0:T(8,128)(2,1)}), bf16[1,768,2304]{2,1,0:T(8,128)(2,1)}) %all-gather.63.cloned.1.call-update) | async-done | bytes 3538960 | tf_op jit(solution)/shard_map/all_gather | solution.py:36
  614.1 40.9 %all-gather.65.cloned.1.call-done = bf16[1024,1536]{1,0:T(8,128)(2,1)} async-done(((bf16[512,1536]{1,0:T(8,128)(2,1)}), bf16[1024,1536]{1,0:T(8,128)(2,1)}) %all-gather.65.cloned.1.call-update) | async-done | bytes 3145744 | tf_op jit(solution)/shard_map/all_gather | solution.py:202
  698.4 51.7 %all-gather.69.cloned.1.call-done = bf16[1,768,3072]{2,1,0:T(8,128)(2,1)} async-done(((bf16[1,48,3072]{2,1,0:T(8,128)(2,1)}), bf16[1,768,3072]{2,1,0:T(8,128)(2,1)}) %all-gather.69.cloned.1.call-update) | async-done | bytes 4718608 | tf_op jit(solution)/shard_map/all_gather | solution.py:38
  757.3 47.6 %all-gather.71.cloned.1.call-done = bf16[1,3072,768]{2,1,0:T(8,128)(2,1)} async-done(((bf16[1,192,768]{2,1,0:T(8,128)(2,1)}), bf16[1,3072,768]{2,1,0:T(8,128)(2,1)}) %all-gather.71.cloned.1.call-update) | async-done | bytes 4718608 | tf_op jit(solution)/shard_map/all_gather | solution.py:39
  994.3 22.3 reduce-scatter.50.cloned.1.call-done
  1243.2 55.2 %reduce-scatter.94.cloned.1.call-done = bf16[48,4]{1,0:T(8,128)(2,1)} async-done(((bf16[768,4]{1,0:T(8,128)(2,1)}), bf16[48,4]{1,0:T(8,128)(2,1)}) %reduce-scatter.94.cloned.1.call-update) | async-done | bytes 400
  1299.2 58.1 %all-reduce.6 = (bf16[3072]{0:T(1024)(128)(2,1)S(1)}, bf16[3072]{0:T(1024)(128)(2,1)S(1)}, bf16[3072]{0:T(1024)(128)(2,1)S(1)}) all-reduce(bf16[3072]{0:T(1024)(128)(2,1)S(1)} %copy-done.133, bf16[3072]{0:T(1024)(128)(2,1)S(1)} %copy-done.134, bf16[3072]{0:T(1024)(128)(2,1)S(1)} %copy-done.135), channel_id=56, replica_groups=mesh['own'=16,'dp'=2] {'own'}, use_global_device_ids=true, to_apply=%region_106.107.clone | all-reduce | flops 9216 | bytes 36864
  1358.3 52.3 %reduce-scatter.84.cloned.1.call-done = bf16[48,2]{1,0:T(8,128)(2,1)} async-done(((bf16[768,2]{1,0:T(8,128)(2,1)}), bf16[48,2]{1,0:T(8,128)(2,1)}) %reduce-scatter.84.cloned.1.call-update) | async-done | bytes 208
  1411.4 55.2 %reduce-scatter.96.cloned.1.call-done = bf16[48,4]{1,0:T(8,128)(2,1)} async-done(((bf16[768,4]{1,0:T(8,128)(2,1)}), bf16[48,4]{1,0:T(8,128)(2,1)}) %reduce-scatter.96.cloned.1.call-update) | async-done | bytes 400
  1470.6 52.1 %reduce-scatter.86.cloned.1.call-done = bf16[48,2]{1,0:T(8,128)(2,1)} async-done(((bf16[768,2]{1,0:T(8,128)(2,1)}), bf16[48,2]{1,0:T(8,128)(2,1)}) %reduce-scatter.86.cloned.1.call-update) | async-done | bytes 208
  1523.6 55.3 %reduce-scatter.92.cloned.1.call-done = bf16[48,2]{1,0:T(8,128)(2,1)} async-done(((bf16[768,2]{1,0:T(8,128)(2,1)}), bf16[48,2]{1,0:T(8,128)(2,1)}) %reduce-scatter.92.cloned.1.call-update) | async-done | bytes 208
  1579.7 55.2 %reduce-scatter.98.cloned.1.call-done = bf16[48,4]{1,0:T(8,128)(2,1)} async-done(((bf16[768,4]{1,0:T(8,128)(2,1)}), bf16[48,4]{1,0:T(8,128)(2,1)}) %reduce-scatter.98.cloned.1.call-update) | async-done | bytes 400
  1640.7 55.6 %reduce-scatter.64.cloned.1.call-done = bf16[48,768]{1,0:T(8,128)(2,1)} async-done(((bf16[768,768]{1,0:T(8,128)(2,1)}), bf16[48,768]{1,0:T(8,128)(2,1)}) %reduce-scatter.64.cloned.1.call-update) | async-done | bytes 73744 | tf_op jit(solution)/shard_map/reduce_scatter | solution.py:67
  1696.3 61.3 %reduce-scatter.66.cloned.1.call-done = bf16[48,768]{1,0:T(8,128)(2,1)} async-done(((bf16[768,768]{1,0:T(8,128)(2,1)}), bf16[48,768]{1,0:T(8,128)(2,1)}) %reduce-scatter.66.cloned.1.call-update) | async-done | bytes 73744 | tf_op jit(solution)/shard_map/reduce_scatter | solution.py:67
  1757.6 78.3 %reduce-scatter.70.cloned.1.call-done = bf16[48,3072]{1,0:T(8,128)(2,1)} async-done(((bf16[768,3072]{1,0:T(8,128)(2,1)}), bf16[48,3072]{1,0:T(8,128)(2,1)}) %reduce-scatter.70.cloned.1.call-update) | async-done | bytes 294928 | tf_op jit(solution)/shard_map/reduce_scatter | solution.py:70
  1835.9 79.0 %reduce-scatter.76.cloned.1.call-done = bf16[192,768]{1,0:T(8,128)(2,1)} async-done(((bf16[3072,768]{1,0:T(8,128)(2,1)}), bf16[192,768]{1,0:T(8,128)(2,1)}) %reduce-scatter.76.cloned.1.call-update) | async-done | bytes 294928 | tf_op jit(solution)/shard_map/reduce_scatter | solution.py:73
  1914.9 60.8 %reduce-scatter.68.cloned.1.call-done = bf16[48,768]{1,0:T(8,128)(2,1)} async-done(((bf16[768,768]{1,0:T(8,128)(2,1)}), bf16[48,768]{1,0:T(8,128)(2,1)}) %reduce-scatter.68.cloned.1.call-update) | async-done | bytes 73744 | tf_op jit(solution)/shard_map/reduce_scatter | solution.py:67
  1975.7 70.8 %reduce-scatter.58.cloned.1.call-done = bf16[48,2304]{1,0:T(8,128)(2,1)} async-done(((bf16[768,2304]{1,0:T(8,128)(2,1)}), bf16[48,2304]{1,0:T(8,128)(2,1)}) %reduce-scatter.58.cloned.1.call-update) | async-done | bytes 221200 | tf_op jit(solution)/shard_map/reduce_scatter | solution.py:64
  2046.5 78.2 %reduce-scatter.72.cloned.1.call-done = bf16[48,3072]{1,0:T(8,128)(2,1)} async-done(((bf16[768,3072]{1,0:T(8,128)(2,1)}), bf16[48,3072]{1,0:T(8,128)(2,1)}) %reduce-scatter.72.cloned.1.call-update) | async-done | bytes 294928 | tf_op jit(solution)/shard_map/reduce_scatter | solution.py:70
  2124.7 79.0 %reduce-scatter.78.cloned.1.call-done = bf16[192,768]{1,0:T(8,128)(2,1)} async-done(((bf16[3072,768]{1,0:T(8,128)(2,1)}), bf16[192,768]{1,0:T(8,128)(2,1)}) %reduce-scatter.78.cloned.1.call-update) | async-done | bytes 294928 | tf_op jit(solution)/shard_map/reduce_scatter | solution.py:73
  2203.7 70.8 %reduce-scatter.60.cloned.1.call-done = bf16[48,2304]{1,0:T(8,128)(2,1)} async-done(((bf16[768,2304]{1,0:T(8,128)(2,1)}), bf16[48,2304]{1,0:T(8,128)(2,1)}) %reduce-scatter.60.cloned.1.call-update) | async-done | bytes 221200 | tf_op jit(solution)/shard_map/reduce_scatter | solution.py:64
  2274.5 78.3 %reduce-scatter.74.cloned.1.call-done = bf16[48,3072]{1,0:T(8,128)(2,1)} async-done(((bf16[768,3072]{1,0:T(8,128)(2,1)}), bf16[48,3072]{1,0:T(8,128)(2,1)}) %reduce-scatter.74.cloned.1.call-update) | async-done | bytes 294928 | tf_op jit(solution)/shard_map/reduce_scatter | solution.py:70
  2352.7 79.0 %reduce-scatter.80.cloned.1.call-done = bf16[192,768]{1,0:T(8,128)(2,1)} async-done(((bf16[3072,768]{1,0:T(8,128)(2,1)}), bf16[192,768]{1,0:T(8,128)(2,1)}) %reduce-scatter.80.cloned.1.call-update) | async-done | bytes 294928 | tf_op jit(solution)/shard_map/reduce_scatter | solution.py:73
  2431.7 71.0 %reduce-scatter.62.cloned.1.call-done = bf16[48,2304]{1,0:T(8,128)(2,1)} async-done(((bf16[768,2304]{1,0:T(8,128)(2,1)}), bf16[48,2304]{1,0:T(8,128)(2,1)}) %reduce-scatter.62.cloned.1.call-update) | async-done | bytes 221200 | tf_op jit(solution)/shard_map/reduce_scatter | solution.py:64
  2503.1 78.3 %all-reduce.12.cloned.1.call-done = (bf16[1,48,2304]{2,1,0:T(8,128)(2,1)}, bf16[48,2304]{1,0:T(8,128)(2,1)}, bf16[48,2304]{1,0:T(8,128)(2,1)}, bf16[1,48,768]{2,...) async-done(((bf16[1,48,2304]{2,1,0:T(8,128)(2,1)}, ...) | async-done | bytes 2654224 | tf_op jit(solution)/shard_map/psum | solution.py:91
  (713 shorter events, 814.7 us)
Async XLA Ops:
  16.5 240.7 %all-gather.45.cloned.1.call-start = ((), (), s32[]{:S(2)}) async-start(), calls=%async_computation.46 | async-start | bytes 4718592 | tf_op jit(solution)/shard_map/all_gather | solution.py:202
  110.6 184.4 %all-gather.47.cloned.1.call-start = ((), (), s32[]{:S(2)}) async-start(), calls=%async_computation.47 | async-start | bytes 1253376 | tf_op jit(solution)/shard_map/all_gather | solution.py:37
  111.4 186.5 %all-gather.49.cloned.1.call-start = ((), (), s32[]{:S(2)}) async-start(), calls=%async_computation.48 | async-start | bytes 5013504 | tf_op jit(solution)/shard_map/all_gather | solution.py:38
  112.4 196.0 %all-gather.51.cloned.1.call-start = ((), (), s32[]{:S(2)}) async-start(), calls=%async_computation.49 | async-start | bytes 5013504 | tf_op jit(solution)/shard_map/all_gather | solution.py:39
  113.4 242.9 %all-gather.53.cloned.1.call-start = ((), (), s32[]{:S(2)}) async-start(), calls=%async_computation.50 | async-start | bytes 3760128 | tf_op jit(solution)/shard_map/all_gather | solution.py:36
  114.0 333.2 %all-gather.55.cloned.1.call-start = ((), (), s32[]{:S(2)}) async-start(), calls=%async_computation.51 | async-start | bytes 4718592 | tf_op jit(solution)/shard_map/all_gather | solution.py:202
  364.1 192.9 %all-gather.61.cloned.1.call-start = ((), (), s32[]{:S(2)}) async-start(), calls=%async_computation.54 | async-start | bytes 5013504 | tf_op jit(solution)/shard_map/all_gather | solution.py:39
  364.7 240.4 %all-gather.63.cloned.1.call-start = ((), (), s32[]{:S(2)}) async-start(), calls=%async_computation.55 | async-start | bytes 3760128 | tf_op jit(solution)/shard_map/all_gather | solution.py:36
  365.4 289.6 %all-gather.65.cloned.1.call-start = ((), (), s32[]{:S(2)}) async-start(), calls=%async_computation.56 | async-start | bytes 4718592 | tf_op jit(solution)/shard_map/all_gather | solution.py:202
  612.3 192.6 %all-gather.71.cloned.1.call-start = ((), (), s32[]{:S(2)}) async-start(), calls=%async_computation.59 | async-start | bytes 5013504 | tf_op jit(solution)/shard_map/all_gather | solution.py:39
  612.9 273.3 %reduce-scatter.48.cloned.1.call-start = ((), (), s32[]{:S(2)}) async-start(), calls=%async_computation.28 | async-start | bytes 2359296 | tf_op jit(solution)/shard_map/reduce_scatter | solution.py:263
  1098.5 143.9 %reduce-scatter.82.cloned.1.call-start = ((), (), s32[]{:S(2)}) async-start(), calls=%async_computation.60 | async-start | bytes 208896
  1100.8 197.6 %reduce-scatter.94.cloned.1.call-start = ((), (), s32[]{:S(2)}) async-start(), calls=%async_computation.66 | async-start | bytes 208896
  1101.9 255.6 %reduce-scatter.90.cloned.1.call-start = ((), (), s32[]{:S(2)}) async-start(), calls=%async_computation.64 | async-start | bytes 208896
  1112.8 297.9 %reduce-scatter.84.cloned.1.call-start = ((), (), s32[]{:S(2)}) async-start(), calls=%async_computation.61 | async-start | bytes 208896
  1115.0 351.6 %reduce-scatter.96.cloned.1.call-start = ((), (), s32[]{:S(2)}) async-start(), calls=%async_computation.67 | async-start | bytes 208896
  1116.1 406.7 %reduce-scatter.86.cloned.1.call-start = ((), (), s32[]{:S(2)}) async-start(), calls=%async_computation.62 | async-start | bytes 208896
  1135.9 443.0 %reduce-scatter.92.cloned.1.call-start = ((), (), s32[]{:S(2)}) async-start(), calls=%async_computation.65 | async-start | bytes 208896
  1138.2 496.7 %reduce-scatter.98.cloned.1.call-start = ((), (), s32[]{:S(2)}) async-start(), calls=%async_computation.68 | async-start | bytes 208896
  1139.2 557.1 %reduce-scatter.64.cloned.1.call-start = ((), (), s32[]{:S(2)}) async-start(), calls=%async_computation.36 | async-start | bytes 1253376 | tf_op jit(solution)/shard_map/reduce_scatter | solution.py:67
  1142.4 615.2 %reduce-scatter.66.cloned.1.call-start = ((), (), s32[]{:S(2)}) async-start(), calls=%async_computation.37 | async-start | bytes 1253376 | tf_op jit(solution)/shard_map/reduce_scatter | solution.py:67
  1145.7 690.2 %reduce-scatter.70.cloned.1.call-start = ((), (), s32[]{:S(2)}) async-start(), calls=%async_computation.39 | async-start | bytes 5013504 | tf_op jit(solution)/shard_map/reduce_scatter | solution.py:70
  1153.2 761.7 %reduce-scatter.76.cloned.1.call-start = ((), (), s32[]{:S(2)}) async-start(), calls=%async_computation.42 | async-start | bytes 5013504 | tf_op jit(solution)/shard_map/reduce_scatter | solution.py:73
  1162.8 812.9 %reduce-scatter.68.cloned.1.call-start = ((), (), s32[]{:S(2)}) async-start(), calls=%async_computation.38 | async-start | bytes 1253376 | tf_op jit(solution)/shard_map/reduce_scatter | solution.py:67
  1166.1 880.4 %reduce-scatter.58.cloned.1.call-start = ((), (), s32[]{:S(2)}) async-start(), calls=%async_computation.33 | async-start | bytes 3760128 | tf_op jit(solution)/shard_map/reduce_scatter | solution.py:64
  1172.6 952.0 %reduce-scatter.72.cloned.1.call-start = ((), (), s32[]{:S(2)}) async-start(), calls=%async_computation.40 | async-start | bytes 5013504 | tf_op jit(solution)/shard_map/reduce_scatter | solution.py:70
  1180.8 1022.9 %reduce-scatter.78.cloned.1.call-start = ((), (), s32[]{:S(2)}) async-start(), calls=%async_computation.43 | async-start | bytes 5013504 | tf_op jit(solution)/shard_map/reduce_scatter | solution.py:73
  1190.4 1084.1 %reduce-scatter.60.cloned.1.call-start = ((), (), s32[]{:S(2)}) async-start(), calls=%async_computation.34 | async-start | bytes 3760128 | tf_op jit(solution)/shard_map/reduce_scatter | solution.py:64
  1197.6 1155.1 %reduce-scatter.74.cloned.1.call-start = ((), (), s32[]{:S(2)}) async-start(), calls=%async_computation.41 | async-start | bytes 5013504 | tf_op jit(solution)/shard_map/reduce_scatter | solution.py:70
  1205.5 1226.3 %reduce-scatter.80.cloned.1.call-start = ((), (), s32[]{:S(2)}) async-start(), calls=%async_computation.44 | async-start | bytes 5013504 | tf_op jit(solution)/shard_map/reduce_scatter | solution.py:73
  1214.5 1288.3 %reduce-scatter.62.cloned.1.call-start = ((), (), s32[]{:S(2)}) async-start(), calls=%async_computation.35 | async-start | bytes 3760128 | tf_op jit(solution)/shard_map/reduce_scatter | solution.py:64
  1221.3 1360.1 %all-reduce.12.cloned.1.call-start = ((), (), s32[]{:S(2)}) async-start(), calls=%async_computation.69 | async-start | bytes 5308416 | tf_op jit(solution)/shard_map/psum | solution.py:91
  (179 other events, 6942.6 us)
Sparse Core Ops, SparseCore 0:
  16.6 52.5 all-gather.42
  196.6 56.5 all-gather.48
  255.9 52.3 all-gather.50
  310.5 45.7 all-gather.52
  362.7 43.9 all-gather.54
  449.9 52.3 all-gather.58
  505.0 51.9 all-gather.60
  559.3 45.7 all-gather.62
  697.8 52.3 all-gather.68
  752.9 51.9 all-gather.70
  1132.0 53.5 reduce-scatter.87
  1189.8 52.6 reduce-scatter.81
  1245.8 52.5 reduce-scatter.93
  1301.9 52.6 reduce-scatter.89
  1357.9 52.6 reduce-scatter.83
  1414.0 52.6 reduce-scatter.95
  1470.1 52.6 reduce-scatter.85
  1526.3 52.5 reduce-scatter.91
  1582.3 52.5 reduce-scatter.97
  1639.1 57.1 reduce-scatter.63
  1700.5 57.0 reduce-scatter.65
  1761.3 74.5 reduce-scatter.69
  1840.3 74.6 reduce-scatter.75
  1918.6 57.1 reduce-scatter.67
  1979.5 66.9 reduce-scatter.57
  2050.2 74.4 reduce-scatter.71
  2129.0 74.6 reduce-scatter.77
  2207.4 67.0 reduce-scatter.59
  2278.3 74.3 reduce-scatter.73
  2357.1 74.6 reduce-scatter.79
  2435.6 67.0 reduce-scatter.61
  2505.7 75.7 all-reduce.11
  (11 shorter events, 356.1 us)
where the time goes:
time: 2610 us; the launch traced here: 2600 us
  waiting for transfers between devices  1630 us (62%)
  matrix products  420 us (16%)
  blocking collectives  306 us (12%)
  other arithmetic  140 us (5%)
  local copies, waits for them, and re-layouts  73.3 us (3%)
    unnamed x52, waiting for transfers between devices  341 us
    reduce_scatter x3, waiting for transfers between devices, reduce_grads(): lax.psum_scatter(g_proj.astype(jnp.bfloat16), 'own', scatter_dimension=0,...  237 us
    reduce_scatter x3, waiting for transfers between devices, reduce_grads(): lax.psum_scatter(g_fc.astype(jnp.bfloat16), 'own', scatter_dimension=0, t...  235 us
    reduce_scatter x3, waiting for transfers between devices, reduce_grads(): lax.psum_scatter(g_qkv.astype(jnp.bfloat16), 'own', scatter_dimension=0,...  213 us
    reduce_scatter x3, waiting for transfers between devices, reduce_grads(): lax.psum_scatter(g_out.astype(jnp.bfloat16), 'own', scatter_dimension=0,...  178 us
    unnamed x2, blocking collectives  116 us
    all_gather x3, waiting for transfers between devices, fetch_forward(): lax.all_gather(proj_w, 'own', axis=0, tiled=True)  98.5 us
    psum x1, waiting for transfers between devices, reduce_grads(): lax.psum(s_qkv.astype(jnp.bfloat16), 'dp').astype(jnp.float32)  78.3 us
  transfers between devices with their start and end apart: 43, of which 32 were waited for; matrix products, arithmetic and copies ran while one was open for 17% of the time, Pallas kernels for 0%

commit v1 on v0

v1 whole, which is shorter than its diff:
```python
import functools

import jax
import jax.numpy as jnp
from jax import lax
from jax.experimental import pallas as pl
from jax.experimental.pallas import tpu as pltpu
from jax.sharding import PartitionSpec as P

D = 768
HEADS = 12
PAIRS = HEADS // 2
FF = 3072
NC = FF // D
NG = 16
GR = D // NG
PR = FF // NG
SMALL = 16
NORM_EPS = 1e-05
GELU_C = 0.7978845608028654
GELU_A = 0.044715
BF = jnp.bfloat16
F32 = jnp.float32
VMEM_LIMIT = 50 * 2**20


def dot(a, b):
    return lax.dot_general(a, b, (((1,), (0,)), ((), ())), preferred_element_type=F32)


def dot_nt(a, b):
    return lax.dot_general(a, b, (((1,), (1,)), ((), ())), preferred_element_type=F32)


def dot_tn(a, b):
    return lax.dot_general(a, b, (((0,), (0,)), ((), ())), preferred_element_type=F32)


def norm_parts(x):
    centred = x - jnp.mean(x, -1, keepdims=True)
    rstd = lax.rsqrt(jnp.mean(centred * centred, -1, keepdims=True) + NORM_EPS)
    return centred * rstd, rstd


def norm_back(xhat, rstd, gain, dy):
    dxh = dy * gain
    return rstd * (
        dxh
        - jnp.mean(dxh, -1, keepdims=True)
        - xhat * jnp.mean(dxh * xhat, -1, keepdims=True)
    )


def params_of(prm):
    return jnp.sum(prm[...].astype(F32), (0, 1))


SEL, CORE, PLANE, YPOS, ZPOS, ZLOW, ZHIGH, UPS = range(8)
COUNTS = {"a": 1, "b": 1, "a2": 2, "b4": 4}
A_ROWS, B_ROWS = 4 * GR + SMALL, NC * GR + PR


class Weights:
    def __init__(self, kinds, refs, meta):
        self.meta, self.srcs = meta, []
        for kind in kinds:
            parts = []
            for part in kind:
                parts.append((part, refs[: COUNTS[part]]))
                refs = refs[COUNTS[part] :]
            self.srcs.append(parts)

    @staticmethod
    def count(kinds):
        return sum(COUNTS[part] for kind in kinds for part in kind)

    def pair(self, refs, view, dst, sem):
        core = self.meta[CORE]
        pltpu.make_async_copy(view(refs[0]), dst.at[:, core], sem).start()
        pltpu.make_async_copy(view(refs[1]), dst.at[:, 1 - core], sem).start()

    def of_half(self, refs, half, view, dst, sem):
        mine = self.meta[PLANE] == half
        pl.when(mine)(lambda: self.pair(refs[:2], view, dst, sem))
        pl.when(jnp.logical_not(mine))(lambda: self.pair(refs[2:], view, dst, sem))

    def each(self, part, copy):
        if len(self.srcs) == 1:
            copy(*self.srcs[0][part])
        else:
            for number, parts in enumerate(self.srcs):
                pl.when(self.meta[SEL] == number)(functools.partial(copy, *parts[part]))

    def start_a(self, row, size, dst, sem):
        def copy(kind, refs):
            if kind == "a":
                pltpu.make_async_copy(rows_of(refs[0], row, size), dst, sem).start()
            else:
                self.pair(refs, lambda r: rows_of(r, row, size), dst, sem)

        self.each(0, copy)

    def start_qk(self, dst, sem):
        self.start_a(0, 2 * GR, dst, sem)

    def start_v(self, dst, sem):
        self.start_a(2 * GR, GR, dst, sem)

    def start_out(self, dst, sem):
        self.start_a(3 * GR, GR, dst, sem)

    def start_small(self, dst, sem):
        self.start_a(4 * GR, SMALL, dst, sem)

    def start_in(self, c, dst, sem):
        def copy(kind, refs):
            if kind == "b":
                view = rows_of(refs[0], A_ROWS + c * GR, GR)
                pltpu.make_async_copy(view, dst, sem).start()
            else:
                half, at = divmod(c, NC // 2)
                self.of_half(refs, half, lambda r: rows_of(r, at * GR, GR), dst, sem)

        self.each(1, copy)

    def start_proj(self, c, dst, sem):
        owners = pl.ds(c * (NG // 2 // NC), NG // 2 // NC)

        def copy(kind, refs):
            if kind == "b":
                view = rows_of(refs[0].at[owners], A_ROWS + NC * GR, PR)
                pltpu.make_async_copy(view, dst, sem).start()
                return
            size = PR // 2
            view = lambda r: rows_of(r.at[owners], NC // 2 * GR, size)
            for half in range(2):
                part = dst.at[:, :, pl.ds(half * size, size), :]
                self.of_half(refs, half, view, part, sem)

        self.each(1, copy)


def rows_of(ref, row, size):
    if len(ref.shape) == 4:
        return ref.at[:, :, pl.ds(row, size), :]
    return ref.at[:, pl.ds(row, size), :]


def landed(dst, sem):
    pltpu.make_async_copy(dst, dst, sem).wait()


def qkv_kernel(kinds, meta, resid, *rest):
    nw = Weights.count(kinds)
    weights = Weights(kinds, rest[:nw], meta)
    q_out, kv_out, wqk, wv, prm, sems = rest[nw:]
    weights.start_small(prm, sems.at[0])
    weights.start_qk(wqk, sems.at[1])
    weights.start_v(wv, sems.at[2])
    xhat, _ = norm_parts(resid[...])
    landed(prm, sems.at[0])
    par = params_of(prm)
    normed = (xhat * par[0:1] + par[2:3]).astype(BF)
    landed(wqk, sems.at[1])
    kv_out[0] = dot(normed, wqk[:, :, GR:, :].reshape(D, D)).astype(BF)
    landed(wv, sems.at[2])
    kv_out[1] = (dot(normed, wv[...].reshape(D, D)) + par[5:6]).astype(BF)
    q = (dot(normed, wqk[:, :, :GR, :].reshape(D, D)) + par[4:5]).astype(BF)
    q_out[...] = q * BF((D // HEADS) ** -0.5)


def by_head(x, first):
    return jnp.concatenate([jnp.where(first, x, 0), jnp.where(first, 0, x)], 0)


def pair_masks(half, axis):
    lane = lax.broadcasted_iota(jnp.int32, (1, 2 * D // HEADS), 1)
    shape = (2 * half, half) if axis == 0 else (half, 2 * half)
    query = lax.broadcasted_iota(jnp.int32, shape, axis)
    query = jnp.where(query >= half, query - half, query)
    key = lax.broadcasted_iota(jnp.int32, shape, 1 - axis)
    return lane < D // HEADS, key <= query


def attn_fwd_kernel(others, meta, q_ref, ko, vo, kx, vx, mixed, lse, lse_scr):
    step = pl.program_id(0)
    rows = q_ref.shape[0]
    half = rows // 2
    lanes = 2 * D // HEADS
    first, tri = pair_masks(half, 0)
    highs = [meta[UPS + t] > 0 for t in range(others)]
    q_lo, q_hi = by_head(q_ref[:half], first), by_head(q_ref[half:], first)
    ones = jnp.ones((half, 128), BF)
    wide = lambda v: jnp.concatenate([v, ones], 1)
    s_ll = jnp.where(tri, dot_nt(q_lo, ko[0, :half]), -1e30)
    s_hl = dot_nt(q_hi, ko[0, :half])
    s_hh = jnp.where(tri, dot_nt(q_hi, ko[0, half:]), -1e30)
    top = jnp.maximum(s_hl, s_hh)
    s_ho, s_x, m_x = [], [], []
    for t in range(others):
        s_ho.append(dot_nt(q_hi, kx[t, 0, :half]))
        top = jnp.maximum(top, s_ho[t])
        k_x = jnp.where(highs[t], kx[t, 0, half:], kx[t, 0, :half])
        s_x.append(dot_nt(jnp.where(highs[t], q_hi, q_lo), k_x))
        m_x.append(jnp.max(s_x[t], -1, keepdims=True))
    m_lo = jnp.max(s_ll, -1, keepdims=True)
    m_hi = jnp.max(top, -1, keepdims=True)
    for t in range(others):
        m_hi = jnp.maximum(m_hi, jnp.where(highs[t], m_x[t], -1e30))
        m_lo = jnp.maximum(m_lo, jnp.where(highs[t], -1e30, m_x[t]))
    prob = lambda s, m: jnp.exp(s - m).astype(BF)
    v_lo = wide(vo[0, :half])
    o_lo = dot(prob(s_ll, m_lo), v_lo)
    o_hi = dot(prob(s_hl, m_hi), v_lo) + dot(prob(s_hh, m_hi), wide(vo[0, half:]))
    for t in range(others):
        v_x = jnp.where(highs[t], vx[t, 0, half:], vx[t, 0, :half])
        o_x = dot(prob(s_x[t], jnp.where(highs[t], m_hi, m_lo)), wide(v_x))
        o_hi = o_hi + dot(prob(s_ho[t], m_hi), wide(vx[t, 0, :half]))
        o_hi = o_hi + jnp.where(highs[t], o_x, 0.0)
        o_lo = o_lo + jnp.where(highs[t], 0.0, o_x)
    at = lax.broadcasted_iota(jnp.int32, (1, 128), 1)
    for part, (o, m) in enumerate(((o_lo, m_lo), (o_hi, m_hi))):
        out_rows = slice(part * half, (part + 1) * half)
        total = o[:, lanes:]
        norm = o[:, :lanes] / total
        mixed[out_rows] = jnp.where(first, norm[:half], norm[half:]).astype(BF)
        log = m + jnp.log(total)
        old = jnp.where(at == 2 * step, log[:half], lse_scr[out_rows])
        lse_scr[out_rows] = jnp.where(at == 2 * step + 1, log[half:], old)

    @pl.when(step == PAIRS - 1)
    def _():
        lse[0] = jnp.transpose(lse_scr[:half])[:16]
        lse[1] = jnp.transpose(lse_scr[half:])[:16]


def mlp_kernel(kinds, meta, resid, mixed, *rest):
    nw = Weights.count(kinds)
    weights = Weights(kinds, rest[:nw], meta)
    middle, pre_out, result, ow, prm, fw, pw, nm, acc, par, sems = rest[nw:]
    weights.start_out(ow, sems.at[0])
    weights.start_small(prm, sems.at[1])
    for c in range(NC):
        weights.start_in(c, fw.at[c], sems.at[2 + c])
        weights.start_proj(c, pw.at[c], sems.at[2 + NC + c])
    landed(prm, sems.at[1])
    par[...] = params_of(prm)
    landed(ow, sems.at[0])
    mid = resid[...] + dot(mixed[...], ow[...].reshape(D, D)) + par[6:7]
    middle[...] = mid
    xhat, _ = norm_parts(mid)
    nm[...] = (xhat * par[1:2] + par[3:4]).astype(BF)
    acc[...] = mid + par[7:8]

    def chunk(c, carry):
        landed(fw.at[c], sems.at[2 + c])
        pre = dot(nm[...], fw[c].reshape(D, D)) + par[pl.ds(8 + c, 1), :]
        pre_out[c] = pre.astype(BF)
        act = 0.5 * pre * (1.0 + jnp.tanh(GELU_C * (pre + GELU_A * pre * pre * pre)))
        landed(pw.at[c], sems.at[2 + NC + c])
        acc[...] += dot(act.astype(BF), pw[c].reshape(D, D))
        return carry

    lax.fori_loop(0, NC, chunk, 0)
    result[...] = acc[...]


def sort_terms(mode, keep, term, prev):
    if mode == 0:
        return (term,)
    if mode == 2:
        return (term + prev.astype(F32),)
    prev = prev.astype(F32)
    mine, old = keep
    return (mine * term + old * prev, (1.0 - mine) * term + (1.0 - old) * prev)


def to_cores(buf, mine, other, core, sem_mine, sem_other):
    return [
        pltpu.make_async_copy(buf.at[:, core], mine, sem_mine),
        pltpu.make_async_copy(buf.at[:, 1 - core], other, sem_other),
    ]


def mlp_back_kernel(kinds, mode, meta, keep_ref, dres, mid, pre, mixed, *rest):
    nw = Weights.count(kinds)
    weights = Weights(kinds, rest[:nw], meta)
    rest = rest[nw:]
    prev_b, prev_o = rest[:2] if mode else (None, None)
    rest = rest[2:] if mode else rest
    nout = 2 if mode == 1 else 1
    d_middle, d_mixed, dt, small = rest[:4]
    rest = rest[4:]
    done = mode > 0
    if done:
        done_mine, done_other, done_o = rest[:3]
        rest = rest[3:]
    if mode < 2:
        open_b, open_o = rest[:2]
        rest = rest[2:]
    (ow, prm, fw, pw, nm, acc, par, d_br, sems, osems) = rest[:10]
    stage = rest[10:]
    bufs = [stage[3 * i : 3 * i + 3] for i in range(nout)]
    core = meta[CORE]
    groups = NG // 2 // NC
    keep = (keep_ref[0], keep_ref[1])
    weights.start_small(prm, sems.at[1])
    for c in range(NC):
        weights.start_proj(c, pw.at[c], sems.at[2 + NC + c])
        weights.start_in(c, fw.at[c], sems.at[2 + c])
    weights.start_out(ow, sems.at[0])

    def in_view(ref, c):
        return rows_of(ref, c * GR, GR)

    def proj_view(ref, c):
        return rows_of(ref.at[pl.ds(c * groups, groups)], NC * GR, PR)

    def prev_copies(c):
        slot = lax.rem(c, 2)
        return [
            pltpu.make_async_copy(
                in_view(prev_b, c), bufs[-1][0].at[slot], sems.at[2 + 2 * NC + c]
            ),
            pltpu.make_async_copy(
                proj_view(prev_b, c), bufs[-1][1].at[slot], sems.at[2 + 3 * NC + c]
            ),
        ]

    if mode:
        for copy in prev_copies(0):
            copy.start()
        prev_o_copy = pltpu.make_async_copy(prev_o, bufs[-1][2], sems.at[2 + 4 * NC])
        prev_o_copy.start()
    landed(prm, sems.at[1])
    par[...] = params_of(prm)
    xhat, _ = norm_parts(mid[...])
    nm[...] = jnp.transpose((xhat * par[1:2] + par[3:4]).astype(BF))
    d_br[...] = dres[...].astype(BF)
    small[...] = jnp.zeros_like(small)
    small[7:8, :] = jnp.sum(d_br[...].astype(F32), 0, keepdims=True)
    ones = jnp.ones((8, d_br.shape[0]), BF)

    def out_copies(c):
        slot = lax.rem(c, 2)
        copies = []
        if done:
            f, j = bufs[0][0].at[slot], bufs[0][1].at[slot]
            sem = lambda k: osems.at[k, c]
            copies += to_cores(
                f, in_view(done_mine, c), in_view(done_other, c), core, sem(0), sem(1)
            )
            copies += to_cores(
                j, proj_view(done_mine, c), proj_view(done_other, c), core, sem(2), sem(3)
            )
        if mode < 2:
            f, j = bufs[-1][0].at[slot], bufs[-1][1].at[slot]
            copies.append(pltpu.make_async_copy(f, in_view(open_b, c), osems.at[4, c]))
            copies.append(pltpu.make_async_copy(j, proj_view(open_b, c), osems.at[5, c]))
        return copies

    acc[...] = jnp.zeros_like(acc)

    def chunk(c, carry):
        slot = lax.rem(c, 2)
        landed(pw.at[c], sems.at[2 + NC + c])
        d_act = dot_nt(pw[c].reshape(D, D), d_br[...])
        x = jnp.transpose(pre[c]).astype(F32)
        x2 = x * x
        th = jnp.tanh(x * (GELU_C + GELU_C * GELU_A * x2))
        up = 0.5 + 0.5 * th
        act = (x * up).astype(BF)
        slope = up + (x * (0.5 - 0.5 * th * th)) * (GELU_C + 3.0 * GELU_C * GELU_A * x2)
        d_pre = (d_act * slope).astype(BF)
        small[pl.ds(8 + c, 1), :] = dot_nt(ones, d_pre)[0:1]
        landed(fw.at[c], sems.at[2 + c])
        acc[...] += dot(fw[c].reshape(D, D), d_pre)
        g_fc = dot_nt(nm[...], d_pre)
        g_proj = dot(act, d_br[...])

        @pl.when(c > 0)
        def _():
            for copy in out_copies(c - 1):
                copy.wait()

        if mode:

            @pl.when(c < NC - 1)
            def _():
                for copy in prev_copies(c + 1):
                    copy.start()

            for copy in prev_copies(c):
                copy.wait()
        for part, val in ((0, g_fc), (1, g_proj)):
            prev = bufs[-1][part][slot].reshape(D, D) if mode else None
            for which, term in enumerate(sort_terms(mode, keep, val, prev)):
                ref = bufs[which][part]
                ref[slot] = term.astype(BF).reshape(ref.shape[1:])
        for copy in out_copies(c):
            copy.start()
        return carry

    lax.fori_loop(0, NC, chunk, 0)
    xhat, rstd = norm_parts(mid[...])
    dy = jnp.transpose(acc[...])
    small[1:2, :] = jnp.sum(dy * xhat, 0, keepdims=True)
    small[3:4, :] = jnp.sum(dy, 0, keepdims=True)
    d_mid = dres[...] + norm_back(xhat, rstd, par[1:2], dy)
    d_middle[...] = d_mid
    d_attn = d_mid.astype(BF)
    small[6:7, :] = jnp.sum(d_attn.astype(F32), 0, keepdims=True)
    landed(ow, sems.at[0])
    d_mix = dot_nt(d_attn, ow[...].reshape(D, D)).astype(BF)
    d_mixed[...] = d_mix
    g_out = dot_tn(mixed[...], d_attn)
    if mode:
        prev_o_copy.wait()
    prev = bufs[-1][2][...].reshape(D, D) if mode else None
    o_refs = ([done_o] if done else []) + ([open_o] if mode < 2 else [])
    o_copies = []
    for which, term in enumerate(sort_terms(mode, keep, g_out, prev)):
        bufs[which][2][...] = term.astype(BF).reshape(NG // 2, 2, GR, D)
        copy = pltpu.make_async_copy(bufs[which][2], o_refs[which], osems.at[6 + which, 0])
        copy.start()
        o_copies.append(copy)
    prod = d_mix.astype(F32) * mixed[...].astype(F32)
    big = prod.astype(BF)
    rest_part = (prod - big.astype(F32)).astype(BF)
    heads = lax.broadcasted_iota(jnp.int32, (16, D), 1) // (D // HEADS)
    ind = jnp.where(heads == lax.broadcasted_iota(jnp.int32, (16, D), 0), 1.0, 0.0).astype(BF)
    half = prod.shape[0] // 2
    for part in range(2):
        rows = slice(part * half, (part + 1) * half)
        dt[part] = dot_nt(ind, big[rows]) + dot_nt(ind, rest_part[rows])
    for copy in out_copies(NC - 1) + o_copies:
        copy.wait()


def attn_back_kernel(others, meta, q_ref, ko, vo, kx, vx, do_ref, lse, dt, dq, dkv, dkvx):
    step = pl.program_id(0)
    rows = q_ref.shape[0]
    half = rows // 2
    first, tri = pair_masks(half, 1)
    highs = [meta[UPS + t] > 0 for t in range(others)]
    scale = (D // HEADS) ** -0.5

    def stats(part):
        both = [
            (lse[part, pl.ds(2 * step + h, 1), :], dt[part, pl.ds(2 * step + h, 1), :])
            for h in range(2)
        ]
        return tuple(jnp.concatenate(x, 1) for x in zip(*both))

    q_lo, q_hi = by_head(q_ref[:half], first), by_head(q_ref[half:], first)
    do_lo, do_hi = by_head(do_ref[:half], first), by_head(do_ref[half:], first)
    low = (q_lo, do_lo) + stats(0)
    high = (q_hi, do_hi) + stats(1)

    def tile(queries, k, v, diag):
        q, do, row_lse, row_dt = queries
        p = jnp.exp(dot_nt(k, q) - row_lse)
        if diag:
            p = jnp.where(tri, p, 0.0)
        ds = (p * (dot_nt(v, do) - row_dt)).astype(BF)
        return dot_tn(ds, k), dot(ds, q), dot(p.astype(BF), do)

    k_lo, k_hi, v_lo, v_hi = ko[0, :half], ko[0, half:], vo[0, :half], vo[0, half:]
    dq_lo, dk_a, dv_a = tile(low, k_lo, v_lo, True)
    dq_hi, dk_b, dv_b = tile(high, k_lo, v_lo, False)
    dkv[0, :half] = (dk_a + dk_b).astype(BF)
    dkv[1, :half] = (dv_a + dv_b).astype(BF)
    dq_add, dk, dv = tile(high, k_hi, v_hi, True)
    dq_hi = dq_hi + dq_add
    dkv[0, half:] = dk.astype(BF)
    dkv[1, half:] = dv.astype(BF)
    for t in range(others):
        up = highs[t]
        dq_add, dk, dv = tile(high, kx[t, 0, :half], vx[t, 0, :half], False)
        dq_hi = dq_hi + dq_add
        both = tuple(jnp.where(up, a, b) for a, b in zip(high, low))
        k_x = jnp.where(up, kx[t, 0, half:], kx[t, 0, :half])
        v_x = jnp.where(up, vx[t, 0, half:], vx[t, 0, :half])
        dq_add, dk_x, dv_x = tile(both, k_x, v_x, False)
        dq_hi = dq_hi + jnp.where(up, dq_add, 0.0)
        dq_lo = dq_lo + jnp.where(up, 0.0, dq_add)
        dkvx[t, 0, :half] = (dk + jnp.where(up, 0.0, dk_x)).astype(BF)
        dkvx[t, 1, :half] = (dv + jnp.where(up, 0.0, dv_x)).astype(BF)
        dkvx[t, 0, half:] = jnp.where(up, dk_x, 0.0).astype(BF)
        dkvx[t, 1, half:] = jnp.where(up, dv_x, 0.0).astype(BF)
    dq[:half] = (jnp.where(first, dq_lo[:half], dq_lo[half:]) * scale).astype(BF)
    dq[half:] = (jnp.where(first, dq_hi[:half], dq_hi[half:]) * scale).astype(BF)


def qkv_back_kernel(
    kinds, mode, others, meta, keep_ref, resid, dq, dkv, dkvx, d_middle, small_in, *rest
):
    nw = Weights.count(kinds)
    weights = Weights(kinds, rest[:nw], meta)
    rest = rest[nw:]
    done = mode > 0
    if done:
        prev_ref, done_o = rest[:2]
        rest = rest[2:]
    nout = 2 if mode == 1 else 1
    dres = rest[0]
    rest = rest[1:]
    if done:
        done_mine, done_other = rest[:2]
        rest = rest[2:]
    if mode < 2:
        open_a = rest[0]
        rest = rest[1:]
    wqk, wv, prm, sems, osems = rest[:5]
    bufs = rest[5:]
    core = meta[CORE]
    keep = (keep_ref[0], keep_ref[1])
    weights.start_small(prm, sems.at[0])
    weights.start_qk(wqk, sems.at[1])
    weights.start_v(wv, sems.at[2])
    copies = []
    if done:
        prev_copy = pltpu.make_async_copy(prev_ref, bufs[-1], sems.at[3])
        prev_copy.start()
        copies += to_cores(
            done_o,
            rows_of(done_mine, 3 * GR, GR),
            rows_of(done_other, 3 * GR, GR),
            core,
            osems.at[0],
            osems.at[1],
        )
        for copy in copies:
            copy.start()
    landed(prm, sems.at[0])
    par = params_of(prm)
    xhat, rstd = norm_parts(resid[...])
    normed = jnp.transpose((xhat * par[0:1] + par[2:3]).astype(BF))
    parts = [dq[...]]
    for i in range(2):
        total = dkv[i].astype(F32)
        for t in range(others):
            total = total + dkvx[t, i].astype(F32)
        parts.append(total.astype(BF))
    landed(wqk, sems.at[1])
    landed(wv, sems.at[2])
    if done:
        prev_copy.wait()
    ws = [wqk[:, :, :GR, :], wqk[:, :, GR:, :], wv[...]]
    dy = 0.0
    for i, part in enumerate(parts):
        rows = slice(i * GR, (i + 1) * GR)
        dy = dy + dot_nt(part, ws[i].reshape(D, D))
        prev = bufs[-1][:, :, rows, :].reshape(D, D) if mode else None
        for which, val in enumerate(sort_terms(mode, keep, dot(normed, part), prev)):
            bufs[which][:, :, rows, :] = val.astype(BF).reshape(NG // 2, 2, GR, D)
    small = jnp.concatenate(
        [
            jnp.sum(dy * xhat, 0, keepdims=True),
            small_in[1:2],
            jnp.sum(dy, 0, keepdims=True),
            small_in[3:4],
            jnp.sum(parts[0].astype(F32), 0, keepdims=True),
            jnp.sum(parts[2].astype(F32), 0, keepdims=True),
            small_in[6:],
        ],
        0,
    )
    prev = bufs[-1][0, 0, 3 * GR :, :] if mode else None
    for which, val in enumerate(sort_terms(mode, keep, small, prev)):
        bufs[which][:, :, 3 * GR :, :] = jnp.broadcast_to(
            val.astype(BF)[None, None], (NG // 2, 2, SMALL, D)
        )
    later = []
    if done:
        for k, (lo, size, to) in enumerate(((0, 3 * GR, 0), (3 * GR, SMALL, 4 * GR))):
            later += to_cores(
                rows_of(bufs[0], lo, size),
                rows_of(done_mine, to, size),
                rows_of(done_other, to, size),
                core,
                osems.at[2 + 2 * k],
                osems.at[3 + 2 * k],
            )
    if mode < 2:
        later.append(pltpu.make_async_copy(bufs[-1], open_a, osems.at[6]))
    for copy in later:
        copy.start()
    dres[...] = d_middle[...] + norm_back(xhat, rstd, par[0:1], dy)
    for copy in copies + later:
        copy.wait()


def pack_kernel(meta, small_in, qkv, out, fc, proj, *rest):
    outs, smalls, sems = rest[:4], rest[4], rest[5]
    first, plane, at = meta[0], meta[1], meta[2]
    copies = []

    def cols(ref, src, i):
        return ref.at[src, :, pl.ds(i * D, D)]

    def copy(src, dst):
        copies.append(pltpu.make_async_copy(src, dst, sems.at[len(copies)]))
        copies[-1].start()

    for i, src in enumerate((first, 1 - first)):
        attn, ffn = outs[2 * i : 2 * i + 2]
        for k in range(NC // 2):
            col = pl.multiple_of((plane * (NC // 2) + k) * D, D)
            copy(fc.at[src, :, pl.ds(col, D)], ffn.at[pl.ds(k * GR, GR)])
        row = pl.multiple_of(plane * (PR // 2), 16)
        copy(proj.at[src, pl.ds(row, PR // 2)], ffn.at[pl.ds(NC // 2 * GR, PR // 2)])
        for k in range(3):
            copy(cols(qkv, src, k), attn.at[pl.ds(k * GR, GR)])
        copy(out.at[src], attn.at[pl.ds(3 * GR, GR)])

    lane = lax.broadcasted_iota(jnp.int32, (GR, D), 1)
    row = lax.broadcasted_iota(jnp.int32, (GR, D), 0)
    spread = jnp.where(lane == row + at * GR, 1.0, 0.0).astype(BF)
    lane = lax.broadcasted_iota(jnp.int32, (PR, D), 1)
    row = lax.broadcasted_iota(jnp.int32, (PR, D), 0)
    spread_h = jnp.where(lane == row + lax.rem(at, NG // NC) * PR, 1.0, 0.0).astype(BF)
    line = lax.broadcasted_iota(jnp.int32, (8, D), 0)
    for i, src in enumerate((first, 1 - first)):
        smalls[i, 0:8, :] = dot(small_in[src, :, :GR], spread).astype(BF)
        hid = dot(small_in[src, :, GR : GR + PR], spread_h)
        smalls[i, 8:16, :] = jnp.where(line == at // (NG // NC), hid[0:1], 0.0).astype(BF)
        copy(smalls.at[i], outs[2 * i].at[pl.ds(4 * GR, SMALL)])
    for one in copies:
        one.wait()


def assemble_kernel(meta, mine, other, whole, sems):
    copies = []
    for side, ref in enumerate((mine, other)):
        for low in range(2):
            for high in range(2):
                z = jnp.bitwise_xor(meta[ZPOS], low + 2 * high)
                y = meta[YPOS] if side == 0 else 1 - meta[YPOS]
                copies.append(
                    pltpu.make_async_copy(
                        ref.at[low, high], whole.at[z * 2 + y], sems.at[len(copies)]
                    )
                )
                copies[-1].start()
    for copy in copies:
        copy.wait()


def add_cores_kernel(segments, meta, mine, got, *outs):
    total = (mine[...].astype(F32) + got[...].astype(F32)).astype(BF)
    for i, (order, low, high, size) in enumerate(segments):
        if order == "x":
            sides, which = (total[:, low : low + size], total[:, high : high + size]), PLANE
        else:
            sides, which = (total[0:1, low : low + size], total[1:2, low : low + size]), YPOS
        outs[2 * i][...] = jnp.where(meta[which] == 0, sides[0], sides[1])
        outs[2 * i + 1][...] = jnp.where(meta[which] == 0, sides[1], sides[0])


def add_split_kernel(bits, meta, *refs):
    ins, outs = refs[: 2 * len(bits)], list(refs[2 * len(bits) :])
    for i, bit in enumerate(bits):
        mine, got = ins[2 * i], ins[2 * i + 1]
        if bit is None:
            outs.pop(0)[...] = (mine[0].astype(F32) + got[0].astype(F32)).astype(BF)
            continue
        keep, send = outs.pop(0), outs.pop(0)

        def pair(g, carry):
            for out, at in ((keep, 2 * g + meta[bit]), (send, 2 * g + 1 - meta[bit])):
                out[g] = (mine[at].astype(F32) + got[at].astype(F32)).astype(BF)
            return carry

        lax.fori_loop(0, mine.shape[0] // 2, pair, 0)


def finish_kernel(meta, *refs):
    ins, outs = refs[:12], refs[12:]
    qkv_g, out_g, fc_g, proj_g, gains_g, shifts_g, bias_g, hidden_g = outs
    first, plane, at = meta[0], meta[1], meta[2]
    low = lambda mine, peer: jnp.where(plane == 0, mine[...], peer[...])
    high = lambda mine, peer: jnp.where(plane == 0, peer[...], mine[...])
    pick = lax.broadcasted_iota(jnp.int32, (D, GR), 0) == (
        lax.broadcasted_iota(jnp.int32, (D, GR), 1) + at * GR
    )
    pick = jnp.where(pick, 1.0, 0.0).astype(BF)
    pick_h = lax.broadcasted_iota(jnp.int32, (D, PR), 0) == (
        lax.broadcasted_iota(jnp.int32, (D, PR), 1) + lax.rem(at, NG // NC) * PR
    )
    pick_h = jnp.where(pick_h, 1.0, 0.0).astype(BF)
    line = lax.broadcasted_iota(jnp.int32, (SMALL, D), 0)
    here = line == 8 + at // (NG // NC)

    def write(src, in_pair, proj_pair, qk, vo, small):
        ins_ = (low(*in_pair), high(*in_pair))
        for k in range(NC):
            rows = slice(k % (NC // 2) * GR, (k % (NC // 2) + 1) * GR)
            fc_g[src, :, k * D : (k + 1) * D] = ins_[k // (NC // 2)][rows].astype(F32)
        proj_g[src] = proj_pair[0][...].astype(F32) + proj_pair[1][...].astype(F32)
        for k, part in enumerate(qk + vo[:1]):
            qkv_g[src, :, k * D : (k + 1) * D] = part
        out_g[src] = vo[1]
        vals = dot(small, pick)
        row = jnp.sum(jnp.where(here, small.astype(F32), 0.0), 0, keepdims=True)
        hid = dot(jnp.broadcast_to(row, (8, D)).astype(BF), pick_h)
        gains_g[src] = vals[0:2]
        shifts_g[src] = vals[2:4]
        bias_g[src] = vals[4:8]
        hidden_g[src] = hid[0:1]

    for k, src in enumerate((1 - first, first)):
        ins_ = ins[4 * k : 4 * k + 4] + ins[8 + 2 * k : 10 + 2 * k]
        part_l, part_h = low(*ins_[4:6]), high(*ins_[4:6])
        write(
            src,
            ins_[0:2],
            ins_[2:4],
            (part_l[:GR].astype(F32), part_l[GR : 2 * GR].astype(F32)),
            (part_h[:GR].astype(F32), part_h[GR : 2 * GR].astype(F32)),
            part_h[2 * GR :],
        )


VM = pl.BlockSpec(memory_space=pltpu.VMEM)
SM = pl.BlockSpec(memory_space=pltpu.SMEM)
HB = pl.BlockSpec(memory_space=pl.ANY)
DMA = pltpu.SemaphoreType.DMA


def call(kernel, outs, in_specs, out_specs, scratch, flops, name, weight=8, **more):
    cost = pl.CostEstimate(flops=int(flops * weight), bytes_accessed=1024, transcendentals=0)
    return pl.pallas_call(
        kernel,
        out_shape=outs,
        in_specs=in_specs,
        out_specs=out_specs,
        scratch_shapes=scratch,
        compiler_params=pltpu.CompilerParams(vmem_limit_bytes=VMEM_LIMIT),
        cost_estimate=cost,
        name=name,
        **more,
    )


def sds(shape, dtype):
    return jax.ShapeDtypeStruct(shape, dtype)


def run_qkv(meta, resid, kinds, weights):
    rows = resid.shape[0]
    return call(
        functools.partial(qkv_kernel, kinds),
        (sds((rows, D), BF), sds((2, rows, D), BF)),
        [SM, VM] + [HB] * len(weights),
        (VM, VM),
        qkv_scratch() + [DMA((3,))],
        2 * rows * D * 3 * D,
        "qkv",
        8 if len(kinds) > 1 else 0.01,
    )(meta, resid, *weights)


def qkv_scratch():
    return [
        pltpu.VMEM((NG // 2, 2, 2 * GR, D), BF),
        pltpu.VMEM((NG // 2, 2, GR, D), BF),
        pltpu.VMEM((NG // 2, 2, SMALL, D), BF),
    ]


def pair_specs(rows, others):
    lanes = 2 * D // HEADS
    return [
        SM,
        pl.BlockSpec((rows, lanes), lambda i: (0, i)),
        pl.BlockSpec((1, rows, lanes), lambda i: (0, 0, i)),
        pl.BlockSpec((1, rows, lanes), lambda i: (1, 0, i)),
        pl.BlockSpec((others, 1, rows, lanes), lambda i: (0, 0, 0, i)),
        pl.BlockSpec((others, 1, rows, lanes), lambda i: (0, 1, 0, i)),
    ]


def run_attn(meta, q, kv, kvx, weight):
    rows, others = q.shape[0], kvx.shape[0]
    half = rows // 2
    return call(
        functools.partial(attn_fwd_kernel, others),
        (sds((rows, D), BF), sds((2, 16, half), F32)),
        pair_specs(rows, others),
        (
            pl.BlockSpec((rows, 2 * D // HEADS), lambda i: (0, i)),
            pl.BlockSpec((2, 16, half), lambda i: (0, 0, 0)),
        ),
        [pltpu.VMEM((rows, 128), F32)],
        HEADS * (3 + 2 * others) * half * half * 256 * 4,
        "attn",
        weight,
        grid=(PAIRS,),
    )(meta, q, kv, kv, kvx, kvx)


def weight_scratch(rows, flipped=False):
    shape = (D, rows) if flipped else (rows, D)
    return [
        pltpu.VMEM((NG // 2, 2, GR, D), BF),
        pltpu.VMEM((NG // 2, 2, SMALL, D), BF),
        pltpu.VMEM((NC, NG // 2, 2, GR, D), BF),
        pltpu.VMEM((NC, NG // 2 // NC, 2, PR, D), BF),
        pltpu.VMEM(shape, BF),
        pltpu.VMEM(shape, F32),
        pltpu.VMEM((SMALL, D), F32),
    ]


def run_mlp(meta, resid, mixed, kinds, weights):
    rows = resid.shape[0]
    return call(
        functools.partial(mlp_kernel, kinds),
        (sds((rows, D), F32), sds((NC, rows, D), BF), sds((rows, D), F32)),
        [SM, VM, VM] + [HB] * len(weights),
        (VM, VM, VM),
        weight_scratch(rows) + [DMA((2 + 2 * NC,))],
        2 * rows * D * (D + 2 * FF),
        "mlp",
        8 if len(kinds) > 1 else 0.01,
    )(meta, resid, mixed, *weights)


def run_mlp_back(mode, meta, keep, dres, mid, pre, mixed, kinds, weights, prev):
    rows = dres.shape[0]
    nout = 2 if mode == 1 else 1
    b_rows = NC * GR + PR
    o_shape = sds((NG // 2, 2, GR, D), BF)
    outs = ()
    if mode:
        outs += (sds((NG // 2, b_rows, D), BF),) * 2 + (o_shape,)
    if mode < 2:
        outs += (sds((NG // 2, 2, b_rows, D), BF), o_shape)
    stage = [
        pltpu.VMEM((2, NG // 2, 2, GR, D), BF),
        pltpu.VMEM((2, NG // 2 // NC, 2, PR, D), BF),
        pltpu.VMEM((NG // 2, 2, GR, D), BF),
    ] * nout
    return call(
        functools.partial(mlp_back_kernel, kinds, mode),
        (
            sds((rows, D), F32),
            sds((rows, D), BF),
            sds((2, 16, rows // 2), F32),
            sds((SMALL, D), F32),
        )
        + outs,
        [SM, SM, VM, VM, VM, VM] + [HB] * (len(weights) + len(prev)),
        (VM, VM, VM, VM) + (HB,) * len(outs),
        weight_scratch(rows, True)
        + [pltpu.VMEM((rows, D), BF), DMA((3 + 4 * NC,)), DMA((8, NC))]
        + stage,
        4 * rows * D * (D + 2 * FF),
        "mlp_back",
    )(meta, keep, dres, mid, pre, mixed, *weights, *prev)


def run_attn_back(meta, q, kv, kvx, d_mixed, lse, dt):
    rows, others = q.shape[0], kvx.shape[0]
    half = rows // 2
    lanes = 2 * D // HEADS
    stat = pl.BlockSpec((2, 16, half), lambda i: (0, 0, 0))
    block = pl.BlockSpec((rows, lanes), lambda i: (0, i))
    return call(
        functools.partial(attn_back_kernel, others),
        (sds((rows, D), BF), sds((2, rows, D), BF), sds((others, 2, rows, D), BF)),
        pair_specs(rows, others) + [block, stat, stat],
        (
            block,
            pl.BlockSpec((2, rows, lanes), lambda i: (0, 0, i)),
            pl.BlockSpec((others, 2, rows, lanes), lambda i: (0, 0, 0, i)),
        ),
        [],
        HEADS * (3 + 2 * others) * half * half * 256 * 10,
        "attn_back",
        grid=(PAIRS,),
    )(meta, q, kv, kv, kvx, kvx, d_mixed, lse, dt)


def run_qkv_back(
    mode, meta, keep, resid, dq, dkv, dkvx, d_middle, small, kinds, weights, prev
):
    rows, others = resid.shape[0], dkvx.shape[0]
    nout = 2 if mode == 1 else 1
    shape = (NG // 2, 2, 3 * GR + SMALL, D)
    outs = ()
    if mode:
        outs += (sds((NG // 2, 4 * GR + SMALL, D), BF),) * 2
    if mode < 2:
        outs += (sds(shape, BF),)
    return call(
        functools.partial(qkv_back_kernel, kinds, mode, others),
        (sds((rows, D), F32),) + outs,
        [SM, SM] + [VM] * 6 + [HB] * (len(weights) + min(mode, 1)) + [VM] * min(mode, 1),
        (VM,) + (HB,) * len(outs),
        qkv_scratch() + [DMA((4,)), DMA((7,))] + [pltpu.VMEM(shape, BF)] * nout,
        4 * rows * D * 3 * D,
        "qkv_back",
    )(meta, keep, resid, dq, dkv, dkvx, d_middle, small, *weights, *prev)


def run_pack(meta, small, qkv, out, fc, proj):
    rows = (A_ROWS, B_ROWS // 2) * 2
    return call(
        pack_kernel,
        tuple(sds((r, D), BF) for r in rows),
        [SM, VM] + [HB] * 4,
        (HB,) * 4,
        [pltpu.VMEM((2, SMALL, D), BF), DMA((2 * (NC // 2 + 6),))],
        2 * 16 * PR * D,
        "pack",
    )(meta, small, qkv, out, fc, proj)


def run_assemble(meta, mine, other):
    rows = mine.shape[-2]
    return call(
        assemble_kernel,
        sds((NG // 2, rows, D), BF),
        [SM, HB, HB],
        VM,
        [DMA((NG // 2,))],
        NG * rows * D,
        "assemble",
    )(meta, mine, other)


def run_add_cores(meta, mine, got, segments, weight):
    groups, rows = mine.shape[:2]
    outs, specs = [], []
    for order, _, _, size in segments:
        step = 2 if order == "x" else 1
        outs += [sds((groups // 2 * step, size, D), BF)] * 2
        specs += [pl.BlockSpec((step, size, D), lambda i: (i, 0, 0))] * 2
    block = pl.BlockSpec((2, rows, D), lambda i: (i, 0, 0))
    return call(
        functools.partial(add_cores_kernel, segments),
        outs,
        [SM, block, block],
        specs,
        [],
        mine.size * weight,
        "add_cores",
        grid=(groups // 2,),
    )(meta, mine, got)


def run_add_split(meta, bits, pairs, weight):
    outs = []
    for bit, (mine, _) in zip(bits, pairs):
        groups, rows = mine.shape[:2]
        if bit is None:
            outs.append(sds((rows, D), BF))
        else:
            outs += [sds((groups // 2, rows, D), BF)] * 2
    ins = [x for pair in pairs for x in pair]
    return call(
        functools.partial(add_split_kernel, bits),
        outs,
        [SM] + [VM] * len(ins),
        [VM] * len(outs),
        [],
        sum(x.size for x in ins) * weight,
        "add_split",
    )(meta, *ins)


def run_finish(meta, parts):
    outs = (
        sds((2, GR, 3 * D), F32),
        sds((2, GR, D), F32),
        sds((2, GR, FF), F32),
        sds((2, PR, D), F32),
        sds((2, 2, GR), F32),
        sds((2, 2, GR), F32),
        sds((2, 4, GR), F32),
        sds((2, 1, PR), F32),
    )
    return call(
        finish_kernel, outs, [SM] + [VM] * len(parts), (VM,) * 8, [], 2**20, "finish"
    )(meta, *parts)


def regroup(packed, own_from, own_to, widths):
    if own_from == own_to:
        return packed
    parts, at = [], 0
    for width in widths:
        rows = width // own_from
        part = packed[:, at : at + rows].reshape(width, D)
        parts.append(part.reshape(own_to, width // own_to, D))
        at += rows
    return jnp.concatenate(parts, 1)


def blocks(table):
    return jnp.concatenate([table[:, i : i + D] for i in range(0, table.shape[1], D)], 0)


def unblock(rows, count):
    size = rows.shape[0] // count
    return jnp.concatenate([rows[i * size : (i + 1) * size] for i in range(count)], 1)


def place_small(gains, shifts, bias_m, bias_h, at):
    vecs = jnp.concatenate([gains, shifts, bias_m], 0)
    wide = lax.dynamic_update_slice(jnp.zeros((8, D), BF), vecs, (0, at * vecs.shape[1]))
    hid = lax.dynamic_update_slice(jnp.zeros((FF,), BF), bias_h, (at * bias_h.shape[0],))
    return jnp.concatenate([wide, hid.reshape(NC, D), jnp.zeros((SMALL - 8 - NC, D), BF)], 0)


def per_device(own, n, tokens, tie, qkv_w, out_w, fc_w, proj_w, gains, shifts, bias_m, bias_h, cotangent):
    axes = ("own", "dp")
    o = lax.axis_index("own")
    d = lax.axis_index("dp")
    core = o % 2
    rows = tokens.shape[1]
    half = rows // 2
    others = n - 1

    def at(pair, s, j):
        return (2 * pair + j % 2) * n + s * (n // 2) + j // 2

    j = (d % (n // 2)) * 2 + core

    def place(block):
        return block if block < n else 2 * n - 1 - block

    def moves(odd):
        return [
            ((2 * pair + s) * n + dd, at(pair, s, place(2 * dd + odd)))
            for pair in range(own // 2)
            for s in range(2)
            for dd in range(n)
        ]

    def to_chip(x):
        x = x.reshape(rows, D)
        even = lax.ppermute(x[:half], axes, moves(0))
        odd = lax.ppermute(x[half:], axes, moves(1))
        return jnp.concatenate(
            [jnp.where(core == 0, even, odd), jnp.where(core == 0, odd, even)], 0
        )

    def from_chip(x):
        back = [[(b, a) for a, b in moves(odd)] for odd in range(2)]
        even = lax.ppermute(jnp.where(core == 0, x[:half], x[half:]), axes, back[0])
        odd = lax.ppermute(jnp.where(core == 0, x[half:], x[:half]), axes, back[1])
        return jnp.concatenate([even, odd], 0).reshape(tokens.shape)

    def shift(x, step):
        pairs = [
            (at(pair, s, (place_ + step) % n), at(pair, s, place_))
            for pair in range(own // 2)
            for s in range(2)
            for place_ in range(n)
        ]
        return lax.ppermute(x, axes, pairs)

    plane, y, z = d % 2, (o // 2) % 2, o // 4
    nz = own // 4

    def device(zz, yy, cc, dd):
        return ((zz * 2 + yy) * 2 + cc) * n + dd

    everyone = [
        (zz, yy, cc, dd)
        for zz in range(nz)
        for yy in range(2)
        for cc in range(2)
        for dd in range(n)
    ]

    def swap(x, axis):
        turn = {
            "core": lambda zz, yy, cc, dd: device(zz, yy, 1 - cc, dd),
            "y": lambda zz, yy, cc, dd: device(zz, 1 - yy, cc, dd),
            "x": lambda zz, yy, cc, dd: device(zz, yy, cc, dd ^ 1),
            "z1": lambda zz, yy, cc, dd: device(zz ^ 1, yy, cc, dd),
            "z2": lambda zz, yy, cc, dd: device(zz ^ 2, yy, cc, dd),
        }[axis]
        return lax.ppermute(x, axes, [(device(*at_), turn(*at_)) for at_ in everyone])

    def from_z(x, step):
        pairs = [
            (device((zz + step) % nz, yy, cc, dd), device(zz, yy, cc, dd))
            for zz, yy, cc, dd in everyone
        ]
        return lax.ppermute(x, axes, pairs)

    def after(x, *deps):
        return lax.optimization_barrier((x, *deps))[0]

    def after_all(xs, *deps):
        return lax.optimization_barrier((tuple(xs), *deps))[0]

    open_src = tie[0]
    isin = lambda u: (tie[u] != open_src).astype(jnp.int32)
    ups = [((j + t) % n > j).astype(jnp.int32) for t in range(1, n)]
    metas = [jnp.stack([isin(u), core, plane, y, z, z % 2, z // 2] + ups).astype(jnp.int32) for u in range(3)]
    keep = jnp.stack([isin(1), isin(2)]).astype(F32)
    direct = own == NG and n == 2

    if direct:
        small = jnp.concatenate([gains, shifts, bias_m], 1)
        hid = jnp.broadcast_to(bias_h[:, None], (2, 8, bias_h.shape[1]))
        packed = run_pack(
            jnp.stack([open_src, plane, o]).astype(jnp.int32),
            jnp.concatenate([small, hid], 2),
            qkv_w,
            out_w,
            fc_w,
            proj_w,
        )

        def square(x, axis):
            return jnp.stack([x, swap(x, axis)], 0)

        def cores_of(part):
            return [part, swap(part, "core")]

        twos, lines, sides = [], [], []
        for part in (packed[1], packed[3], packed[0], packed[2]):
            twos.append(square(after(part, twos[-1]) if twos else part, "z2"))
            two = after(twos[-1], lines[-1]) if lines else twos[-1]
            lines.append(square(two, "z1"))
            line = after(lines[-1], sides[-1][1]) if sides else lines[-1]
            sides.append((line, swap(line, "y")))
        resid = to_chip(after(tokens, twos[0])).astype(F32)
        dres = to_chip(after(cotangent, twos[0])).astype(F32)
        ffn = [run_assemble(after(metas[0], resid, dres, lines[1]), *sides[0])]
        peers = [swap(ffn[0], "x")]
        ffn.append(run_assemble(after(metas[0], lines[2]), *sides[1]))
        peers.append(swap(after(ffn[1], peers[0]), "x"))
        attn = run_assemble(after(metas[0], lines[3]), *sides[2])
        first_a, first_b = cores_of(attn), cores_of(ffn[0]) + cores_of(peers[0])
        kinds = (("a2", "b4"),) * 2
        second_b = cores_of(ffn[1]) + cores_of(peers[1])
        metas[0] = after(metas[0], *first_a, *first_b, *second_b[:2])
    else:
        resid = to_chip(tokens).astype(F32)
        dres = to_chip(cotangent).astype(F32)
        sources = []
        for src in (open_src, 1 - open_src):
            pick = lambda table: lax.dynamic_index_in_dim(table, src, 0, keepdims=False)
            part = jnp.concatenate(
                [blocks(pick(qkv_w)), pick(out_w), blocks(pick(fc_w)), pick(proj_w)], 0
            )
            full = lax.all_gather(part, "own", axis=0, tiled=False)
            full = regroup(full, own, NG, [D] * (4 + NC) + [FF])
            small = place_small(pick(gains), pick(shifts), pick(bias_m), pick(bias_h), o)
            small = lax.psum(small.astype(F32), "own").astype(BF)
            small = jnp.concatenate([small[None], jnp.zeros((NG - 1, SMALL, D), BF)], 0)
            full = jnp.concatenate([full[:, : 4 * GR], small, full[:, 4 * GR :]], 1)
            sources.append([full.reshape(NG // 2, 2, -1, D)])
        first_a = first_b = sources[0]
        second_a = second_b = sources[1]
        kinds = (("a", "b"),) * 2

    def weights_of(u, attn_only=False):
        many = 1 if u == 0 else 2
        arrays = first_a + ([] if attn_only else first_b)
        if u:
            arrays = arrays + second_a + ([] if attn_only else second_b)
        return tuple(kind[: 1 if attn_only else 2] for kind in kinds[:many]), arrays

    saved = []
    for u in range(3):
        meta = metas[u]
        q, kv = run_qkv(meta, resid, *weights_of(u, True))
        kvx = jnp.stack([shift(kv, t) for t in range(1, n)], 0)
        mixed, lse = run_attn(meta, q, kv, kvx, 8 if u else 0.01)
        middle, pre, result = run_mlp(meta, resid, mixed, *weights_of(u))
        if u == 0 and direct:
            second_a = cores_of(run_assemble(after(metas[1], middle, peers[1]), *sides[3]))
            metas[1] = after(metas[1], *second_a)
        saved.append((resid, q, kv, kvx, mixed, lse, middle, pre))
        resid = result
    output = from_chip(resid.astype(BF))

    def scatter_full(mine, other, widths, small_rows):
        pair = jnp.where(core == 0, jnp.stack([mine, other], 1), jnp.stack([other, mine], 1))
        grad = pair.reshape(NG, -1, D)
        body = grad.shape[1] - small_rows
        tail = grad[:1, body:]
        grad = regroup(grad[:, :body], NG, own, widths)
        if small_rows:
            tail = jnp.broadcast_to(tail, (own, small_rows, D))
            grad = jnp.concatenate([grad, tail], 1)
        part = lax.psum_scatter(grad, "own", scatter_dimension=0, tiled=False)
        return lax.psum(part, "dp").astype(F32)


    class Scatter:
        NEXT = {"x": ("y", YPOS), "y": ("z1", ZLOW), "z1": ("z2", ZHIGH), "z2": ("x", None)}

        def __init__(self, order, keep_, send):
            self.stage, self.keep, self.done = order, keep_, None
            self.got = swap(send, order)

    def step(meta, chunks, weight=1):
        moves_ = [Scatter.NEXT[one.stage] for one in chunks]
        outs = run_add_split(
            meta,
            tuple(bit for _, bit in moves_),
            [(one.keep, one.got) for one in chunks],
            weight,
        )
        first_out, outs = outs[0], list(outs)
        for one, (stage, bit) in zip(chunks, moves_):
            one.stage = stage
            one.keep = outs.pop(0)
            one.got = swap(one.keep if bit is None else outs.pop(0), stage)
            if bit is None:
                one.done = [one.keep, one.got]
        return first_out

    def scatter_start(meta, mine, got, segs, weight):
        outs = run_add_cores(meta, mine, got, segs, weight)
        return [Scatter(seg[0], *outs[2 * i : 2 * i + 2]) for i, seg in enumerate(segs)], outs[0]

    in_rows, a_rows = NC // 2 * GR, 4 * GR + SMALL
    b_segs = (("x", 0, in_rows, in_rows), ("y", NC * GR, 0, PR))
    a_segs = (("x", 0, 2 * GR, 2 * GR + SMALL),)

    prev_b, prev_a = [], []
    shares, fin, opn = {}, [], []
    wr, pr = D // own, FF // own
    for u in (2, 1, 0):
        mode = 2 - u
        meta = metas[u]
        resid, q, kv, kvx, mixed, lse, middle, pre = saved[u]
        outs = run_mlp_back(
            mode, meta, keep, dres, middle, pre, mixed, *weights_of(u), prev_b
        )
        d_middle, d_mixed, dt, small = outs[:4]
        if mode:
            mine_b, other_b, done_o = outs[4:7]
            if direct:
                got_b = swap(other_b, "core")
        prev_b = list(outs[-2:])
        if mode == 0:
            meta = after(meta, output)
        if mode == 2 and direct:
            slot = after(meta, d_mixed)
            more, last = scatter_start(slot, *fin_a, a_segs, 1)
            last = step(after(slot, last), fin, 4096)
            fin += more
            opn, last = scatter_start(after(slot, last), mine_b, got_b, b_segs, 1)
            meta = after(meta, last)
        dq, dkv, dkvx = run_attn_back(meta, q, kv, kvx, d_mixed, lse, dt)
        back = jnp.stack([shift(dkvx[t - 1], n - t) for t in range(1, n)], 0)
        if mode and direct:
            slot = after(meta, dq)
            if mode == 1:
                fin, last = scatter_start(slot, mine_b, got_b, b_segs, 4096)
            else:
                last = step(slot, fin, 4096)
            meta = after(meta, last)
        outs = run_qkv_back(
            mode,
            meta,
            keep,
            resid,
            dq,
            dkv,
            back,
            d_middle,
            small,
            *weights_of(u, True),
            prev_a + ([done_o] if mode else []),
        )
        dres = outs[0]
        prev_a = [outs[-1]]
        if not mode:
            continue
        mine_a, other_a = outs[1:3]
        if direct:
            if mode == 1:
                fin_a = (mine_a, swap(other_a, "core"))
            else:
                slot = after(metas[0], dres)
                got_a = swap(other_a, "core")
                last = step(slot, fin, 4096)
                more, last = scatter_start(after(slot, last), mine_a, got_a, a_segs, 1)
                last = step(after(slot, last), opn, 4096)
                left = [one for one in fin if one.done is None]
                last = step(after(slot, last), left, 1024)
                chunks = fin[:2] + opn + fin[2:] + more
                while any(one.done is None for one in chunks):
                    for group, weight in ((more, 1), (fin + opn, 4096)):
                        left = [one for one in group if one.done is None]
                        if left:
                            last = step(after(slot, last), left, weight)
                done = [x for one in chunks for x in one.done]
        else:
            g_b = scatter_full(mine_b, other_b, [D] * NC + [FF], 0)
            g_in, g_proj = g_b[: NC * wr], g_b[NC * wr :]
            g_a = scatter_full(mine_a, other_a, [D] * 4, SMALL)
            shares[mode] = (g_a, g_in, g_proj)
    input_grad = from_chip(dres.astype(BF))

    if direct:
        place_meta = jnp.stack([open_src, plane, o]).astype(jnp.int32)
        grads = list(run_finish(place_meta, done))
        grads[-1] = grads[-1].reshape(2, -1)
        return (output, input_grad, *grads)

    flip = open_src == 0

    def both(make):
        fin, opn = make(*shares[1]), make(*shares[2])
        return jnp.stack([jnp.where(flip, opn, fin), jnp.where(flip, fin, opn)], 0)

    def lanes(a, lo, hi):
        at_row = 4 * wr
        return lax.dynamic_slice(a[at_row + lo : at_row + hi], (0, o * wr), (hi - lo, wr))

    def hidden(a):
        return lax.dynamic_slice(a[4 * wr + 8 : 4 * wr + 8 + NC].reshape(FF), (o * pr,), (pr,))

    return (
        output,
        input_grad,
        both(lambda a, f, p: unblock(a[: 3 * wr], 3)),
        both(lambda a, f, p: a[3 * wr : 4 * wr]),
        both(lambda a, f, p: unblock(f, NC)),
        both(lambda a, f, p: p),
        both(lambda a, f, p: lanes(a, 0, 2)),
        both(lambda a, f, p: lanes(a, 2, 4)),
        both(lambda a, f, p: lanes(a, 4, 8)),
        both(lambda a, f, p: hidden(a)),
    )


def solution(mesh):
    return jax.shard_map(
        functools.partial(per_device, mesh.shape["own"], mesh.shape["dp"]),
        mesh=mesh,
        in_specs=(
            P("own", "dp", None),
            P(),
            P(None, "own", None),
            P(None, "own", None),
            P(None, "own", None),
            P(None, "own", None),
            P(None, None, "own"),
            P(None, None, "own"),
            P(None, None, "own"),
            P(None, "own"),
            P("own", "dp", None),
        ),
        out_specs=(
            P("own", "dp", None),
            P("own", "dp", None),
            P(None, "own", None),
            P(None, "own", None),
            P(None, "own", None),
            P(None, "own", None),
            P(None, None, "own"),
            P(None, None, "own"),
            P(None, None, "own"),
            P(None, "own"),
        ),
        check_vma=False,
    )
```

time: 2610 us -> 623 us (0.24)
  waiting for transfers between devices: 1630 us -> 192 us
  matrix products: 420 us -> 0 us
  Pallas kernels: 0 us -> 306 us
  blocking collectives: 306 us -> 0 us
  other arithmetic: 140 us -> 10.5 us
  starting transfers between devices: 2.55 us -> 67 us
  local copies, waits for them, and re-layouts: 73.3 us -> 39.2 us
    reduce_scatter x18 -> x0, waiting for transfers between devices: 916 us -> none  [the longest x3 237 us: reduce_grads(): lax.psum_scatter(g_proj.astype(jnp.bfloat16), 'own', scatter_dimension=0,...]
    dot_general x51 -> x0, matrix products: 368 us -> none  [the longest x3 50.3 us: per_device(): jnp.einsum('bqhd,bkhd->bhqk', d_mixed, v_heads, preferred_element_type=jn...]
    unnamed x52 -> x0, waiting for transfers between devices: 341 us -> none
    pallas_call x0 -> x40, Pallas kernels: none -> 306 us  [the longest x3 83.1 us: run_mlp_back(): call(functools.partial(mlp_back_kernel, kinds, mode), (sds((rows, D), F32...]
    all_gather x15 -> x0, waiting for transfers between devices: 293 us -> none  [the longest x3 98.5 us: fetch_forward(): lax.all_gather(proj_w, 'own', axis=0, tiled=True)]
    ppermute x0 -> x66, waiting for transfers between devices: none -> 192 us  [the longest x52 175 us: swap(): lax.ppermute(x, axes, [(device(*at_), turn(*at_)) for at_ in everyone])]
    all_gather x9 -> x0, blocking collectives: 185 us -> none  [the longest x3 64.8 us: fetch_forward(): lax.all_gather(gains, 'own', axis=1, tiled=True)]
    unnamed x2 -> x0, blocking collectives: 116 us -> none
  transfers between devices with their start and end apart: 43 -> 66, of which waited for: 32 -> 28; matrix products, arithmetic and copies ran while one was open for 17% -> 1% of each run, Pallas kernels for 0% -> 31%
where the time goes in v1:
time: 623 us; the launch traced here: 620 us
  Pallas kernels  306 us (49%)
  waiting for transfers between devices  192 us (31%)
  starting transfers between devices  67 us (11%)
  local copies, waits for them, and re-layouts  39.2 us (6%)
  other arithmetic  10.5 us (2%)
    ppermute x52, waiting for transfers between devices, swap(): lax.ppermute(x, axes, [(device(*at_), turn(*at_)) for at_ in everyone])  175 us
    pallas_call x3, Pallas kernels, run_mlp_back(): call(functools.partial(mlp_back_kernel, kinds, mode), (sds((rows, D), F32...  83.1 us
    pallas_call x3, Pallas kernels, run_attn_back(): call(functools.partial(attn_back_kernel, others), (sds((rows, D), BF), sd...  52.3 us
    ppermute x52, starting transfers between devices, swap(): lax.ppermute(x, axes, [(device(*at_), turn(*at_)) for at_ in everyone])  51.8 us
    pallas_call x3, Pallas kernels, run_mlp(): call(functools.partial(mlp_kernel, kinds), (sds((rows, D), F32), sds((NC,...  39.2 us
    pallas_call x3, Pallas kernels, run_qkv_back(): call(functools.partial(qkv_back_kernel, kinds, mode, others), (sds((rows,...  38.9 us
    unnamed x125, local copies, waits for them, and re-layouts  35.9 us
    pallas_call x3, Pallas kernels, run_attn(): call(functools.partial(attn_fwd_kernel, others), (sds((rows, D), BF), sds...  27.4 us
  transfers between devices with their start and end apart: 66, of which 28 were waited for; matrix products, arithmetic and copies ran while one was open for 1% of the time, Pallas kernels for 31%

profile of v1, /device:TPU:0, one launch (start us, length us, event | category | flops | bytes accessed | tf_op | source)
XLA Modules:
  0.0 619.6 jit_solution(9538727181038263875)
XLA Ops:
  14.3 13.3 %collective-permute-done = bf16[192,768]{1,0:T(8,128)(2,1)S(1)} collective-permute-done((bf16[192,768]{1,0:T(8,128)(2,1)S(1)}, bf16[192,768]{1,0:T(8,128)(2,1)S(1)}, u32[]{:S(2)}, u32[]{:S(2)}) %collective-permute-start) | collective-permute-done | bytes 294944 | tf_op jit(solution)/shard_map/ppermute | solution.py:1088
  31.9 16.7 %collective-permute-done.4 = bf16[2,192,768]{2,1,0:T(8,128)(2,1)S(1)} collective-permute-done((bf16[2,192,768]{2,1,0:T(8,128)(2,1)S(1)}, bf16[2,192,768]{2,1,0:T(8,128)(2,1)S(1)}, u32[]{:S(2)}, u32[]{:S(2)}) %collective-permute-start.4) | collective-permute-done | bytes 589856 | tf_op jit(solution)/shard_map/ppermute | solution.py:1088
  66.2 5.8 collective-permute-done.13
  73.5 9.7 %collective-permute-done.5 = bf16[2,192,768]{2,1,0:T(8,128)(2,1)} collective-permute-done((bf16[2,192,768]{2,1,0:T(8,128)(2,1)}, bf16[2,192,768]{2,1,0:T(8,128)(2,1)}, u32[]{:S(2)}, u32[]{:S(2)}) %collective-permute-start.5) | collective-permute-done | bytes 589856 | tf_op jit(solution)/shard_map/ppermute | solution.py:1088
  91.0 15.0 %collective-permute-done.6 = bf16[2,208,768]{2,1,0:T(8,128)(2,1)S(1)} collective-permute-done((bf16[2,208,768]{2,1,0:T(8,128)(2,1)S(1)}, bf16[2,208,768]{2,1,0:T(8,128)(2,1)S(1)}, u32[]{:S(2)}, u32[]{:S(2)}) %collective-permute-start.6) | collective-permute-done | bytes 639008 | tf_op jit(solution)/shard_map/ppermute | solution.py:1088
  106.1 5.7 collective-permute-done.9.other
  114.9 12.7 %collective-permute-done.3 = bf16[208,768]{1,0:T(8,128)(2,1)S(1)} collective-permute-done((bf16[208,768]{1,0:T(8,128)(2,1)S(1)}, bf16[208,768]{1,0:T(8,128)(2,1)S(1)}, u32[]{:S(2)}, u32[]{:S(2)}) %collective-permute-start.3) | collective-permute-done | bytes 319520 | tf_op jit(solution)/shard_map/ppermute | solution.py:1088
  128.4 14.6 %collective-permute-done.7 = bf16[2,208,768]{2,1,0:T(8,128)(2,1)S(1)} collective-permute-done((bf16[2,208,768]{2,1,0:T(8,128)(2,1)S(1)}, bf16[2,208,768]{2,1,0:T(8,128)(2,1)S(1)}, u32[]{:S(2)}, u32[]{:S(2)}) %collective-permute-start.7) | collective-permute-done | bytes 639008 | tf_op jit(solution)/shard_map/ppermute | solution.py:1088
  150.8 7.5 %collective-permute-done.16.rest_3_ = bf16[8,192,768]{2,1,0:T(8,128)(2,1)S(1)} collective-permute-done((bf16[8,192,768]{2,1,0:T(8,128)(2,1)S(1)}, bf16[8,192,768]{2,1,0:T(8,128)(2,1)S(1)}, u32[]{:S(2)}, u32[]{:S(2)}) %collective-permute-start.16) | collective-permute-done | bytes 2359328 | tf_op jit(solution)/shard_map/ppermute | solution.py:1088
  176.5 9.1 %attn.3 = (bf16[512,768]{1,0:T(8,128)(2,1)S(1)}, f32[2,16,256]{2,1,0:T(8,128)S(1)}) custom-call(s32[8]{0:T(128)S(1)} %stack.165.meta, bf16[512,768]{1,0:T(8,128)(2,1)S(1)} %copy-done.7, bf16[2,512,768]{2,1,0:T(8,128)(2,1)S(1)} %get-tuple-element.188.ko.vo, bf16[2,512,768]{2,1,0:T(8,128)(2,1)S(1)} %get-tuple-element.188.ko.vo, ...), custom_call_target="tpu_custom_call" | custom-call | flops 40265320 | bytes 1024 | tf_op jit(solution)/shard_map/attn/pallas_call | solution.py:787
  185.6 13.3 %mlp.3 = (f32[512,768]{1,0:T(8,128)S(1)}, bf16[4,512,768]{2,1,0:T(8,128)(2,1)}, f32[512,768]{1,0:T(8,128)S(1)}) custom-call(s32[8]{0:T(128)S(1)} %stack.165.meta, f32[512,768]{1,0:T(8,128)} %copy-done, bf16[512,768]{1,0:T(8,128)(2,1)S(1)} %get-tuple-element.189.mixed, bf16[8,208,768]{2,1,0:T(8,128)(2,1)} %assemble.4.rest_0_, ...), custom_call_target="tpu_custom_call" | custom-call | flops 54358180 | bytes 1024 | tf_op jit(solution)/shard_map/mlp/pallas_call | solution.py:818
  198.9 5.5 collective-permute-done.21.rest_10_
  222.8 9.3 %attn.4 = (bf16[512,768]{1,0:T(8,128)(2,1)S(1)}, f32[2,16,256]{2,1,0:T(8,128)S(1)}) custom-call(s32[8]{0:T(128)S(1)} %stack.164.meta, bf16[512,768]{1,0:T(8,128)(2,1)S(1)} %get-tuple-element.196.q_ref, bf16[2,512,768]{2,1,0:T(8,128)(2,1)S(1)} %get-tuple-element.197.ko.vo, bf16[2,512,768]{2,1,0:T(8,128)(2,1)S(1)} %get-tuple-element.197.ko.vo, ...), custom_call_target="tpu_custom_call" | custom-call | flops 32212254720 | bytes 1024 | tf_op jit(solution)/shard_map/attn/pallas_call | solution.py:787
  233.5 12.9 %mlp.4 = (f32[512,768]{1,0:T(8,128)S(1)}, bf16[4,512,768]{2,1,0:T(8,128)(2,1)}, f32[512,768]{1,0:T(8,128)S(1)}) custom-call(s32[8]{0:T(128)S(1)} %stack.164.meta, f32[512,768]{1,0:T(8,128)} %copy-done.16, bf16[512,768]{1,0:T(8,128)(2,1)S(1)} %get-tuple-element.198.mixed, bf16[8,208,768]{2,1,0:T(8,128)(2,1)} %assemble.4.rest_0_, ...), custom_call_target="tpu_custom_call" | custom-call | flops 43486543872 | bytes 1024 | tf_op jit(solution)/shard_map/mlp/pallas_call | solution.py:818
  256.2 9.1 %attn.5 = (bf16[512,768]{1,0:T(8,128)(2,1)S(1)}, f32[2,16,256]{2,1,0:T(8,128)S(1)}) custom-call(s32[8]{0:T(128)S(1)} %stack.163.meta, bf16[512,768]{1,0:T(8,128)(2,1)S(1)} %get-tuple-element.200.q_ref, bf16[2,512,768]{2,1,0:T(8,128)(2,1)S(1)} %get-tuple-element.201.ko.vo, bf16[2,512,768]{2,1,0:T(8,128)(2,1)S(1)} %get-tuple-element.201.ko.vo, ...), custom_call_target="tpu_custom_call" | custom-call | flops 32212254720 | bytes 1024 | tf_op jit(solution)/shard_map/attn/pallas_call | solution.py:787
  265.3 13.0 %mlp.5 = (f32[512,768]{1,0:T(8,128)S(1)}, bf16[4,512,768]{2,1,0:T(8,128)(2,1)}, f32[512,768]{1,0:T(8,128)S(1)}) custom-call(s32[8]{0:T(128)S(1)} %stack.163.meta, f32[512,768]{1,0:T(8,128)} %copy-done.23, bf16[512,768]{1,0:T(8,128)(2,1)S(1)} %get-tuple-element.202.mixed, bf16[8,208,768]{2,1,0:T(8,128)(2,1)} %assemble.4.rest_0_, ...), custom_call_target="tpu_custom_call" | custom-call | flops 43486543872 | bytes 1024 | tf_op jit(solution)/shard_map/mlp/pallas_call | solution.py:818
  283.6 25.3 %mlp_back.3 = (f32[512,768]{1,0:T(8,128)}, bf16[512,768]{1,0:T(8,128)(2,1)S(1)}, f32[2,16,256]{2,1,0:T(8,128)S(1)}, f32[16,768]{1,0:T(8,128)S(1)}, bf16[8,2,384,...) custom-call(s32[8]{0:T(128)S(1)} %stack.163.meta, f32[2]{0:T(128)S(1)} %add_convert_fusion.keep_ref, ...), custom_call_target="tpu_custom_call" | custom-call | flops 86973087744 | bytes 1024 | tf_op jit(solution)/shard_map/mlp_back/pallas_call | solution.py:845
  310.1 17.6 %attn_back.3 = (bf16[512,768]{1,0:T(8,128)(2,1)S(1)}, bf16[2,512,768]{2,1,0:T(8,128)(2,1)S(1)}, bf16[1,2,512,768]{3,2,1,0:T(8,128)(2,1)}) custom-call(s32[8]{0:T(128)S(1)} %stack.163.meta, bf16[512,768]{1,0:T(8,128)(2,1)S(1)} %get-tuple-element.200.q_ref, bf16[2,512,768]{2,1,0:T(8,128)(2,1)} %copy-done.18, bf16[2,512,768]{2,1,0:T(8,128)(2,1)} %copy-done.18, ...), custom_call_target="tpu_custom_call" | custom-call | flops 80530636800 | bytes 1024 | tf_op jit(solution)/shard_map/attn_back/pallas_call | solution.py:870
  333.7 11.1 %qkv_back.3 = (f32[512,768]{1,0:T(8,128)S(1)}, bf16[8,2,160,768]{3,2,1,0:T(8,128)(2,1)}) custom-call(s32[8]{0:T(128)S(1)} %stack.163.meta, f32[2]{0:T(128)S(1)} %add_convert_fusion.keep_ref, f32[512,768]{1,0:T(8,128)S(1)} %copy-done.24, bf16[512,768]{1,0:T(8,128)(2,1)S(1)} %get-tuple-element.210.dq, bf16[2,512,768]{2,1,0:T(8,128)(2,1)} %copy-done.29, ...), custom_call_target="tpu_custom_call" | custom-call | flops 28991029248 | bytes 1024 | tf_op jit(solution)/shard_map/qkv_back/pallas_call | solution.py:897
  345.9 30.5 %mlp_back.4 = (f32[512,768]{1,0:T(8,128)}, bf16[512,768]{1,0:T(8,128)(2,1)S(1)}, f32[2,16,256]{2,1,0:T(8,128)S(1)}, f32[16,768]{1,0:T(8,128)S(1)}, bf16[8,384,76...) custom-call(s32[8]{0:T(128)S(1)} %stack.164.meta, ...), custom_call_target="tpu_custom_call" | custom-call | flops 86973087744 | bytes 1024 | tf_op jit(solution)/shard_map/mlp_back/pallas_call | solution.py:845
  376.7 17.3 %attn_back.4 = (bf16[512,768]{1,0:T(8,128)(2,1)S(1)}, bf16[2,512,768]{2,1,0:T(8,128)(2,1)S(1)}, bf16[1,2,512,768]{3,2,1,0:T(8,128)(2,1)}) custom-call(s32[8]{0:T(128)S(1)} %stack.164.meta, bf16[512,768]{1,0:T(8,128)(2,1)S(1)} %get-tuple-element.196.q_ref, bf16[2,512,768]{2,1,0:T(8,128)(2,1)} %copy-done.17, bf16[2,512,768]{2,1,0:T(8,128)(2,1)} %copy-done.17, ...), custom_call_target="tpu_custom_call" | custom-call | flops 80530636800 | bytes 1024 | tf_op jit(solution)/shard_map/attn_back/pallas_call | solution.py:870
  395.5 5.8 add_cores.4
  404.2 14.9 %qkv_back.4 = (f32[512,768]{1,0:T(8,128)S(1)}, bf16[8,208,768]{2,1,0:T(8,128)(2,1)}, bf16[8,208,768]{2,1,0:T(8,128)(2,1)}, bf16[8,2,160,768]{3,2,1,0:T(8,128)(2,1)}) custom-call(s32[8]{0:T(128)S(1)} %stack.164.meta, f32[2]{0:T(128)S(1)} %add_convert_fusion.keep_ref, f32[512,768]{1,0:T(8,128)} %copy-done.16, bf16[512,768]{1,0:T(8,128)(2,1)S(1)} %get-tuple-element.223.dq, ...), custom_call_target="tpu_custom_call" | custom-call | flops 28991029248 | bytes 1024 | tf_op jit(solution)/shard_map/qkv_back/pallas_call | solution.py:897
  420.2 27.3 %mlp_back.5 = (f32[512,768]{1,0:T(8,128)}, bf16[512,768]{1,0:T(8,128)(2,1)S(1)}, f32[2,16,256]{2,1,0:T(8,128)S(1)}, f32[16,768]{1,0:T(8,128)S(1)}, bf16[8,384,76...) custom-call(s32[8]{0:T(128)S(1)} %stack.165.meta, ...), custom_call_target="tpu_custom_call" | custom-call | flops 86973087744 | bytes 1024 | tf_op jit(solution)/shard_map/mlp_back/pallas_call | solution.py:845
  463.1 5.7 add_cores.6
  469.8 17.4 %attn_back.5 = (bf16[512,768]{1,0:T(8,128)(2,1)S(1)}, bf16[2,512,768]{2,1,0:T(8,128)(2,1)S(1)}, bf16[1,2,512,768]{3,2,1,0:T(8,128)(2,1)}) custom-call(s32[8]{0:T(128)S(1)} %stack.165.meta, bf16[512,768]{1,0:T(8,128)(2,1)S(1)} %copy-done.8, bf16[2,512,768]{2,1,0:T(8,128)(2,1)} %copy-done.1, bf16[2,512,768]{2,1,0:T(8,128)(2,1)} %copy-done.1, ...), custom_call_target="tpu_custom_call" | custom-call | flops 80530636800 | bytes 1024 | tf_op jit(solution)/shard_map/attn_back/pallas_call | solution.py:870
  505.7 13.0 %qkv_back.5 = (f32[512,768]{1,0:T(8,128)S(1)}, bf16[8,208,768]{2,1,0:T(8,128)(2,1)}, bf16[8,208,768]{2,1,0:T(8,128)(2,1)}) custom-call(s32[8]{0:T(128)S(1)} %stack.165.meta, f32[2]{0:T(128)S(1)} %copy-done.22, f32[512,768]{1,0:T(8,128)} %copy-done, bf16[512,768]{1,0:T(8,128)(2,1)S(1)} %get-tuple-element.256.dq, bf16[2,512,768]{2,1,0:T(8,128)(2,1)} %copy-done.27, ...), custom_call_target="tpu_custom_call" | custom-call | flops 28991029248 | bytes 1024 | tf_op jit(solution)/shard_map/qkv_back/pallas_call | solution.py:897
  529.4 13.1 %collective-permute-done.47.refs_3_ = bf16[4,192,768]{2,1,0:T(8,128)(2,1)} collective-permute-done((bf16[4,192,768]{2,1,0:T(8,128)(2,1)}, bf16[4,192,768]{2,1,0:T(8,128)(2,1)}, u32[]{:S(2)}, u32[]{:S(2)}) %collective-permute-start.47) | collective-permute-done | bytes 1179680 | tf_op jit(solution)/shard_map/ppermute | solution.py:1088
  549.4 11.6 %collective-permute-done.52.refs_1_ = bf16[8,112,768]{2,1,0:T(8,128)(2,1)S(1)} collective-permute-done((bf16[8,112,768]{2,1,0:T(8,128)(2,1)S(1)}, bf16[8,112,768]{2,1,0:T(8,128)(2,1)S(1)}, u32[]{:S(2)}, u32[]{:S(2)}) %collective-permute-start.52) | collective-permute-done | bytes 1376288 | tf_op jit(solution)/shard_map/ppermute | solution.py:1088
  567.9 12.6 %collective-permute-done.56.refs_1_ = bf16[4,112,768]{2,1,0:T(8,128)(2,1)S(1)} collective-permute-done((bf16[4,112,768]{2,1,0:T(8,128)(2,1)S(1)}, bf16[4,112,768]{2,1,0:T(8,128)(2,1)S(1)}, u32[]{:S(2)}, u32[]{:S(2)}) %collective-permute-start.56) | collective-permute-done | bytes 688160 | tf_op jit(solution)/shard_map/ppermute | solution.py:1088
  586.1 6.7 %collective-permute-done.59.refs_1_ = bf16[2,112,768]{2,1,0:T(8,128)(2,1)S(1)} collective-permute-done((bf16[2,112,768]{2,1,0:T(8,128)(2,1)S(1)}, bf16[2,112,768]{2,1,0:T(8,128)(2,1)S(1)}, u32[]{:S(2)}, u32[]{:S(2)}) %collective-permute-start.59) | collective-permute-done | bytes 344096 | tf_op jit(solution)/shard_map/ppermute | solution.py:1088
  607.2 7.3 %collective-permute-done.50.refs_1_ = bf16[96,768]{1,0:T(8,128)(2,1)S(1)} collective-permute-done((bf16[96,768]{1,0:T(8,128)(2,1)S(1)}, bf16[96,768]{1,0:T(8,128)(2,1)S(1)}, u32[]{:S(2)}, u32[]{:S(2)}) %collective-permute-start.50) | collective-permute-done | bytes 147488 | tf_op jit(solution)/shard_map/ppermute | solution.py:1088
  (292 shorter events, 205.1 us)
Async XLA Ops:
  27.7 20.9 %collective-permute-start.4 = (bf16[2,192,768]{2,1,0:T(8,128)(2,1)S(1)}, bf16[2,192,768]{2,1,0:T(8,128)(2,1)S(1)}, u32[]{:S(2)}, u32[]{:S(2)}) collective-permute-start(bf16[2,192,768]{2,1,0:T(8,128)(2,1)S(1)} %get-tuple-element.341), channel_id=1, source_target_pairs={{0,8},{1,9},{2,10},{3,11},{4,12},{5,13},{6,14},{7,15},{8,0},{9,1},... | collective-permute-start | bytes 1769480 | tf_op jit(solution)/shard_map/ppermute | solution.py:1088
  28.5 30.6 %collective-permute-start.1 = (bf16[192,768]{1,0:T(8,128)(2,1)S(1)}, bf16[192,768]{1,0:T(8,128)(2,1)S(1)}, u32[]{:S(2)}, u32[]{:S(2)}) collective-permute-start(bf16[192,768]{1,0:T(8,128)(2,1)S(1)} %get-tuple-element.173), channel_id=1, source_target_pairs={{0,16},{1,17},{2,18},{3,19},{4,20},{5,21},{6,22},{7,23},{8,24},{9,... | collective-permute-start | bytes 884744 | tf_op jit(solution)/shard_map/ppermute | solution.py:1088
  48.8 35.8 %collective-permute-start.8 = (bf16[2,2,192,768]{3,2,1,0:T(8,128)(2,1)S(1)}, bf16[2,2,192,768]{3,2,1,0:T(8,128)(2,1)S(1)}, u32[]{:S(2)}, u32[]{:S(2)}) collective-permute-start(bf16[2,2,192,768]{3,2,1,0:T(8,128)(2,1)S(1)} %pad_maximum_fusion.2.mine), channel_id=1, source_target_pairs={{0,4},{1,5},{2,6},{3,7},{4,0},{5,1},{6,2},{7,3},{8,12},{9,13},{10,... | collective-permute-start | bytes 3538952 | tf_op jit(solution)/shard_map/ppermute | solution.py:1088
  60.7 22.5 %collective-permute-start.5 = (bf16[2,192,768]{2,1,0:T(8,128)(2,1)}, bf16[2,192,768]{2,1,0:T(8,128)(2,1)}, u32[]{:S(2)}, u32[]{:S(2)}) collective-permute-start(bf16[2,192,768]{2,1,0:T(8,128)(2,1)} %pad_maximum_fusion.7), channel_id=1, source_target_pairs={{0,8},{1,9},{2,10},{3,11},{4,12},{5,13},{6,14},{7,15},{8,0},{9,1},... | collective-permute-start | bytes 1769480 | tf_op jit(solution)/shard_map/ppermute | solution.py:1088
  63.6 27.2 %collective-permute-start.2 = (bf16[208,768]{1,0:T(8,128)(2,1)S(1)}, bf16[208,768]{1,0:T(8,128)(2,1)S(1)}, u32[]{:S(2)}, u32[]{:S(2)}) collective-permute-start(bf16[208,768]{1,0:T(8,128)(2,1)S(1)} %get-tuple-element.174), channel_id=1, source_target_pairs={{0,16},{1,17},{2,18},{3,19},{4,20},{5,21},{6,22},{7,23},{8,24},{9,... | collective-permute-start | bytes 958472 | tf_op jit(solution)/shard_map/ppermute | solution.py:1088
  84.6 27.2 %collective-permute-start.9 = (bf16[2,2,192,768]{3,2,1,0:T(8,128)(2,1)S(1)}, bf16[2,2,192,768]{3,2,1,0:T(8,128)(2,1)S(1)}, u32[]{:S(2)}, u32[]{:S(2)}) collective-permute-start(bf16[2,2,192,768]{3,2,1,0:T(8,128)(2,1)S(1)} %pad_maximum_fusion.3.mine), channel_id=1, source_target_pairs={{0,4},{1,5},{2,6},{3,7},{4,0},{5,1},{6,2},{7,3},{8,12},{9,13},{10,... | collective-permute-start | bytes 3538952 | tf_op jit(solution)/shard_map/ppermute | solution.py:1088
  90.5 59.9 %collective-permute-start.17 = (bf16[8,192,768]{2,1,0:T(8,128)(2,1)}, bf16[8,192,768]{2,1,0:T(8,128)(2,1)S(1)}, u32[]{:S(2)}, u32[]{:S(2)}) collective-permute-start(bf16[8,192,768]{2,1,0:T(8,128)(2,1)} %assemble.5.rest_2_), channel_id=1, source_target_pairs={{0,1},{1,0},{2,3},{3,2},{4,5},{5,4},{6,7},{7,6},{8,9},{9,8},{10,11... | collective-permute-start | bytes 7077896 | tf_op jit(solution)/shard_map/ppermute | solution.py:1088
  111.8 32.3 %collective-permute-start.10 = (bf16[2,2,208,768]{3,2,1,0:T(8,128)(2,1)S(1)}, bf16[2,2,208,768]{3,2,1,0:T(8,128)(2,1)S(1)}, u32[]{:S(2)}, u32[]{:S(2)}) collective-permute-start(bf16[2,2,208,768]{3,2,1,0:T(8,128)(2,1)S(1)} %pad_maximum_fusion.mine), channel_id=1, source_target_pairs={{0,4},{1,5},{2,6},{3,7},{4,0},{5,1},{6,2},{7,3},{8,12},{9,13},{10,... | collective-permute-start | bytes 3833864 | tf_op jit(solution)/shard_map/ppermute | solution.py:1088
  150.8 53.6 %collective-permute-start.21 = (bf16[8,192,768]{2,1,0:T(8,128)(2,1)}, bf16[8,192,768]{2,1,0:T(8,128)(2,1)}, u32[]{:S(2)}, u32[]{:S(2)}) collective-permute-start(bf16[8,192,768]{2,1,0:T(8,128)(2,1)} %assemble.6.rest_8_), channel_id=1, source_target_pairs={{0,1},{1,0},{2,3},{3,2},{4,5},{5,4},{6,7},{7,6},{8,9},{9,8},{10,11... | collective-permute-start | bytes 7077896 | tf_op jit(solution)/shard_map/ppermute | solution.py:1088
  171.9 32.4 %collective-permute-start.22 = (bf16[2,2,208,768]{3,2,1,0:T(8,128)(2,1)}, bf16[2,2,208,768]{3,2,1,0:T(8,128)(2,1)S(1)}, u32[]{:S(2)}, u32[]{:S(2)}) collective-permute-start(bf16[2,2,208,768]{3,2,1,0:T(8,128)(2,1)} %pad_maximum_fusion.1.mine), channel_id=1, source_target_pairs={{0,4},{1,5},{2,6},{3,7},{4,0},{5,1},{6,2},{7,3},{8,12},{9,13},{10,... | collective-permute-start | bytes 3833864 | tf_op jit(solution)/shard_map/ppermute | solution.py:1088
  279.5 29.4 %collective-permute-start.27 = (bf16[256,768]{1,0:T(8,128)(2,1)S(1)}, bf16[256,768]{1,0:T(8,128)(2,1)S(1)}, u32[]{:S(2)}, u32[]{:S(2)}) collective-permute-start(bf16[256,768]{1,0:T(8,128)(2,1)S(1)} %get-tuple-element.330), channel_id=1, source_target_pairs={{0,0},{2,1},{1,2},{3,3},{4,4},{6,5},{5,6},{7,7},{8,8},{10,9},{9,10... | collective-permute-start | bytes 1179656 | tf_op jit(solution)/shard_map/ppermute | solution.py:1053
  280.5 28.3 %collective-permute-start.28 = (bf16[256,768]{1,0:T(8,128)(2,1)S(1)}, bf16[256,768]{1,0:T(8,128)(2,1)S(1)}, u32[]{:S(2)}, u32[]{:S(2)}) collective-permute-start(bf16[256,768]{1,0:T(8,128)(2,1)S(1)} %get-tuple-element.331), channel_id=1, source_target_pairs={{2,0},{0,1},{3,2},{1,3},{6,4},{4,5},{7,6},{5,7},{10,8},{8,9},{11,1... | collective-permute-start | bytes 1179656 | tf_op jit(solution)/shard_map/ppermute | solution.py:1054
  376.5 19.1 %collective-permute-start.30 = (bf16[8,384,768]{2,1,0:T(8,128)(2,1)}, bf16[8,384,768]{2,1,0:T(8,128)(2,1)}, u32[]{:S(2)}, u32[]{:S(2)}) collective-permute-start(bf16[8,384,768]{2,1,0:T(8,128)(2,1)} %get-tuple-element.226), channel_id=1, source_target_pairs={{0,2},{1,3},{2,0},{3,1},{4,6},{5,7},{6,4},{7,5},{8,10},{9,11},{10,... | collective-permute-start | bytes 14155784 | tf_op jit(solution)/shard_map/ppermute | solution.py:1088
  401.3 53.7 %collective-permute-start.33 = (bf16[8,96,768]{2,1,0:T(8,128)(2,1)S(1)}, bf16[8,96,768]{2,1,0:T(8,128)(2,1)S(1)}, u32[]{:S(2)}, u32[]{:S(2)}) collective-permute-start(bf16[8,96,768]{2,1,0:T(8,128)(2,1)S(1)} %get-tuple-element.245), channel_id=1, source_target_pairs={{0,1},{1,0},{2,3},{3,2},{4,5},{5,4},{6,7},{7,6},{8,9},{9,8},{10,11... | collective-permute-start | bytes 3538952 | tf_op jit(solution)/shard_map/ppermute | solution.py:1088
  401.4 53.6 %collective-permute-start.34 = (bf16[4,192,768]{2,1,0:T(8,128)(2,1)}, bf16[4,192,768]{2,1,0:T(8,128)(2,1)}, u32[]{:S(2)}, u32[]{:S(2)}) collective-permute-start(bf16[4,192,768]{2,1,0:T(8,128)(2,1)} %get-tuple-element.247), channel_id=1, source_target_pairs={{0,4},{1,5},{2,6},{3,7},{4,0},{5,1},{6,2},{7,3},{8,12},{9,13},{10,... | collective-permute-start | bytes 3538952 | tf_op jit(solution)/shard_map/ppermute | solution.py:1088
  420.2 28.7 %collective-permute-start.32 = (bf16[8,208,768]{2,1,0:T(8,128)(2,1)}, bf16[8,208,768]{2,1,0:T(8,128)(2,1)S(1)}, u32[]{:S(2)}, u32[]{:S(2)}) collective-permute-start(bf16[8,208,768]{2,1,0:T(8,128)(2,1)} %get-tuple-element.242), channel_id=1, source_target_pairs={{0,2},{1,3},{2,0},{3,1},{4,6},{5,7},{6,4},{7,5},{8,10},{9,11},{10,... | collective-permute-start | bytes 7667720 | tf_op jit(solution)/shard_map/ppermute | solution.py:1088
  458.8 29.5 %collective-permute-start.36 = (bf16[4,96,768]{2,1,0:T(8,128)(2,1)S(1)}, bf16[4,96,768]{2,1,0:T(8,128)(2,1)S(1)}, u32[]{:S(2)}, u32[]{:S(2)}) collective-permute-start(bf16[4,96,768]{2,1,0:T(8,128)(2,1)S(1)} %get-tuple-element.258), channel_id=1, source_target_pairs={{0,4},{1,5},{2,6},{3,7},{4,0},{5,1},{6,2},{7,3},{8,12},{9,13},{10,... | collective-permute-start | bytes 1769480 | tf_op jit(solution)/shard_map/ppermute | solution.py:1088
  459.4 28.9 %collective-permute-start.37 = (bf16[2,192,768]{2,1,0:T(8,128)(2,1)S(1)}, bf16[2,192,768]{2,1,0:T(8,128)(2,1)S(1)}, u32[]{:S(2)}, u32[]{:S(2)}) collective-permute-start(bf16[2,192,768]{2,1,0:T(8,128)(2,1)S(1)} %get-tuple-element.260), channel_id=1, source_target_pairs={{0,8},{1,9},{2,10},{3,11},{4,12},{5,13},{6,14},{7,15},{8,0},{9,1},... | collective-permute-start | bytes 1769480 | tf_op jit(solution)/shard_map/ppermute | solution.py:1088
  461.1 31.8 %collective-permute-start.38 = (bf16[8,112,768]{2,1,0:T(8,128)(2,1)S(1)}, bf16[8,112,768]{2,1,0:T(8,128)(2,1)S(1)}, u32[]{:S(2)}, u32[]{:S(2)}) collective-permute-start(bf16[8,112,768]{2,1,0:T(8,128)(2,1)S(1)} %get-tuple-element.261), channel_id=1, source_target_pairs={{0,1},{1,0},{2,3},{3,2},{4,5},{5,4},{6,7},{7,6},{8,9},{9,8},{10,11... | collective-permute-start | bytes 4128776 | tf_op jit(solution)/shard_map/ppermute | solution.py:1088
  497.6 21.1 %collective-permute-start.42 = (bf16[2,96,768]{2,1,0:T(8,128)(2,1)S(1)}, bf16[2,96,768]{2,1,0:T(8,128)(2,1)S(1)}, u32[]{:S(2)}, u32[]{:S(2)}) collective-permute-start(bf16[2,96,768]{2,1,0:T(8,128)(2,1)S(1)} %get-tuple-element.272), channel_id=1, source_target_pairs={{0,8},{1,9},{2,10},{3,11},{4,12},{5,13},{6,14},{7,15},{8,0},{9,1},... | collective-permute-start | bytes 884744 | tf_op jit(solution)/shard_map/ppermute | solution.py:1088
  497.9 20.9 %collective-permute-start.43 = (bf16[1,192,768]{2,1,0:T(8,128)(2,1)S(1)}, bf16[1,192,768]{2,1,0:T(8,128)(2,1)S(1)}, u32[]{:S(2)}, u32[]{:S(2)}) collective-permute-start(bf16[1,192,768]{2,1,0:T(8,128)(2,1)S(1)} %get-tuple-element.274), channel_id=1, source_target_pairs={{0,16},{1,17},{2,18},{3,19},{4,20},{5,21},{6,22},{7,23},{8,24},{9,... | collective-permute-start | bytes 884744 | tf_op jit(solution)/shard_map/ppermute | solution.py:1088
  501.3 18.6 %collective-permute-start.44 = (bf16[4,112,768]{2,1,0:T(8,128)(2,1)}, bf16[4,112,768]{2,1,0:T(8,128)(2,1)S(1)}, u32[]{:S(2)}, u32[]{:S(2)}) collective-permute-start(bf16[4,112,768]{2,1,0:T(8,128)(2,1)} %get-tuple-element.276), channel_id=1, source_target_pairs={{0,4},{1,5},{2,6},{3,7},{4,0},{5,1},{6,2},{7,3},{8,12},{9,13},{10,... | collective-permute-start | bytes 2064392 | tf_op jit(solution)/shard_map/ppermute | solution.py:1088
  502.8 26.6 %collective-permute-start.46 = (bf16[8,96,768]{2,1,0:T(8,128)(2,1)S(1)}, bf16[8,96,768]{2,1,0:T(8,128)(2,1)S(1)}, u32[]{:S(2)}, u32[]{:S(2)}) collective-permute-start(bf16[8,96,768]{2,1,0:T(8,128)(2,1)S(1)} %get-tuple-element.283), channel_id=1, source_target_pairs={{0,1},{1,0},{2,3},{3,2},{4,5},{5,4},{6,7},{7,6},{8,9},{9,8},{10,11... | collective-permute-start | bytes 3538952 | tf_op jit(solution)/shard_map/ppermute | solution.py:1088
  504.6 37.9 %collective-permute-start.47 = (bf16[4,192,768]{2,1,0:T(8,128)(2,1)}, bf16[4,192,768]{2,1,0:T(8,128)(2,1)}, u32[]{:S(2)}, u32[]{:S(2)}) collective-permute-start(bf16[4,192,768]{2,1,0:T(8,128)(2,1)} %get-tuple-element.285), channel_id=1, source_target_pairs={{0,4},{1,5},{2,6},{3,7},{4,0},{5,1},{6,2},{7,3},{8,12},{9,13},{10,... | collective-permute-start | bytes 3538952 | tf_op jit(solution)/shard_map/ppermute | solution.py:1088
  520.7 27.7 %collective-permute-start.48 = (bf16[1,96,768]{2,1,0:T(8,128)(2,1)S(1)}, bf16[1,96,768]{2,1,0:T(8,128)(2,1)S(1)}, u32[]{:S(2)}, u32[]{:S(2)}) collective-permute-start(bf16[1,96,768]{2,1,0:T(8,128)(2,1)S(1)} %get-tuple-element.288), channel_id=1, source_target_pairs={{0,16},{1,17},{2,18},{3,19},{4,20},{5,21},{6,22},{7,23},{8,24},{9,... | collective-permute-start | bytes 442376 | tf_op jit(solution)/shard_map/ppermute | solution.py:1088
  520.8 27.6 %collective-permute-start.49 = (bf16[2,112,768]{2,1,0:T(8,128)(2,1)S(1)}, bf16[2,112,768]{2,1,0:T(8,128)(2,1)S(1)}, u32[]{:S(2)}, u32[]{:S(2)}) collective-permute-start(bf16[2,112,768]{2,1,0:T(8,128)(2,1)S(1)} %get-tuple-element.290), channel_id=1, source_target_pairs={{0,8},{1,9},{2,10},{3,11},{4,12},{5,13},{6,14},{7,15},{8,0},{9,1},... | collective-permute-start | bytes 1032200 | tf_op jit(solution)/shard_map/ppermute | solution.py:1088
  528.7 32.3 %collective-permute-start.52 = (bf16[8,112,768]{2,1,0:T(8,128)(2,1)S(1)}, bf16[8,112,768]{2,1,0:T(8,128)(2,1)S(1)}, u32[]{:S(2)}, u32[]{:S(2)}) collective-permute-start(bf16[8,112,768]{2,1,0:T(8,128)(2,1)S(1)} %get-tuple-element.294), channel_id=1, source_target_pairs={{0,1},{1,0},{2,3},{3,2},{4,5},{5,4},{6,7},{7,6},{8,9},{9,8},{10,11... | collective-permute-start | bytes 4128776 | tf_op jit(solution)/shard_map/ppermute | solution.py:1088
  545.1 19.7 %collective-permute-start.54 = (bf16[4,96,768]{2,1,0:T(8,128)(2,1)S(1)}, bf16[4,96,768]{2,1,0:T(8,128)(2,1)S(1)}, u32[]{:S(2)}, u32[]{:S(2)}) collective-permute-start(bf16[4,96,768]{2,1,0:T(8,128)(2,1)S(1)} %get-tuple-element.299), channel_id=1, source_target_pairs={{0,4},{1,5},{2,6},{3,7},{4,0},{5,1},{6,2},{7,3},{8,12},{9,13},{10,... | collective-permute-start | bytes 1769480 | tf_op jit(solution)/shard_map/ppermute | solution.py:1088
  567.5 36.3 %collective-permute-start.51 = (bf16[192,768]{1,0:T(8,128)(2,1)S(1)}, bf16[192,768]{1,0:T(8,128)(2,1)S(1)}, u32[]{:S(2)}, u32[]{:S(2)}) collective-permute-start(bf16[192,768]{1,0:T(8,128)(2,1)S(1)} %get-tuple-element.292.refs_2_), channel_id=1, source_target_pairs={{0,1},{1,0},{2,3},{3,2},{4,5},{5,4},{6,7},{7,6},{8,9},{9,8},{10,11... | collective-permute-start | bytes 884744 | tf_op jit(solution)/shard_map/ppermute | solution.py:1088
  583.9 20.4 %collective-permute-start.40 = (bf16[256,768]{1,0:T(8,128)(2,1)S(1)}, bf16[256,768]{1,0:T(8,128)(2,1)S(1)}, u32[]{:S(2)}, u32[]{:S(2)}) collective-permute-start(bf16[256,768]{1,0:T(8,128)(2,1)S(1)} %get-tuple-element.328), channel_id=1, source_target_pairs={{0,0},{2,1},{1,2},{3,3},{4,4},{6,5},{5,6},{7,7},{8,8},{10,9},{9,10... | collective-permute-start | bytes 1179656 | tf_op jit(solution)/shard_map/ppermute | solution.py:1053
  584.6 21.4 %collective-permute-start.41 = (bf16[256,768]{1,0:T(8,128)(2,1)S(1)}, bf16[256,768]{1,0:T(8,128)(2,1)S(1)}, u32[]{:S(2)}, u32[]{:S(2)}) collective-permute-start(bf16[256,768]{1,0:T(8,128)(2,1)S(1)} %get-tuple-element.329), channel_id=1, source_target_pairs={{2,0},{0,1},{3,2},{1,3},{6,4},{4,5},{7,6},{5,7},{10,8},{8,9},{11,1... | collective-permute-start | bytes 1179656 | tf_op jit(solution)/shard_map/ppermute | solution.py:1054
  592.8 21.7 %collective-permute-start.62 = (bf16[192,768]{1,0:T(8,128)(2,1)S(1)}, bf16[192,768]{1,0:T(8,128)(2,1)S(1)}, u32[]{:S(2)}, u32[]{:S(2)}) collective-permute-start(bf16[192,768]{1,0:T(8,128)(2,1)S(1)} %get-tuple-element.317.refs_6_), channel_id=1, source_target_pairs={{0,1},{1,0},{2,3},{3,2},{4,5},{5,4},{6,7},{7,6},{8,9},{9,8},{10,11... | collective-permute-start | bytes 884744 | tf_op jit(solution)/shard_map/ppermute | solution.py:1088
  (96 other events, 1020.0 us)

commit v2 on v1

--- a/solution.py
+++ b/solution.py
@@ -293,8 +293,8 @@
     rest = rest[4:]
     done = mode > 0
     if done:
-        done_mine, done_other, done_o = rest[:3]
-        rest = rest[3:]
+        done_mine, done_other = rest[:2]
+        rest = rest[2:]
     if mode < 2:
         open_b, open_o = rest[:2]
         rest = rest[2:]
@@ -417,13 +417,17 @@
     if mode:
         prev_o_copy.wait()
     prev = bufs[-1][2][...].reshape(D, D) if mode else None
-    o_refs = ([done_o] if done else []) + ([open_o] if mode < 2 else [])
     o_copies = []
     for which, term in enumerate(sort_terms(mode, keep, g_out, prev)):
-        bufs[which][2][...] = term.astype(BF).reshape(NG // 2, 2, GR, D)
-        copy = pltpu.make_async_copy(bufs[which][2], o_refs[which], osems.at[6 + which, 0])
+        buf = bufs[which][2]
+        buf[...] = term.astype(BF).reshape(NG // 2, 2, GR, D)
+        if done and which == 0:
+            views = [rows_of(ref, NC * GR + PR, GR) for ref in (done_mine, done_other)]
+            o_copies += to_cores(buf, *views, core, osems.at[6, 0], osems.at[6, 1])
+        else:
+            o_copies.append(pltpu.make_async_copy(buf, open_o, osems.at[7, 0]))
+    for copy in o_copies:
         copy.start()
-        o_copies.append(copy)
     prod = d_mix.astype(F32) * mixed[...].astype(F32)
     big = prod.astype(BF)
     rest_part = (prod - big.astype(F32)).astype(BF)
@@ -500,8 +504,8 @@
     rest = rest[nw:]
     done = mode > 0
     if done:
-        prev_ref, done_o = rest[:2]
-        rest = rest[2:]
+        prev_ref = rest[0]
+        rest = rest[1:]
     nout = 2 if mode == 1 else 1
     dres = rest[0]
     rest = rest[1:]
@@ -518,20 +522,9 @@
     weights.start_small(prm, sems.at[0])
     weights.start_qk(wqk, sems.at[1])
     weights.start_v(wv, sems.at[2])
-    copies = []
     if done:
         prev_copy = pltpu.make_async_copy(prev_ref, bufs[-1], sems.at[3])
         prev_copy.start()
-        copies += to_cores(
-            done_o,
-            rows_of(done_mine, 3 * GR, GR),
-            rows_of(done_other, 3 * GR, GR),
-            core,
-            osems.at[0],
-            osems.at[1],
-        )
-        for copy in copies:
-            copy.start()
     landed(prm, sems.at[0])
     par = params_of(prm)
     xhat, rstd = norm_parts(resid[...])
@@ -573,21 +566,13 @@
         )
     later = []
     if done:
-        for k, (lo, size, to) in enumerate(((0, 3 * GR, 0), (3 * GR, SMALL, 4 * GR))):
-            later += to_cores(
-                rows_of(bufs[0], lo, size),
-                rows_of(done_mine, to, size),
-                rows_of(done_other, to, size),
-                core,
-                osems.at[2 + 2 * k],
-                osems.at[3 + 2 * k],
-            )
+        later += to_cores(bufs[0], done_mine, done_other, core, osems.at[0], osems.at[1])
     if mode < 2:
-        later.append(pltpu.make_async_copy(bufs[-1], open_a, osems.at[6]))
+        later.append(pltpu.make_async_copy(bufs[-1], open_a, osems.at[2]))
     for copy in later:
         copy.start()
     dres[...] = d_middle[...] + norm_back(xhat, rstd, par[0:1], dy)
-    for copy in copies + later:
+    for copy in later:
         copy.wait()
 
 
@@ -692,15 +677,20 @@
     line = lax.broadcasted_iota(jnp.int32, (SMALL, D), 0)
     here = line == 8 + at // (NG // NC)
 
-    def write(src, in_pair, proj_pair, qk, vo, small):
-        ins_ = (low(*in_pair), high(*in_pair))
-        for k in range(NC):
-            rows = slice(k % (NC // 2) * GR, (k % (NC // 2) + 1) * GR)
-            fc_g[src, :, k * D : (k + 1) * D] = ins_[k // (NC // 2)][rows].astype(F32)
-        proj_g[src] = proj_pair[0][...].astype(F32) + proj_pair[1][...].astype(F32)
-        for k, part in enumerate(qk + vo[:1]):
-            qkv_g[src, :, k * D : (k + 1) * D] = part
-        out_g[src] = vo[1]
+    for k, src in enumerate((1 - first, first)):
+        pairs = ins[4 * k : 4 * k + 4] + ins[8 + 2 * k : 10 + 2 * k]
+        halves = (low(*pairs[0:2]), high(*pairs[0:2]))
+        for c in range(NC):
+            half, at_row = divmod(c, NC // 2)
+            rows = halves[half][at_row * GR : (at_row + 1) * GR]
+            fc_g[src, :, c * D : (c + 1) * D] = rows.astype(F32)
+        sums = pairs[2][...].astype(F32) + pairs[3][...].astype(F32)
+        proj_g[src] = sums[:PR]
+        out_g[src] = sums[PR:]
+        attn = jnp.concatenate([low(*pairs[4:6]), high(*pairs[4:6])], 0)
+        for c in range(3):
+            qkv_g[src, :, c * D : (c + 1) * D] = attn[c * GR : (c + 1) * GR].astype(F32)
+        small = attn[3 * GR :]
         vals = dot(small, pick)
         row = jnp.sum(jnp.where(here, small.astype(F32), 0.0), 0, keepdims=True)
         hid = dot(jnp.broadcast_to(row, (8, D)).astype(BF), pick_h)
@@ -708,18 +698,6 @@
         shifts_g[src] = vals[2:4]
         bias_g[src] = vals[4:8]
         hidden_g[src] = hid[0:1]
-
-    for k, src in enumerate((1 - first, first)):
-        ins_ = ins[4 * k : 4 * k + 4] + ins[8 + 2 * k : 10 + 2 * k]
-        part_l, part_h = low(*ins_[4:6]), high(*ins_[4:6])
-        write(
-            src,
-            ins_[0:2],
-            ins_[2:4],
-            (part_l[:GR].astype(F32), part_l[GR : 2 * GR].astype(F32)),
-            (part_h[:GR].astype(F32), part_h[GR : 2 * GR].astype(F32)),
-            part_h[2 * GR :],
-        )
 
 
 VM = pl.BlockSpec(memory_space=pltpu.VMEM)
@@ -834,7 +812,7 @@
     o_shape = sds((NG // 2, 2, GR, D), BF)
     outs = ()
     if mode:
-        outs += (sds((NG // 2, b_rows, D), BF),) * 2 + (o_shape,)
+        outs += (sds((NG // 2, b_rows + GR, D), BF),) * 2
     if mode < 2:
         outs += (sds((NG // 2, 2, b_rows, D), BF), o_shape)
     stage = [
@@ -891,15 +869,15 @@
     shape = (NG // 2, 2, 3 * GR + SMALL, D)
     outs = ()
     if mode:
-        outs += (sds((NG // 2, 4 * GR + SMALL, D), BF),) * 2
+        outs += (sds((NG // 2, 3 * GR + SMALL, D), BF),) * 2
     if mode < 2:
         outs += (sds(shape, BF),)
     return call(
         functools.partial(qkv_back_kernel, kinds, mode, others),
         (sds((rows, D), F32),) + outs,
-        [SM, SM] + [VM] * 6 + [HB] * (len(weights) + min(mode, 1)) + [VM] * min(mode, 1),
+        [SM, SM] + [VM] * 6 + [HB] * (len(weights) + len(prev)),
         (VM,) + (HB,) * len(outs),
-        qkv_scratch() + [DMA((4,)), DMA((7,))] + [pltpu.VMEM(shape, BF)] * nout,
+        qkv_scratch() + [DMA((4,)), DMA((3,))] + [pltpu.VMEM(shape, BF)] * nout,
         4 * rows * D * 3 * D,
         "qkv_back",
     )(meta, keep, resid, dq, dkv, dkvx, d_middle, small, *weights, *prev)
@@ -1226,8 +1204,9 @@
         return [Scatter(seg[0], *outs[2 * i : 2 * i + 2]) for i, seg in enumerate(segs)], outs[0]
 
     in_rows, a_rows = NC // 2 * GR, 4 * GR + SMALL
-    b_segs = (("x", 0, in_rows, in_rows), ("y", NC * GR, 0, PR))
-    a_segs = (("x", 0, 2 * GR, 2 * GR + SMALL),)
+    b_segs = (("x", 0, in_rows, in_rows), ("y", NC * GR, 0, PR + GR))
+    half_a = (3 * GR + SMALL) // 2
+    a_segs = (("x", 0, half_a, half_a),)
 
     prev_b, prev_a = [], []
     shares, fin, opn = {}, [], []
@@ -1241,7 +1220,7 @@
         )
         d_middle, d_mixed, dt, small = outs[:4]
         if mode:
-            mine_b, other_b, done_o = outs[4:7]
+            mine_b, other_b = outs[4:6]
             if direct:
                 got_b = swap(other_b, "core")
         prev_b = list(outs[-2:])
@@ -1274,7 +1253,7 @@
             d_middle,
             small,
             *weights_of(u, True),
-            prev_a + ([done_o] if mode else []),
+            prev_a,
         )
         dres = outs[0]
         prev_a = [outs[-1]]
@@ -1289,20 +1268,23 @@
                 got_a = swap(other_a, "core")
                 last = step(slot, fin, 4096)
                 more, last = scatter_start(after(slot, last), mine_a, got_a, a_segs, 1)
-                last = step(after(slot, last), opn, 4096)
                 left = [one for one in fin if one.done is None]
-                last = step(after(slot, last), left, 1024)
+                last = step(after(slot, last), left)
+                last = step(after(slot, last), opn, 1)
                 chunks = fin[:2] + opn + fin[2:] + more
+                old, new = [], []
                 while any(one.done is None for one in chunks):
-                    for group, weight in ((more, 1), (fin + opn, 4096)):
+                    for group, weight in ((more, 16384), (fin + opn, 1)):
                         left = [one for one in group if one.done is None]
                         if left:
-                            last = step(after(slot, last), left, weight)
+                            last = step(after(slot, last, *old), left, weight)
+                            old, new = new, [one.got for one in left if one.done]
                 done = [x for one in chunks for x in one.done]
         else:
-            g_b = scatter_full(mine_b, other_b, [D] * NC + [FF], 0)
-            g_in, g_proj = g_b[: NC * wr], g_b[NC * wr :]
-            g_a = scatter_full(mine_a, other_a, [D] * 4, SMALL)
+            g_b = scatter_full(mine_b, other_b, [D] * NC + [FF, D], 0)
+            g_in, g_proj, g_out = jnp.split(g_b, [NC * wr, NC * wr + pr])
+            g_a = scatter_full(mine_a, other_a, [D] * 3, SMALL)
+            g_a = jnp.concatenate([g_a[: 3 * wr], g_out, g_a[3 * wr :]], 0)
             shares[mode] = (g_a, g_in, g_proj)
     input_grad = from_chip(dres.astype(BF))
 

time: 623 us -> 619 us (level)
    ppermute x52, waiting for transfers between devices: 175 us -> 167 us  [swap(): lax.ppermute(x, axes, [(device(*at_), turn(*at_)) for at_ in everyone])]
    unnamed x125 -> x121, local copies, waits for them, and re-layouts: 35.9 us -> 35.1 us
  transfers between devices with their start and end apart: 66 -> 66, of which waited for: 28 -> 31; matrix products, arithmetic and copies ran while one was open for 1% -> 1% of each run, Pallas kernels for 31% -> 31%
where the time goes in v2:
time: 619 us; the launch traced here: 614 us
  Pallas kernels  303 us (49%)
  waiting for transfers between devices  187 us (30%)
  starting transfers between devices  70.5 us (11%)
  local copies, waits for them, and re-layouts  38.4 us (6%)
  other arithmetic  10.4 us (2%)
    ppermute x52, waiting for transfers between devices, swap(): lax.ppermute(x, axes, [(device(*at_), turn(*at_)) for at_ in everyone])  167 us
    pallas_call x3, Pallas kernels, run_mlp_back(): call(functools.partial(mlp_back_kernel, kinds, mode), (sds((rows, D), F32...  82.8 us
    ppermute x52, starting transfers between devices, swap(): lax.ppermute(x, axes, [(device(*at_), turn(*at_)) for at_ in everyone])  56.8 us
    pallas_call x3, Pallas kernels, run_attn_back(): call(functools.partial(attn_back_kernel, others), (sds((rows, D), BF), sd...  52.3 us
    pallas_call x3, Pallas kernels, run_mlp(): call(functools.partial(mlp_kernel, kinds), (sds((rows, D), F32), sds((NC,...  39 us
    pallas_call x3, Pallas kernels, run_qkv_back(): call(functools.partial(qkv_back_kernel, kinds, mode, others), (sds((rows,...  37 us
    unnamed x121, local copies, waits for them, and re-layouts  35.1 us
    pallas_call x3, Pallas kernels, run_attn(): call(functools.partial(attn_fwd_kernel, others), (sds((rows, D), BF), sds...  27.4 us
  transfers between devices with their start and end apart: 66, of which 31 were waited for; matrix products, arithmetic and copies ran while one was open for 1% of the time, Pallas kernels for 31%

profile of v2, /device:TPU:0, one launch (start us, length us, event | category | flops | bytes accessed | tf_op | source)
XLA Modules:
  0.0 613.7 jit_solution(2173779828408235202)
XLA Ops:
  14.3 13.3 %collective-permute-done = bf16[192,768]{1,0:T(8,128)(2,1)S(1)} collective-permute-done((bf16[192,768]{1,0:T(8,128)(2,1)S(1)}, bf16[192,768]{1,0:T(8,128)(2,1)S(1)}, u32[]{:S(2)}, u32[]{:S(2)}) %collective-permute-start) | collective-permute-done | bytes 294944 | tf_op jit(solution)/shard_map/ppermute | solution.py:1066
  31.9 16.7 %collective-permute-done.4 = bf16[2,192,768]{2,1,0:T(8,128)(2,1)S(1)} collective-permute-done((bf16[2,192,768]{2,1,0:T(8,128)(2,1)S(1)}, bf16[2,192,768]{2,1,0:T(8,128)(2,1)S(1)}, u32[]{:S(2)}, u32[]{:S(2)}) %collective-permute-start.4) | collective-permute-done | bytes 589856 | tf_op jit(solution)/shard_map/ppermute | solution.py:1066
  66.2 5.8 collective-permute-done.13
  73.5 9.7 %collective-permute-done.5 = bf16[2,192,768]{2,1,0:T(8,128)(2,1)} collective-permute-done((bf16[2,192,768]{2,1,0:T(8,128)(2,1)}, bf16[2,192,768]{2,1,0:T(8,128)(2,1)}, u32[]{:S(2)}, u32[]{:S(2)}) %collective-permute-start.5) | collective-permute-done | bytes 589856 | tf_op jit(solution)/shard_map/ppermute | solution.py:1066
  91.0 15.0 %collective-permute-done.6 = bf16[2,208,768]{2,1,0:T(8,128)(2,1)S(1)} collective-permute-done((bf16[2,208,768]{2,1,0:T(8,128)(2,1)S(1)}, bf16[2,208,768]{2,1,0:T(8,128)(2,1)S(1)}, u32[]{:S(2)}, u32[]{:S(2)}) %collective-permute-start.6) | collective-permute-done | bytes 639008 | tf_op jit(solution)/shard_map/ppermute | solution.py:1066
  106.2 5.7 collective-permute-done.9.other
  114.9 12.7 %collective-permute-done.3 = bf16[208,768]{1,0:T(8,128)(2,1)S(1)} collective-permute-done((bf16[208,768]{1,0:T(8,128)(2,1)S(1)}, bf16[208,768]{1,0:T(8,128)(2,1)S(1)}, u32[]{:S(2)}, u32[]{:S(2)}) %collective-permute-start.3) | collective-permute-done | bytes 319520 | tf_op jit(solution)/shard_map/ppermute | solution.py:1066
  128.4 14.6 %collective-permute-done.7 = bf16[2,208,768]{2,1,0:T(8,128)(2,1)S(1)} collective-permute-done((bf16[2,208,768]{2,1,0:T(8,128)(2,1)S(1)}, bf16[2,208,768]{2,1,0:T(8,128)(2,1)S(1)}, u32[]{:S(2)}, u32[]{:S(2)}) %collective-permute-start.7) | collective-permute-done | bytes 639008 | tf_op jit(solution)/shard_map/ppermute | solution.py:1066
  150.9 7.6 %collective-permute-done.16.rest_3_ = bf16[8,192,768]{2,1,0:T(8,128)(2,1)} collective-permute-done((bf16[8,192,768]{2,1,0:T(8,128)(2,1)S(1)}, bf16[8,192,768]{2,1,0:T(8,128)(2,1)}, u32[]{:S(2)}, u32[]{:S(2)}) %collective-permute-start.16) | collective-permute-done | bytes 2359328 | tf_op jit(solution)/shard_map/ppermute | solution.py:1066
  175.7 9.1 %attn.3 = (bf16[512,768]{1,0:T(8,128)(2,1)S(1)}, f32[2,16,256]{2,1,0:T(8,128)S(1)}) custom-call(s32[8]{0:T(128)S(1)} %stack.165.meta, bf16[512,768]{1,0:T(8,128)(2,1)S(1)} %copy-done.11, bf16[2,512,768]{2,1,0:T(8,128)(2,1)S(1)} %get-tuple-element.186.ko.vo, bf16[2,512,768]{2,1,0:T(8,128)(2,1)S(1)} %get-tuple-element.186.ko.vo, ...), custom_call_target="tpu_custom_call" | custom-call | flops 40265320 | bytes 1024 | tf_op jit(solution)/shard_map/attn/pallas_call | solution.py:765
  184.8 13.1 %mlp.3 = (f32[512,768]{1,0:T(8,128)S(1)}, bf16[4,512,768]{2,1,0:T(8,128)(2,1)}, f32[512,768]{1,0:T(8,128)S(1)}) custom-call(s32[8]{0:T(128)S(1)} %stack.165.meta, f32[512,768]{1,0:T(8,128)} %copy-done, bf16[512,768]{1,0:T(8,128)(2,1)S(1)} %get-tuple-element.187.mixed, bf16[8,208,768]{2,1,0:T(8,128)(2,1)} %assemble.4.rest_0_, ...), custom_call_target="tpu_custom_call" | custom-call | flops 54358180 | bytes 1024 | tf_op jit(solution)/shard_map/mlp/pallas_call | solution.py:796
  198.0 6.4 %collective-permute-done.21.rest_10_ = bf16[8,192,768]{2,1,0:T(8,128)(2,1)} collective-permute-done((bf16[8,192,768]{2,1,0:T(8,128)(2,1)}, bf16[8,192,768]{2,1,0:T(8,128)(2,1)}, u32[]{:S(2)}, u32[]{:S(2)}) %collective-permute-start.21) | collective-permute-done | bytes 2359328 | tf_op jit(solution)/shard_map/ppermute | solution.py:1066
  222.8 9.3 %attn.4 = (bf16[512,768]{1,0:T(8,128)(2,1)S(1)}, f32[2,16,256]{2,1,0:T(8,128)S(1)}) custom-call(s32[8]{0:T(128)S(1)} %stack.164.meta, bf16[512,768]{1,0:T(8,128)(2,1)S(1)} %get-tuple-element.194.q_ref, bf16[2,512,768]{2,1,0:T(8,128)(2,1)S(1)} %get-tuple-element.195.ko.vo, bf16[2,512,768]{2,1,0:T(8,128)(2,1)S(1)} %get-tuple-element.195.ko.vo, ...), custom_call_target="tpu_custom_call" | custom-call | flops 32212254720 | bytes 1024 | tf_op jit(solution)/shard_map/attn/pallas_call | solution.py:765
  233.6 12.9 %mlp.4 = (f32[512,768]{1,0:T(8,128)S(1)}, bf16[4,512,768]{2,1,0:T(8,128)(2,1)}, f32[512,768]{1,0:T(8,128)S(1)}) custom-call(s32[8]{0:T(128)S(1)} %stack.164.meta, f32[512,768]{1,0:T(8,128)} %copy-done.20, bf16[512,768]{1,0:T(8,128)(2,1)S(1)} %get-tuple-element.196.mixed, bf16[8,208,768]{2,1,0:T(8,128)(2,1)} %assemble.4.rest_0_, ...), custom_call_target="tpu_custom_call" | custom-call | flops 43486543872 | bytes 1024 | tf_op jit(solution)/shard_map/mlp/pallas_call | solution.py:796
  246.6 5.1 qkv.7
  256.3 9.1 %attn.5 = (bf16[512,768]{1,0:T(8,128)(2,1)S(1)}, f32[2,16,256]{2,1,0:T(8,128)S(1)}) custom-call(s32[8]{0:T(128)S(1)} %stack.163.meta, bf16[512,768]{1,0:T(8,128)(2,1)S(1)} %get-tuple-element.198.q_ref, bf16[2,512,768]{2,1,0:T(8,128)(2,1)S(1)} %get-tuple-element.199.ko.vo, bf16[2,512,768]{2,1,0:T(8,128)(2,1)S(1)} %get-tuple-element.199.ko.vo, ...), custom_call_target="tpu_custom_call" | custom-call | flops 32212254720 | bytes 1024 | tf_op jit(solution)/shard_map/attn/pallas_call | solution.py:765
  265.4 12.9 %mlp.5 = (f32[512,768]{1,0:T(8,128)S(1)}, bf16[4,512,768]{2,1,0:T(8,128)(2,1)}, f32[512,768]{1,0:T(8,128)S(1)}) custom-call(s32[8]{0:T(128)S(1)} %stack.163.meta, f32[512,768]{1,0:T(8,128)} %copy-done.25, bf16[512,768]{1,0:T(8,128)(2,1)S(1)} %get-tuple-element.200.mixed, bf16[8,208,768]{2,1,0:T(8,128)(2,1)} %assemble.4.rest_0_, ...), custom_call_target="tpu_custom_call" | custom-call | flops 43486543872 | bytes 1024 | tf_op jit(solution)/shard_map/mlp/pallas_call | solution.py:796
  283.6 25.2 %mlp_back.3 = (f32[512,768]{1,0:T(8,128)}, bf16[512,768]{1,0:T(8,128)(2,1)S(1)}, f32[2,16,256]{2,1,0:T(8,128)S(1)}, f32[16,768]{1,0:T(8,128)S(1)}, bf16[8,2,384,...) custom-call(s32[8]{0:T(128)S(1)} %stack.163.meta, f32[2]{0:T(128)S(1)} %add_convert_fusion.keep_ref, ...), custom_call_target="tpu_custom_call" | custom-call | flops 86973087744 | bytes 1024 | tf_op jit(solution)/shard_map/mlp_back/pallas_call | solution.py:823
  309.8 17.6 %attn_back.3 = (bf16[512,768]{1,0:T(8,128)(2,1)S(1)}, bf16[2,512,768]{2,1,0:T(8,128)(2,1)S(1)}, bf16[1,2,512,768]{3,2,1,0:T(8,128)(2,1)}) custom-call(s32[8]{0:T(128)S(1)} %stack.163.meta, bf16[512,768]{1,0:T(8,128)(2,1)S(1)} %get-tuple-element.198.q_ref, bf16[2,512,768]{2,1,0:T(8,128)(2,1)} %copy-done.23, bf16[2,512,768]{2,1,0:T(8,128)(2,1)} %copy-done.23, ...), custom_call_target="tpu_custom_call" | custom-call | flops 80530636800 | bytes 1024 | tf_op jit(solution)/shard_map/attn_back/pallas_call | solution.py:848
  333.3 11.0 %qkv_back.3 = (f32[512,768]{1,0:T(8,128)S(1)}, bf16[8,2,160,768]{3,2,1,0:T(8,128)(2,1)}) custom-call(s32[8]{0:T(128)S(1)} %stack.163.meta, f32[2]{0:T(128)S(1)} %add_convert_fusion.keep_ref, f32[512,768]{1,0:T(8,128)S(1)} %copy-done.26, bf16[512,768]{1,0:T(8,128)(2,1)S(1)} %get-tuple-element.208.dq, bf16[2,512,768]{2,1,0:T(8,128)(2,1)} %copy-done.30, ...), custom_call_target="tpu_custom_call" | custom-call | flops 28991029248 | bytes 1024 | tf_op jit(solution)/shard_map/qkv_back/pallas_call | solution.py:875
  345.5 30.1 %mlp_back.4 = (f32[512,768]{1,0:T(8,128)}, bf16[512,768]{1,0:T(8,128)(2,1)S(1)}, f32[2,16,256]{2,1,0:T(8,128)S(1)}, f32[16,768]{1,0:T(8,128)S(1)}, bf16[8,432,76...) custom-call(s32[8]{0:T(128)S(1)} %stack.164.meta, ...), custom_call_target="tpu_custom_call" | custom-call | flops 86973087744 | bytes 1024 | tf_op jit(solution)/shard_map/mlp_back/pallas_call | solution.py:823
  375.8 17.3 %attn_back.4 = (bf16[512,768]{1,0:T(8,128)(2,1)S(1)}, bf16[2,512,768]{2,1,0:T(8,128)(2,1)S(1)}, bf16[1,2,512,768]{3,2,1,0:T(8,128)(2,1)}) custom-call(s32[8]{0:T(128)S(1)} %stack.164.meta, bf16[512,768]{1,0:T(8,128)(2,1)S(1)} %get-tuple-element.194.q_ref, bf16[2,512,768]{2,1,0:T(8,128)(2,1)} %copy-done.22, bf16[2,512,768]{2,1,0:T(8,128)(2,1)} %copy-done.22, ...), custom_call_target="tpu_custom_call" | custom-call | flops 80530636800 | bytes 1024 | tf_op jit(solution)/shard_map/attn_back/pallas_call | solution.py:848
  394.7 6.3 %add_cores.4 = (bf16[8,96,768]{2,1,0:T(8,128)(2,1)S(1)}, bf16[8,96,768]{2,1,0:T(8,128)(2,1)S(1)}, bf16[4,240,768]{2,1,0:T(8,128)(2,1)S(1)}, bf16[4,240,768]{2,1,0:T(8,128)(2,1)}) custom-call(s32[8]{0:T(128)S(1)} %stack.164.meta, bf16[8,432,768]{2,1,0:T(8,128)(2,1)} %get-tuple-element.223.mine, bf16[8,432,768]{2,1,0:T(8,128)(2,1)} %collective-permute-done.30.got), custom_call_target="tpu_custom_call" | custom-call | flops 86973087744 | bytes 1024 | tf_op jit(solution)/shard_map/add_cores/pallas_call | solution.py:920
  405.1 13.9 %qkv_back.4 = (f32[512,768]{1,0:T(8,128)S(1)}, bf16[8,160,768]{2,1,0:T(8,128)(2,1)}, bf16[8,160,768]{2,1,0:T(8,128)(2,1)}, bf16[8,2,160,768]{3,2,1,0:T(8,128)(2,1)}) custom-call(s32[8]{0:T(128)S(1)} %stack.164.meta, f32[2]{0:T(128)S(1)} %add_convert_fusion.keep_ref, f32[512,768]{1,0:T(8,128)S(1)} %copy-done.21, bf16[512,768]{1,0:T(8,128)(2,1)S(1)} %get-tuple-element.221.dq, ...), custom_call_target="tpu_custom_call" | custom-call | flops 28991029248 | bytes 1024 | tf_op jit(solution)/shard_map/qkv_back/pallas_call | solution.py:875
  420.2 27.4 %mlp_back.5 = (f32[512,768]{1,0:T(8,128)}, bf16[512,768]{1,0:T(8,128)(2,1)S(1)}, f32[2,16,256]{2,1,0:T(8,128)S(1)}, f32[16,768]{1,0:T(8,128)S(1)}, bf16[8,432,76...) custom-call(s32[8]{0:T(128)S(1)} %stack.165.meta, f32[2]{0:T(128)S(1)} %add_convert_fusion.keep_ref, f32[512,768]{1,0:T(8,128)} %copy-done.28, ...), custom_call_target="tpu_custom_call" | custom-call | flops 86973087744 | bytes 1024 | tf_op jit(solution)/shard_map/mlp_back/pallas_call | solution.py:823
  462.6 6.1 add_cores.6
  469.9 17.4 %attn_back.5 = (bf16[512,768]{1,0:T(8,128)(2,1)S(1)}, bf16[2,512,768]{2,1,0:T(8,128)(2,1)S(1)}, bf16[1,2,512,768]{3,2,1,0:T(8,128)(2,1)}) custom-call(s32[8]{0:T(128)S(1)} %stack.165.meta, bf16[512,768]{1,0:T(8,128)(2,1)S(1)} %copy-done.12, bf16[2,512,768]{2,1,0:T(8,128)(2,1)} %copy-done.2, bf16[2,512,768]{2,1,0:T(8,128)(2,1)} %copy-done.2, ...), custom_call_target="tpu_custom_call" | custom-call | flops 80530636800 | bytes 1024 | tf_op jit(solution)/shard_map/attn_back/pallas_call | solution.py:848
  497.6 12.1 %qkv_back.5 = (f32[512,768]{1,0:T(8,128)S(1)}, bf16[8,160,768]{2,1,0:T(8,128)(2,1)}, bf16[8,160,768]{2,1,0:T(8,128)(2,1)}) custom-call(s32[8]{0:T(128)S(1)} %stack.165.meta, f32[2]{0:T(128)S(1)} %add_convert_fusion.keep_ref, f32[512,768]{1,0:T(8,128)S(1)} %copy-done.1, bf16[512,768]{1,0:T(8,128)(2,1)S(1)} %get-tuple-element.253.dq, ...), custom_call_target="tpu_custom_call" | custom-call | flops 28991029248 | bytes 1024 | tf_op jit(solution)/shard_map/qkv_back/pallas_call | solution.py:875
  521.6 9.4 %collective-permute-done.46.refs_1_ = bf16[1,96,768]{2,1,0:T(8,128)(2,1)S(1)} collective-permute-done((bf16[1,96,768]{2,1,0:T(8,128)(2,1)S(1)}, bf16[1,96,768]{2,1,0:T(8,128)(2,1)S(1)}, u32[]{:S(2)}, u32[]{:S(2)}) %collective-permute-start.46) | collective-permute-done | bytes 147488 | tf_op jit(solution)/shard_map/ppermute | solution.py:1066
  531.7 6.9 %collective-permute-done.51.refs_3_ = bf16[4,240,768]{2,1,0:T(8,128)(2,1)S(1)} collective-permute-done((bf16[4,240,768]{2,1,0:T(8,128)(2,1)}, bf16[4,240,768]{2,1,0:T(8,128)(2,1)S(1)}, u32[]{:S(2)}, u32[]{:S(2)}) %collective-permute-start.51) | collective-permute-done | bytes 1474592 | tf_op jit(solution)/shard_map/ppermute | solution.py:1066
  547.5 15.2 %collective-permute-done.53.refs_1_ = bf16[1,80,768]{2,1,0:T(8,128)(2,1)S(1)} collective-permute-done((bf16[1,80,768]{2,1,0:T(8,128)(2,1)S(1)}, bf16[1,80,768]{2,1,0:T(8,128)(2,1)S(1)}, u32[]{:S(2)}, u32[]{:S(2)}) %collective-permute-start.53) | collective-permute-done | bytes 122912 | tf_op jit(solution)/shard_map/ppermute | solution.py:1066
  576.6 6.2 %collective-permute-done.58.refs_1_ = bf16[2,96,768]{2,1,0:T(8,128)(2,1)S(1)} collective-permute-done((bf16[2,96,768]{2,1,0:T(8,128)(2,1)S(1)}, bf16[2,96,768]{2,1,0:T(8,128)(2,1)S(1)}, u32[]{:S(2)}, u32[]{:S(2)}) %collective-permute-start.58) | collective-permute-done | bytes 294944 | tf_op jit(solution)/shard_map/ppermute | solution.py:1066
  (288 shorter events, 208.0 us)
Async XLA Ops:
  10.2 17.4 %collective-permute-start = (bf16[192,768]{1,0:T(8,128)(2,1)S(1)}, bf16[192,768]{1,0:T(8,128)(2,1)S(1)}, u32[]{:S(2)}, u32[]{:S(2)}) collective-permute-start(bf16[192,768]{1,0:T(8,128)(2,1)S(1)} %get-tuple-element.170), channel_id=1, source_target_pairs={{0,16},{1,17},{2,18},{3,19},{4,20},{5,21},{6,22},{7,23},{8,24},{9,... | collective-permute-start | bytes 884744 | tf_op jit(solution)/shard_map/ppermute | solution.py:1066
  27.7 20.9 %collective-permute-start.4 = (bf16[2,192,768]{2,1,0:T(8,128)(2,1)S(1)}, bf16[2,192,768]{2,1,0:T(8,128)(2,1)S(1)}, u32[]{:S(2)}, u32[]{:S(2)}) collective-permute-start(bf16[2,192,768]{2,1,0:T(8,128)(2,1)S(1)} %get-tuple-element.337), channel_id=1, source_target_pairs={{0,8},{1,9},{2,10},{3,11},{4,12},{5,13},{6,14},{7,15},{8,0},{9,1},... | collective-permute-start | bytes 1769480 | tf_op jit(solution)/shard_map/ppermute | solution.py:1066
  28.5 30.6 %collective-permute-start.1 = (bf16[192,768]{1,0:T(8,128)(2,1)S(1)}, bf16[192,768]{1,0:T(8,128)(2,1)S(1)}, u32[]{:S(2)}, u32[]{:S(2)}) collective-permute-start(bf16[192,768]{1,0:T(8,128)(2,1)S(1)} %get-tuple-element.171), channel_id=1, source_target_pairs={{0,16},{1,17},{2,18},{3,19},{4,20},{5,21},{6,22},{7,23},{8,24},{9,... | collective-permute-start | bytes 884744 | tf_op jit(solution)/shard_map/ppermute | solution.py:1066
  48.8 35.8 %collective-permute-start.8 = (bf16[2,2,192,768]{3,2,1,0:T(8,128)(2,1)S(1)}, bf16[2,2,192,768]{3,2,1,0:T(8,128)(2,1)S(1)}, u32[]{:S(2)}, u32[]{:S(2)}) collective-permute-start(bf16[2,2,192,768]{3,2,1,0:T(8,128)(2,1)S(1)} %pad_maximum_fusion.2.mine), channel_id=1, source_target_pairs={{0,4},{1,5},{2,6},{3,7},{4,0},{5,1},{6,2},{7,3},{8,12},{9,13},{10,... | collective-permute-start | bytes 3538952 | tf_op jit(solution)/shard_map/ppermute | solution.py:1066
  60.7 22.5 %collective-permute-start.5 = (bf16[2,192,768]{2,1,0:T(8,128)(2,1)}, bf16[2,192,768]{2,1,0:T(8,128)(2,1)}, u32[]{:S(2)}, u32[]{:S(2)}) collective-permute-start(bf16[2,192,768]{2,1,0:T(8,128)(2,1)} %pad_maximum_fusion.7), channel_id=1, source_target_pairs={{0,8},{1,9},{2,10},{3,11},{4,12},{5,13},{6,14},{7,15},{8,0},{9,1},... | collective-permute-start | bytes 1769480 | tf_op jit(solution)/shard_map/ppermute | solution.py:1066
  63.6 27.3 %collective-permute-start.2 = (bf16[208,768]{1,0:T(8,128)(2,1)S(1)}, bf16[208,768]{1,0:T(8,128)(2,1)S(1)}, u32[]{:S(2)}, u32[]{:S(2)}) collective-permute-start(bf16[208,768]{1,0:T(8,128)(2,1)S(1)} %get-tuple-element.172), channel_id=1, source_target_pairs={{0,16},{1,17},{2,18},{3,19},{4,20},{5,21},{6,22},{7,23},{8,24},{9,... | collective-permute-start | bytes 958472 | tf_op jit(solution)/shard_map/ppermute | solution.py:1066
  84.6 27.2 %collective-permute-start.9 = (bf16[2,2,192,768]{3,2,1,0:T(8,128)(2,1)S(1)}, bf16[2,2,192,768]{3,2,1,0:T(8,128)(2,1)S(1)}, u32[]{:S(2)}, u32[]{:S(2)}) collective-permute-start(bf16[2,2,192,768]{3,2,1,0:T(8,128)(2,1)S(1)} %pad_maximum_fusion.3.mine), channel_id=1, source_target_pairs={{0,4},{1,5},{2,6},{3,7},{4,0},{5,1},{6,2},{7,3},{8,12},{9,13},{10,... | collective-permute-start | bytes 3538952 | tf_op jit(solution)/shard_map/ppermute | solution.py:1066
  90.5 59.9 %collective-permute-start.17 = (bf16[8,192,768]{2,1,0:T(8,128)(2,1)}, bf16[8,192,768]{2,1,0:T(8,128)(2,1)S(1)}, u32[]{:S(2)}, u32[]{:S(2)}) collective-permute-start(bf16[8,192,768]{2,1,0:T(8,128)(2,1)} %assemble.5.rest_2_), channel_id=1, source_target_pairs={{0,1},{1,0},{2,3},{3,2},{4,5},{5,4},{6,7},{7,6},{8,9},{9,8},{10,11... | collective-permute-start | bytes 7077896 | tf_op jit(solution)/shard_map/ppermute | solution.py:1066
  111.8 32.3 %collective-permute-start.10 = (bf16[2,2,208,768]{3,2,1,0:T(8,128)(2,1)S(1)}, bf16[2,2,208,768]{3,2,1,0:T(8,128)(2,1)S(1)}, u32[]{:S(2)}, u32[]{:S(2)}) collective-permute-start(bf16[2,2,208,768]{3,2,1,0:T(8,128)(2,1)S(1)} %pad_maximum_fusion.mine), channel_id=1, source_target_pairs={{0,4},{1,5},{2,6},{3,7},{4,0},{5,1},{6,2},{7,3},{8,12},{9,13},{10,... | collective-permute-start | bytes 3833864 | tf_op jit(solution)/shard_map/ppermute | solution.py:1066
  147.1 16.6 %collective-permute-start.11 = (bf16[8,208,768]{2,1,0:T(8,128)(2,1)}, bf16[8,208,768]{2,1,0:T(8,128)(2,1)S(1)}, u32[]{:S(2)}, u32[]{:S(2)}) collective-permute-start(bf16[8,208,768]{2,1,0:T(8,128)(2,1)} %assemble.4.rest_0_), channel_id=1, source_target_pairs={{0,2},{1,3},{2,0},{3,1},{4,6},{5,7},{6,4},{7,5},{8,10},{9,11},{10,... | collective-permute-start | bytes 7667720 | tf_op jit(solution)/shard_map/ppermute | solution.py:1066
  150.9 53.6 %collective-permute-start.21 = (bf16[8,192,768]{2,1,0:T(8,128)(2,1)}, bf16[8,192,768]{2,1,0:T(8,128)(2,1)}, u32[]{:S(2)}, u32[]{:S(2)}) collective-permute-start(bf16[8,192,768]{2,1,0:T(8,128)(2,1)} %assemble.6.rest_8_), channel_id=1, source_target_pairs={{0,1},{1,0},{2,3},{3,2},{4,5},{5,4},{6,7},{7,6},{8,9},{9,8},{10,11... | collective-permute-start | bytes 7077896 | tf_op jit(solution)/shard_map/ppermute | solution.py:1066
  171.2 33.2 %collective-permute-start.22 = (bf16[2,2,208,768]{3,2,1,0:T(8,128)(2,1)}, bf16[2,2,208,768]{3,2,1,0:T(8,128)(2,1)S(1)}, u32[]{:S(2)}, u32[]{:S(2)}) collective-permute-start(bf16[2,2,208,768]{3,2,1,0:T(8,128)(2,1)} %pad_maximum_fusion.1.mine), channel_id=1, source_target_pairs={{0,4},{1,5},{2,6},{3,7},{4,0},{5,1},{6,2},{7,3},{8,12},{9,13},{10,... | collective-permute-start | bytes 3833864 | tf_op jit(solution)/shard_map/ppermute | solution.py:1066
  279.5 29.4 %collective-permute-start.27 = (bf16[256,768]{1,0:T(8,128)(2,1)S(1)}, bf16[256,768]{1,0:T(8,128)(2,1)S(1)}, u32[]{:S(2)}, u32[]{:S(2)}) collective-permute-start(bf16[256,768]{1,0:T(8,128)(2,1)S(1)} %get-tuple-element.326), channel_id=1, source_target_pairs={{0,0},{2,1},{1,2},{3,3},{4,4},{6,5},{5,6},{7,7},{8,8},{10,9},{9,10... | collective-permute-start | bytes 1179656 | tf_op jit(solution)/shard_map/ppermute | solution.py:1031
  280.6 28.3 %collective-permute-start.28 = (bf16[256,768]{1,0:T(8,128)(2,1)S(1)}, bf16[256,768]{1,0:T(8,128)(2,1)S(1)}, u32[]{:S(2)}, u32[]{:S(2)}) collective-permute-start(bf16[256,768]{1,0:T(8,128)(2,1)S(1)} %get-tuple-element.327), channel_id=1, source_target_pairs={{2,0},{0,1},{3,2},{1,3},{6,4},{4,5},{7,6},{5,7},{10,8},{8,9},{11,1... | collective-permute-start | bytes 1179656 | tf_op jit(solution)/shard_map/ppermute | solution.py:1032
  375.6 19.1 %collective-permute-start.30 = (bf16[8,432,768]{2,1,0:T(8,128)(2,1)}, bf16[8,432,768]{2,1,0:T(8,128)(2,1)}, u32[]{:S(2)}, u32[]{:S(2)}) collective-permute-start(bf16[8,432,768]{2,1,0:T(8,128)(2,1)} %get-tuple-element.224), channel_id=1, source_target_pairs={{0,2},{1,3},{2,0},{3,1},{4,6},{5,7},{6,4},{7,5},{8,10},{9,11},{10,... | collective-permute-start | bytes 15925256 | tf_op jit(solution)/shard_map/ppermute | solution.py:1066
  402.3 50.9 %collective-permute-start.33 = (bf16[8,96,768]{2,1,0:T(8,128)(2,1)S(1)}, bf16[8,96,768]{2,1,0:T(8,128)(2,1)S(1)}, u32[]{:S(2)}, u32[]{:S(2)}) collective-permute-start(bf16[8,96,768]{2,1,0:T(8,128)(2,1)S(1)} %get-tuple-element.242), channel_id=1, source_target_pairs={{0,1},{1,0},{2,3},{3,2},{4,5},{5,4},{6,7},{7,6},{8,9},{9,8},{10,11... | collective-permute-start | bytes 3538952 | tf_op jit(solution)/shard_map/ppermute | solution.py:1066
  402.4 50.8 %collective-permute-start.34 = (bf16[4,240,768]{2,1,0:T(8,128)(2,1)}, bf16[4,240,768]{2,1,0:T(8,128)(2,1)S(1)}, u32[]{:S(2)}, u32[]{:S(2)}) collective-permute-start(bf16[4,240,768]{2,1,0:T(8,128)(2,1)} %get-tuple-element.244), channel_id=1, source_target_pairs={{0,4},{1,5},{2,6},{3,7},{4,0},{5,1},{6,2},{7,3},{8,12},{9,13},{10,... | collective-permute-start | bytes 4423688 | tf_op jit(solution)/shard_map/ppermute | solution.py:1066
  420.2 28.0 %collective-permute-start.32 = (bf16[8,160,768]{2,1,0:T(8,128)(2,1)}, bf16[8,160,768]{2,1,0:T(8,128)(2,1)S(1)}, u32[]{:S(2)}, u32[]{:S(2)}) collective-permute-start(bf16[8,160,768]{2,1,0:T(8,128)(2,1)} %get-tuple-element.239), channel_id=1, source_target_pairs={{0,2},{1,3},{2,0},{3,1},{4,6},{5,7},{6,4},{7,5},{8,10},{9,11},{10,... | collective-permute-start | bytes 5898248 | tf_op jit(solution)/shard_map/ppermute | solution.py:1066
  458.4 28.9 %collective-permute-start.36 = (bf16[4,96,768]{2,1,0:T(8,128)(2,1)S(1)}, bf16[4,96,768]{2,1,0:T(8,128)(2,1)S(1)}, u32[]{:S(2)}, u32[]{:S(2)}) collective-permute-start(bf16[4,96,768]{2,1,0:T(8,128)(2,1)S(1)} %get-tuple-element.255), channel_id=1, source_target_pairs={{0,4},{1,5},{2,6},{3,7},{4,0},{5,1},{6,2},{7,3},{8,12},{9,13},{10,... | collective-permute-start | bytes 1769480 | tf_op jit(solution)/shard_map/ppermute | solution.py:1066
  458.9 28.4 %collective-permute-start.37 = (bf16[2,240,768]{2,1,0:T(8,128)(2,1)S(1)}, bf16[2,240,768]{2,1,0:T(8,128)(2,1)}, u32[]{:S(2)}, u32[]{:S(2)}) collective-permute-start(bf16[2,240,768]{2,1,0:T(8,128)(2,1)S(1)} %get-tuple-element.257), channel_id=1, source_target_pairs={{0,8},{1,9},{2,10},{3,11},{4,12},{5,13},{6,14},{7,15},{8,0},{9,1},... | collective-permute-start | bytes 2211848 | tf_op jit(solution)/shard_map/ppermute | solution.py:1066
  460.6 26.7 %collective-permute-start.38 = (bf16[8,80,768]{2,1,0:T(8,128)(2,1)S(1)}, bf16[8,80,768]{2,1,0:T(8,128)(2,1)}, u32[]{:S(2)}, u32[]{:S(2)}) collective-permute-start(bf16[8,80,768]{2,1,0:T(8,128)(2,1)S(1)} %get-tuple-element.258), channel_id=1, source_target_pairs={{0,1},{1,0},{2,3},{3,2},{4,5},{5,4},{6,7},{7,6},{8,9},{9,8},{10,11... | collective-permute-start | bytes 2949128 | tf_op jit(solution)/shard_map/ppermute | solution.py:1066
  490.6 19.0 %collective-permute-start.42 = (bf16[2,96,768]{2,1,0:T(8,128)(2,1)S(1)}, bf16[2,96,768]{2,1,0:T(8,128)(2,1)S(1)}, u32[]{:S(2)}, u32[]{:S(2)}) collective-permute-start(bf16[2,96,768]{2,1,0:T(8,128)(2,1)S(1)} %get-tuple-element.268), channel_id=1, source_target_pairs={{0,8},{1,9},{2,10},{3,11},{4,12},{5,13},{6,14},{7,15},{8,0},{9,1},... | collective-permute-start | bytes 884744 | tf_op jit(solution)/shard_map/ppermute | solution.py:1066
  491.0 19.9 %collective-permute-start.43 = (bf16[1,240,768]{2,1,0:T(8,128)(2,1)S(1)}, bf16[1,240,768]{2,1,0:T(8,128)(2,1)S(1)}, u32[]{:S(2)}, u32[]{:S(2)}) collective-permute-start(bf16[1,240,768]{2,1,0:T(8,128)(2,1)S(1)} %get-tuple-element.270), channel_id=1, source_target_pairs={{0,16},{1,17},{2,18},{3,19},{4,20},{5,21},{6,22},{7,23},{8,24},{9,... | collective-permute-start | bytes 1105928 | tf_op jit(solution)/shard_map/ppermute | solution.py:1066
  495.9 35.8 %collective-permute-start.50 = (bf16[8,96,768]{2,1,0:T(8,128)(2,1)S(1)}, bf16[8,96,768]{2,1,0:T(8,128)(2,1)}, u32[]{:S(2)}, u32[]{:S(2)}) collective-permute-start(bf16[8,96,768]{2,1,0:T(8,128)(2,1)S(1)} %get-tuple-element.285), channel_id=1, source_target_pairs={{0,1},{1,0},{2,3},{3,2},{4,5},{5,4},{6,7},{7,6},{8,9},{9,8},{10,11... | collective-permute-start | bytes 3538952 | tf_op jit(solution)/shard_map/ppermute | solution.py:1066
  497.1 41.6 %collective-permute-start.51 = (bf16[4,240,768]{2,1,0:T(8,128)(2,1)}, bf16[4,240,768]{2,1,0:T(8,128)(2,1)S(1)}, u32[]{:S(2)}, u32[]{:S(2)}) collective-permute-start(bf16[4,240,768]{2,1,0:T(8,128)(2,1)} %get-tuple-element.287), channel_id=1, source_target_pairs={{0,4},{1,5},{2,6},{3,7},{4,0},{5,1},{6,2},{7,3},{8,12},{9,13},{10,... | collective-permute-start | bytes 4423688 | tf_op jit(solution)/shard_map/ppermute | solution.py:1066
  517.8 28.1 %collective-permute-start.52 = (bf16[8,80,768]{2,1,0:T(8,128)(2,1)S(1)}, bf16[8,80,768]{2,1,0:T(8,128)(2,1)S(1)}, u32[]{:S(2)}, u32[]{:S(2)}) collective-permute-start(bf16[8,80,768]{2,1,0:T(8,128)(2,1)S(1)} %get-tuple-element.290), channel_id=1, source_target_pairs={{0,1},{1,0},{2,3},{3,2},{4,5},{5,4},{6,7},{7,6},{8,9},{9,8},{10,11... | collective-permute-start | bytes 2949128 | tf_op jit(solution)/shard_map/ppermute | solution.py:1066
  542.6 20.1 %collective-permute-start.54 = (bf16[4,96,768]{2,1,0:T(8,128)(2,1)S(1)}, bf16[4,96,768]{2,1,0:T(8,128)(2,1)S(1)}, u32[]{:S(2)}, u32[]{:S(2)}) collective-permute-start(bf16[4,96,768]{2,1,0:T(8,128)(2,1)S(1)} %get-tuple-element.295), channel_id=1, source_target_pairs={{0,4},{1,5},{2,6},{3,7},{4,0},{5,1},{6,2},{7,3},{8,12},{9,13},{10,... | collective-permute-start | bytes 1769480 | tf_op jit(solution)/shard_map/ppermute | solution.py:1066
  544.2 19.4 %collective-permute-start.55 = (bf16[2,240,768]{2,1,0:T(8,128)(2,1)S(1)}, bf16[2,240,768]{2,1,0:T(8,128)(2,1)S(1)}, u32[]{:S(2)}, u32[]{:S(2)}) collective-permute-start(bf16[2,240,768]{2,1,0:T(8,128)(2,1)S(1)} %get-tuple-element.297), channel_id=1, source_target_pairs={{0,8},{1,9},{2,10},{3,11},{4,12},{5,13},{6,14},{7,15},{8,0},{9,1},... | collective-permute-start | bytes 2211848 | tf_op jit(solution)/shard_map/ppermute | solution.py:1066
  546.7 21.8 %collective-permute-start.56 = (bf16[4,80,768]{2,1,0:T(8,128)(2,1)S(1)}, bf16[4,80,768]{2,1,0:T(8,128)(2,1)S(1)}, u32[]{:S(2)}, u32[]{:S(2)}) collective-permute-start(bf16[4,80,768]{2,1,0:T(8,128)(2,1)S(1)} %get-tuple-element.300), channel_id=1, source_target_pairs={{0,4},{1,5},{2,6},{3,7},{4,0},{5,1},{6,2},{7,3},{8,12},{9,13},{10,... | collective-permute-start | bytes 1474568 | tf_op jit(solution)/shard_map/ppermute | solution.py:1066
  565.9 16.9 %collective-permute-start.58 = (bf16[2,96,768]{2,1,0:T(8,128)(2,1)S(1)}, bf16[2,96,768]{2,1,0:T(8,128)(2,1)S(1)}, u32[]{:S(2)}, u32[]{:S(2)}) collective-permute-start(bf16[2,96,768]{2,1,0:T(8,128)(2,1)S(1)} %get-tuple-element.304), channel_id=1, source_target_pairs={{0,8},{1,9},{2,10},{3,11},{4,12},{5,13},{6,14},{7,15},{8,0},{9,1},... | collective-permute-start | bytes 884744 | tf_op jit(solution)/shard_map/ppermute | solution.py:1066
  569.2 17.9 %collective-permute-start.60 = (bf16[2,80,768]{2,1,0:T(8,128)(2,1)S(1)}, bf16[2,80,768]{2,1,0:T(8,128)(2,1)S(1)}, u32[]{:S(2)}, u32[]{:S(2)}) collective-permute-start(bf16[2,80,768]{2,1,0:T(8,128)(2,1)S(1)} %get-tuple-element.309), channel_id=1, source_target_pairs={{0,8},{1,9},{2,10},{3,11},{4,12},{5,13},{6,14},{7,15},{8,0},{9,1},... | collective-permute-start | bytes 737288 | tf_op jit(solution)/shard_map/ppermute | solution.py:1066
  571.3 33.0 %collective-permute-start.49 = (bf16[240,768]{1,0:T(8,128)(2,1)S(1)}, bf16[240,768]{1,0:T(8,128)(2,1)S(1)}, u32[]{:S(2)}, u32[]{:S(2)}) collective-permute-start(bf16[240,768]{1,0:T(8,128)(2,1)S(1)} %get-tuple-element.283.refs_2_), channel_id=1, source_target_pairs={{0,1},{1,0},{2,3},{3,2},{4,5},{5,4},{6,7},{7,6},{8,9},{9,8},{10,11... | collective-permute-start | bytes 1105928 | tf_op jit(solution)/shard_map/ppermute | solution.py:1066
  (94 other events, 786.9 us)

commit v3 on v2

--- a/solution.py
+++ b/solution.py
@@ -1272,13 +1272,13 @@
                 last = step(after(slot, last), left)
                 last = step(after(slot, last), opn, 1)
                 chunks = fin[:2] + opn + fin[2:] + more
-                old, new = [], []
+                old = []
                 while any(one.done is None for one in chunks):
                     for group, weight in ((more, 16384), (fin + opn, 1)):
                         left = [one for one in group if one.done is None]
                         if left:
                             last = step(after(slot, last, *old), left, weight)
-                            old, new = new, [one.got for one in left if one.done]
+                            old = [one.got for one in left if one.done]
                 done = [x for one in chunks for x in one.done]
         else:
             g_b = scatter_full(mine_b, other_b, [D] * NC + [FF, D], 0)

time: 619 us -> 624 us (level)
  waiting for transfers between devices: 187 us -> 195 us
  transfers between devices with their start and end apart: 66 -> 66, of which waited for: 31 -> 33; matrix products, arithmetic and copies ran while one was open for 1% -> 1% of each run, Pallas kernels for 31% -> 31%
where the time goes in v3:
time: 624 us; the launch traced here: 619 us
  Pallas kernels  303 us (49%)
  waiting for transfers between devices  195 us (31%)
  starting transfers between devices  67.9 us (11%)
  local copies, waits for them, and re-layouts  38.4 us (6%)
  other arithmetic  10.4 us (2%)
    ppermute x52, waiting for transfers between devices, swap(): lax.ppermute(x, axes, [(device(*at_), turn(*at_)) for at_ in everyone])  172 us
    pallas_call x3, Pallas kernels, run_mlp_back(): call(functools.partial(mlp_back_kernel, kinds, mode), (sds((rows, D), F32...  82.8 us
    pallas_call x3, Pallas kernels, run_attn_back(): call(functools.partial(attn_back_kernel, others), (sds((rows, D), BF), sd...  52.3 us
    ppermute x52, starting transfers between devices, swap(): lax.ppermute(x, axes, [(device(*at_), turn(*at_)) for at_ in everyone])  52 us
    pallas_call x3, Pallas kernels, run_mlp(): call(functools.partial(mlp_kernel, kinds), (sds((rows, D), F32), sds((NC,...  39 us
    pallas_call x3, Pallas kernels, run_qkv_back(): call(functools.partial(qkv_back_kernel, kinds, mode, others), (sds((rows,...  37 us
    unnamed x121, local copies, waits for them, and re-layouts  35.1 us
    pallas_call x3, Pallas kernels, run_attn(): call(functools.partial(attn_fwd_kernel, others), (sds((rows, D), BF), sds...  27.4 us
  transfers between devices with their start and end apart: 66, of which 33 were waited for; matrix products, arithmetic and copies ran while one was open for 1% of the time, Pallas kernels for 31%

profile of v3, /device:TPU:0, one launch (start us, length us, event | category | flops | bytes accessed | tf_op | source)
XLA Modules:
  0.0 619.3 jit_solution(12836745164189572277)
XLA Ops:
  14.3 13.3 %collective-permute-done = bf16[192,768]{1,0:T(8,128)(2,1)S(1)} collective-permute-done((bf16[192,768]{1,0:T(8,128)(2,1)S(1)}, bf16[192,768]{1,0:T(8,128)(2,1)S(1)}, u32[]{:S(2)}, u32[]{:S(2)}) %collective-permute-start) | collective-permute-done | bytes 294944 | tf_op jit(solution)/shard_map/ppermute | solution.py:1066
  31.9 16.7 %collective-permute-done.4 = bf16[2,192,768]{2,1,0:T(8,128)(2,1)S(1)} collective-permute-done((bf16[2,192,768]{2,1,0:T(8,128)(2,1)S(1)}, bf16[2,192,768]{2,1,0:T(8,128)(2,1)S(1)}, u32[]{:S(2)}, u32[]{:S(2)}) %collective-permute-start.4) | collective-permute-done | bytes 589856 | tf_op jit(solution)/shard_map/ppermute | solution.py:1066
  66.2 5.8 collective-permute-done.13
  73.5 9.7 %collective-permute-done.5 = bf16[2,192,768]{2,1,0:T(8,128)(2,1)} collective-permute-done((bf16[2,192,768]{2,1,0:T(8,128)(2,1)}, bf16[2,192,768]{2,1,0:T(8,128)(2,1)}, u32[]{:S(2)}, u32[]{:S(2)}) %collective-permute-start.5) | collective-permute-done | bytes 589856 | tf_op jit(solution)/shard_map/ppermute | solution.py:1066
  91.0 15.0 %collective-permute-done.6 = bf16[2,208,768]{2,1,0:T(8,128)(2,1)S(1)} collective-permute-done((bf16[2,208,768]{2,1,0:T(8,128)(2,1)S(1)}, bf16[2,208,768]{2,1,0:T(8,128)(2,1)S(1)}, u32[]{:S(2)}, u32[]{:S(2)}) %collective-permute-start.6) | collective-permute-done | bytes 639008 | tf_op jit(solution)/shard_map/ppermute | solution.py:1066
  106.2 5.7 collective-permute-done.9.other
  114.9 12.7 %collective-permute-done.3 = bf16[208,768]{1,0:T(8,128)(2,1)S(1)} collective-permute-done((bf16[208,768]{1,0:T(8,128)(2,1)S(1)}, bf16[208,768]{1,0:T(8,128)(2,1)S(1)}, u32[]{:S(2)}, u32[]{:S(2)}) %collective-permute-start.3) | collective-permute-done | bytes 319520 | tf_op jit(solution)/shard_map/ppermute | solution.py:1066
  128.4 14.6 %collective-permute-done.7 = bf16[2,208,768]{2,1,0:T(8,128)(2,1)S(1)} collective-permute-done((bf16[2,208,768]{2,1,0:T(8,128)(2,1)S(1)}, bf16[2,208,768]{2,1,0:T(8,128)(2,1)S(1)}, u32[]{:S(2)}, u32[]{:S(2)}) %collective-permute-start.7) | collective-permute-done | bytes 639008 | tf_op jit(solution)/shard_map/ppermute | solution.py:1066
  150.9 7.6 %collective-permute-done.16.rest_3_ = bf16[8,192,768]{2,1,0:T(8,128)(2,1)} collective-permute-done((bf16[8,192,768]{2,1,0:T(8,128)(2,1)S(1)}, bf16[8,192,768]{2,1,0:T(8,128)(2,1)}, u32[]{:S(2)}, u32[]{:S(2)}) %collective-permute-start.16) | collective-permute-done | bytes 2359328 | tf_op jit(solution)/shard_map/ppermute | solution.py:1066
  175.7 9.1 %attn.3 = (bf16[512,768]{1,0:T(8,128)(2,1)S(1)}, f32[2,16,256]{2,1,0:T(8,128)S(1)}) custom-call(s32[8]{0:T(128)S(1)} %stack.165.meta, bf16[512,768]{1,0:T(8,128)(2,1)S(1)} %copy-done.11, bf16[2,512,768]{2,1,0:T(8,128)(2,1)S(1)} %get-tuple-element.186.ko.vo, bf16[2,512,768]{2,1,0:T(8,128)(2,1)S(1)} %get-tuple-element.186.ko.vo, ...), custom_call_target="tpu_custom_call" | custom-call | flops 40265320 | bytes 1024 | tf_op jit(solution)/shard_map/attn/pallas_call | solution.py:765
  184.8 13.1 %mlp.3 = (f32[512,768]{1,0:T(8,128)S(1)}, bf16[4,512,768]{2,1,0:T(8,128)(2,1)}, f32[512,768]{1,0:T(8,128)S(1)}) custom-call(s32[8]{0:T(128)S(1)} %stack.165.meta, f32[512,768]{1,0:T(8,128)} %copy-done, bf16[512,768]{1,0:T(8,128)(2,1)S(1)} %get-tuple-element.187.mixed, bf16[8,208,768]{2,1,0:T(8,128)(2,1)} %assemble.4.rest_0_, ...), custom_call_target="tpu_custom_call" | custom-call | flops 54358180 | bytes 1024 | tf_op jit(solution)/shard_map/mlp/pallas_call | solution.py:796
  198.0 6.4 %collective-permute-done.21.rest_10_ = bf16[8,192,768]{2,1,0:T(8,128)(2,1)} collective-permute-done((bf16[8,192,768]{2,1,0:T(8,128)(2,1)}, bf16[8,192,768]{2,1,0:T(8,128)(2,1)}, u32[]{:S(2)}, u32[]{:S(2)}) %collective-permute-start.21) | collective-permute-done | bytes 2359328 | tf_op jit(solution)/shard_map/ppermute | solution.py:1066
  222.8 9.3 %attn.4 = (bf16[512,768]{1,0:T(8,128)(2,1)S(1)}, f32[2,16,256]{2,1,0:T(8,128)S(1)}) custom-call(s32[8]{0:T(128)S(1)} %stack.164.meta, bf16[512,768]{1,0:T(8,128)(2,1)S(1)} %get-tuple-element.194.q_ref, bf16[2,512,768]{2,1,0:T(8,128)(2,1)S(1)} %get-tuple-element.195.ko.vo, bf16[2,512,768]{2,1,0:T(8,128)(2,1)S(1)} %get-tuple-element.195.ko.vo, ...), custom_call_target="tpu_custom_call" | custom-call | flops 32212254720 | bytes 1024 | tf_op jit(solution)/shard_map/attn/pallas_call | solution.py:765
  233.6 12.9 %mlp.4 = (f32[512,768]{1,0:T(8,128)S(1)}, bf16[4,512,768]{2,1,0:T(8,128)(2,1)}, f32[512,768]{1,0:T(8,128)S(1)}) custom-call(s32[8]{0:T(128)S(1)} %stack.164.meta, f32[512,768]{1,0:T(8,128)} %copy-done.20, bf16[512,768]{1,0:T(8,128)(2,1)S(1)} %get-tuple-element.196.mixed, bf16[8,208,768]{2,1,0:T(8,128)(2,1)} %assemble.4.rest_0_, ...), custom_call_target="tpu_custom_call" | custom-call | flops 43486543872 | bytes 1024 | tf_op jit(solution)/shard_map/mlp/pallas_call | solution.py:796
  256.3 9.1 %attn.5 = (bf16[512,768]{1,0:T(8,128)(2,1)S(1)}, f32[2,16,256]{2,1,0:T(8,128)S(1)}) custom-call(s32[8]{0:T(128)S(1)} %stack.163.meta, bf16[512,768]{1,0:T(8,128)(2,1)S(1)} %get-tuple-element.198.q_ref, bf16[2,512,768]{2,1,0:T(8,128)(2,1)S(1)} %get-tuple-element.199.ko.vo, bf16[2,512,768]{2,1,0:T(8,128)(2,1)S(1)} %get-tuple-element.199.ko.vo, ...), custom_call_target="tpu_custom_call" | custom-call | flops 32212254720 | bytes 1024 | tf_op jit(solution)/shard_map/attn/pallas_call | solution.py:765
  265.4 12.9 %mlp.5 = (f32[512,768]{1,0:T(8,128)S(1)}, bf16[4,512,768]{2,1,0:T(8,128)(2,1)}, f32[512,768]{1,0:T(8,128)S(1)}) custom-call(s32[8]{0:T(128)S(1)} %stack.163.meta, f32[512,768]{1,0:T(8,128)} %copy-done.25, bf16[512,768]{1,0:T(8,128)(2,1)S(1)} %get-tuple-element.200.mixed, bf16[8,208,768]{2,1,0:T(8,128)(2,1)} %assemble.4.rest_0_, ...), custom_call_target="tpu_custom_call" | custom-call | flops 43486543872 | bytes 1024 | tf_op jit(solution)/shard_map/mlp/pallas_call | solution.py:796
  283.6 25.2 %mlp_back.3 = (f32[512,768]{1,0:T(8,128)}, bf16[512,768]{1,0:T(8,128)(2,1)S(1)}, f32[2,16,256]{2,1,0:T(8,128)S(1)}, f32[16,768]{1,0:T(8,128)S(1)}, bf16[8,2,384,...) custom-call(s32[8]{0:T(128)S(1)} %stack.163.meta, f32[2]{0:T(128)S(1)} %add_convert_fusion.keep_ref, ...), custom_call_target="tpu_custom_call" | custom-call | flops 86973087744 | bytes 1024 | tf_op jit(solution)/shard_map/mlp_back/pallas_call | solution.py:823
  309.8 17.6 %attn_back.3 = (bf16[512,768]{1,0:T(8,128)(2,1)S(1)}, bf16[2,512,768]{2,1,0:T(8,128)(2,1)S(1)}, bf16[1,2,512,768]{3,2,1,0:T(8,128)(2,1)}) custom-call(s32[8]{0:T(128)S(1)} %stack.163.meta, bf16[512,768]{1,0:T(8,128)(2,1)S(1)} %get-tuple-element.198.q_ref, bf16[2,512,768]{2,1,0:T(8,128)(2,1)} %copy-done.23, bf16[2,512,768]{2,1,0:T(8,128)(2,1)} %copy-done.23, ...), custom_call_target="tpu_custom_call" | custom-call | flops 80530636800 | bytes 1024 | tf_op jit(solution)/shard_map/attn_back/pallas_call | solution.py:848
  333.3 11.0 %qkv_back.3 = (f32[512,768]{1,0:T(8,128)S(1)}, bf16[8,2,160,768]{3,2,1,0:T(8,128)(2,1)}) custom-call(s32[8]{0:T(128)S(1)} %stack.163.meta, f32[2]{0:T(128)S(1)} %add_convert_fusion.keep_ref, f32[512,768]{1,0:T(8,128)S(1)} %copy-done.26, bf16[512,768]{1,0:T(8,128)(2,1)S(1)} %get-tuple-element.208.dq, bf16[2,512,768]{2,1,0:T(8,128)(2,1)} %copy-done.30, ...), custom_call_target="tpu_custom_call" | custom-call | flops 28991029248 | bytes 1024 | tf_op jit(solution)/shard_map/qkv_back/pallas_call | solution.py:875
  345.5 30.1 %mlp_back.4 = (f32[512,768]{1,0:T(8,128)}, bf16[512,768]{1,0:T(8,128)(2,1)S(1)}, f32[2,16,256]{2,1,0:T(8,128)S(1)}, f32[16,768]{1,0:T(8,128)S(1)}, bf16[8,432,76...) custom-call(s32[8]{0:T(128)S(1)} %stack.164.meta, ...), custom_call_target="tpu_custom_call" | custom-call | flops 86973087744 | bytes 1024 | tf_op jit(solution)/shard_map/mlp_back/pallas_call | solution.py:823
  375.8 17.3 %attn_back.4 = (bf16[512,768]{1,0:T(8,128)(2,1)S(1)}, bf16[2,512,768]{2,1,0:T(8,128)(2,1)S(1)}, bf16[1,2,512,768]{3,2,1,0:T(8,128)(2,1)}) custom-call(s32[8]{0:T(128)S(1)} %stack.164.meta, bf16[512,768]{1,0:T(8,128)(2,1)S(1)} %get-tuple-element.194.q_ref, bf16[2,512,768]{2,1,0:T(8,128)(2,1)} %copy-done.22, bf16[2,512,768]{2,1,0:T(8,128)(2,1)} %copy-done.22, ...), custom_call_target="tpu_custom_call" | custom-call | flops 80530636800 | bytes 1024 | tf_op jit(solution)/shard_map/attn_back/pallas_call | solution.py:848
  394.7 6.3 %add_cores.4 = (bf16[8,96,768]{2,1,0:T(8,128)(2,1)S(1)}, bf16[8,96,768]{2,1,0:T(8,128)(2,1)S(1)}, bf16[4,240,768]{2,1,0:T(8,128)(2,1)S(1)}, bf16[4,240,768]{2,1,0:T(8,128)(2,1)}) custom-call(s32[8]{0:T(128)S(1)} %stack.164.meta, bf16[8,432,768]{2,1,0:T(8,128)(2,1)} %get-tuple-element.223.mine, bf16[8,432,768]{2,1,0:T(8,128)(2,1)} %collective-permute-done.30.got), custom_call_target="tpu_custom_call" | custom-call | flops 86973087744 | bytes 1024 | tf_op jit(solution)/shard_map/add_cores/pallas_call | solution.py:920
  405.1 13.9 %qkv_back.4 = (f32[512,768]{1,0:T(8,128)S(1)}, bf16[8,160,768]{2,1,0:T(8,128)(2,1)}, bf16[8,160,768]{2,1,0:T(8,128)(2,1)}, bf16[8,2,160,768]{3,2,1,0:T(8,128)(2,1)}) custom-call(s32[8]{0:T(128)S(1)} %stack.164.meta, f32[2]{0:T(128)S(1)} %add_convert_fusion.keep_ref, f32[512,768]{1,0:T(8,128)S(1)} %copy-done.21, bf16[512,768]{1,0:T(8,128)(2,1)S(1)} %get-tuple-element.221.dq, ...), custom_call_target="tpu_custom_call" | custom-call | flops 28991029248 | bytes 1024 | tf_op jit(solution)/shard_map/qkv_back/pallas_call | solution.py:875
  420.2 27.4 %mlp_back.5 = (f32[512,768]{1,0:T(8,128)}, bf16[512,768]{1,0:T(8,128)(2,1)S(1)}, f32[2,16,256]{2,1,0:T(8,128)S(1)}, f32[16,768]{1,0:T(8,128)S(1)}, bf16[8,432,76...) custom-call(s32[8]{0:T(128)S(1)} %stack.165.meta, f32[2]{0:T(128)S(1)} %add_convert_fusion.keep_ref, f32[512,768]{1,0:T(8,128)} %copy-done.28, ...), custom_call_target="tpu_custom_call" | custom-call | flops 86973087744 | bytes 1024 | tf_op jit(solution)/shard_map/mlp_back/pallas_call | solution.py:823
  462.6 6.1 add_cores.6
  469.9 17.4 %attn_back.5 = (bf16[512,768]{1,0:T(8,128)(2,1)S(1)}, bf16[2,512,768]{2,1,0:T(8,128)(2,1)S(1)}, bf16[1,2,512,768]{3,2,1,0:T(8,128)(2,1)}) custom-call(s32[8]{0:T(128)S(1)} %stack.165.meta, bf16[512,768]{1,0:T(8,128)(2,1)S(1)} %copy-done.12, bf16[2,512,768]{2,1,0:T(8,128)(2,1)} %copy-done.2, bf16[2,512,768]{2,1,0:T(8,128)(2,1)} %copy-done.2, ...), custom_call_target="tpu_custom_call" | custom-call | flops 80530636800 | bytes 1024 | tf_op jit(solution)/shard_map/attn_back/pallas_call | solution.py:848
  497.6 12.1 %qkv_back.5 = (f32[512,768]{1,0:T(8,128)S(1)}, bf16[8,160,768]{2,1,0:T(8,128)(2,1)}, bf16[8,160,768]{2,1,0:T(8,128)(2,1)}) custom-call(s32[8]{0:T(128)S(1)} %stack.165.meta, f32[2]{0:T(128)S(1)} %add_convert_fusion.keep_ref, f32[512,768]{1,0:T(8,128)S(1)} %copy-done.1, bf16[512,768]{1,0:T(8,128)(2,1)S(1)} %get-tuple-element.253.dq, ...), custom_call_target="tpu_custom_call" | custom-call | flops 28991029248 | bytes 1024 | tf_op jit(solution)/shard_map/qkv_back/pallas_call | solution.py:875
  521.6 9.4 %collective-permute-done.46.refs_1_ = bf16[1,96,768]{2,1,0:T(8,128)(2,1)S(1)} collective-permute-done((bf16[1,96,768]{2,1,0:T(8,128)(2,1)S(1)}, bf16[1,96,768]{2,1,0:T(8,128)(2,1)S(1)}, u32[]{:S(2)}, u32[]{:S(2)}) %collective-permute-start.46) | collective-permute-done | bytes 147488 | tf_op jit(solution)/shard_map/ppermute | solution.py:1066
  531.7 6.9 %collective-permute-done.51.refs_3_ = bf16[4,240,768]{2,1,0:T(8,128)(2,1)S(1)} collective-permute-done((bf16[4,240,768]{2,1,0:T(8,128)(2,1)}, bf16[4,240,768]{2,1,0:T(8,128)(2,1)S(1)}, u32[]{:S(2)}, u32[]{:S(2)}) %collective-permute-start.51) | collective-permute-done | bytes 1474592 | tf_op jit(solution)/shard_map/ppermute | solution.py:1066
  547.5 15.1 %collective-permute-done.53.refs_1_ = bf16[1,80,768]{2,1,0:T(8,128)(2,1)S(1)} collective-permute-done((bf16[1,80,768]{2,1,0:T(8,128)(2,1)S(1)}, bf16[1,80,768]{2,1,0:T(8,128)(2,1)S(1)}, u32[]{:S(2)}, u32[]{:S(2)}) %collective-permute-start.53) | collective-permute-done | bytes 122912 | tf_op jit(solution)/shard_map/ppermute | solution.py:1066
  571.5 7.1 %collective-permute-done.58.refs_1_ = bf16[2,96,768]{2,1,0:T(8,128)(2,1)S(1)} collective-permute-done((bf16[2,96,768]{2,1,0:T(8,128)(2,1)S(1)}, bf16[2,96,768]{2,1,0:T(8,128)(2,1)S(1)}, u32[]{:S(2)}, u32[]{:S(2)}) %collective-permute-start.58) | collective-permute-done | bytes 294944 | tf_op jit(solution)/shard_map/ppermute | solution.py:1066
  604.9 5.6 collective-permute-done.41
  (288 shorter events, 212.1 us)
Async XLA Ops:
  10.2 17.4 %collective-permute-start = (bf16[192,768]{1,0:T(8,128)(2,1)S(1)}, bf16[192,768]{1,0:T(8,128)(2,1)S(1)}, u32[]{:S(2)}, u32[]{:S(2)}) collective-permute-start(bf16[192,768]{1,0:T(8,128)(2,1)S(1)} %get-tuple-element.170), channel_id=1, source_target_pairs={{0,16},{1,17},{2,18},{3,19},{4,20},{5,21},{6,22},{7,23},{8,24},{9,... | collective-permute-start | bytes 884744 | tf_op jit(solution)/shard_map/ppermute | solution.py:1066
  27.7 20.9 %collective-permute-start.4 = (bf16[2,192,768]{2,1,0:T(8,128)(2,1)S(1)}, bf16[2,192,768]{2,1,0:T(8,128)(2,1)S(1)}, u32[]{:S(2)}, u32[]{:S(2)}) collective-permute-start(bf16[2,192,768]{2,1,0:T(8,128)(2,1)S(1)} %get-tuple-element.337), channel_id=1, source_target_pairs={{0,8},{1,9},{2,10},{3,11},{4,12},{5,13},{6,14},{7,15},{8,0},{9,1},... | collective-permute-start | bytes 1769480 | tf_op jit(solution)/shard_map/ppermute | solution.py:1066
  28.5 30.6 %collective-permute-start.1 = (bf16[192,768]{1,0:T(8,128)(2,1)S(1)}, bf16[192,768]{1,0:T(8,128)(2,1)S(1)}, u32[]{:S(2)}, u32[]{:S(2)}) collective-permute-start(bf16[192,768]{1,0:T(8,128)(2,1)S(1)} %get-tuple-element.171), channel_id=1, source_target_pairs={{0,16},{1,17},{2,18},{3,19},{4,20},{5,21},{6,22},{7,23},{8,24},{9,... | collective-permute-start | bytes 884744 | tf_op jit(solution)/shard_map/ppermute | solution.py:1066
  48.8 35.8 %collective-permute-start.8 = (bf16[2,2,192,768]{3,2,1,0:T(8,128)(2,1)S(1)}, bf16[2,2,192,768]{3,2,1,0:T(8,128)(2,1)S(1)}, u32[]{:S(2)}, u32[]{:S(2)}) collective-permute-start(bf16[2,2,192,768]{3,2,1,0:T(8,128)(2,1)S(1)} %pad_maximum_fusion.2.mine), channel_id=1, source_target_pairs={{0,4},{1,5},{2,6},{3,7},{4,0},{5,1},{6,2},{7,3},{8,12},{9,13},{10,... | collective-permute-start | bytes 3538952 | tf_op jit(solution)/shard_map/ppermute | solution.py:1066
  60.7 22.5 %collective-permute-start.5 = (bf16[2,192,768]{2,1,0:T(8,128)(2,1)}, bf16[2,192,768]{2,1,0:T(8,128)(2,1)}, u32[]{:S(2)}, u32[]{:S(2)}) collective-permute-start(bf16[2,192,768]{2,1,0:T(8,128)(2,1)} %pad_maximum_fusion.7), channel_id=1, source_target_pairs={{0,8},{1,9},{2,10},{3,11},{4,12},{5,13},{6,14},{7,15},{8,0},{9,1},... | collective-permute-start | bytes 1769480 | tf_op jit(solution)/shard_map/ppermute | solution.py:1066
  63.6 27.3 %collective-permute-start.2 = (bf16[208,768]{1,0:T(8,128)(2,1)S(1)}, bf16[208,768]{1,0:T(8,128)(2,1)S(1)}, u32[]{:S(2)}, u32[]{:S(2)}) collective-permute-start(bf16[208,768]{1,0:T(8,128)(2,1)S(1)} %get-tuple-element.172), channel_id=1, source_target_pairs={{0,16},{1,17},{2,18},{3,19},{4,20},{5,21},{6,22},{7,23},{8,24},{9,... | collective-permute-start | bytes 958472 | tf_op jit(solution)/shard_map/ppermute | solution.py:1066
  84.6 27.2 %collective-permute-start.9 = (bf16[2,2,192,768]{3,2,1,0:T(8,128)(2,1)S(1)}, bf16[2,2,192,768]{3,2,1,0:T(8,128)(2,1)S(1)}, u32[]{:S(2)}, u32[]{:S(2)}) collective-permute-start(bf16[2,2,192,768]{3,2,1,0:T(8,128)(2,1)S(1)} %pad_maximum_fusion.3.mine), channel_id=1, source_target_pairs={{0,4},{1,5},{2,6},{3,7},{4,0},{5,1},{6,2},{7,3},{8,12},{9,13},{10,... | collective-permute-start | bytes 3538952 | tf_op jit(solution)/shard_map/ppermute | solution.py:1066
  90.5 59.9 %collective-permute-start.17 = (bf16[8,192,768]{2,1,0:T(8,128)(2,1)}, bf16[8,192,768]{2,1,0:T(8,128)(2,1)S(1)}, u32[]{:S(2)}, u32[]{:S(2)}) collective-permute-start(bf16[8,192,768]{2,1,0:T(8,128)(2,1)} %assemble.5.rest_2_), channel_id=1, source_target_pairs={{0,1},{1,0},{2,3},{3,2},{4,5},{5,4},{6,7},{7,6},{8,9},{9,8},{10,11... | collective-permute-start | bytes 7077896 | tf_op jit(solution)/shard_map/ppermute | solution.py:1066
  111.8 32.3 %collective-permute-start.10 = (bf16[2,2,208,768]{3,2,1,0:T(8,128)(2,1)S(1)}, bf16[2,2,208,768]{3,2,1,0:T(8,128)(2,1)S(1)}, u32[]{:S(2)}, u32[]{:S(2)}) collective-permute-start(bf16[2,2,208,768]{3,2,1,0:T(8,128)(2,1)S(1)} %pad_maximum_fusion.mine), channel_id=1, source_target_pairs={{0,4},{1,5},{2,6},{3,7},{4,0},{5,1},{6,2},{7,3},{8,12},{9,13},{10,... | collective-permute-start | bytes 3833864 | tf_op jit(solution)/shard_map/ppermute | solution.py:1066
  147.1 16.6 %collective-permute-start.11 = (bf16[8,208,768]{2,1,0:T(8,128)(2,1)}, bf16[8,208,768]{2,1,0:T(8,128)(2,1)S(1)}, u32[]{:S(2)}, u32[]{:S(2)}) collective-permute-start(bf16[8,208,768]{2,1,0:T(8,128)(2,1)} %assemble.4.rest_0_), channel_id=1, source_target_pairs={{0,2},{1,3},{2,0},{3,1},{4,6},{5,7},{6,4},{7,5},{8,10},{9,11},{10,... | collective-permute-start | bytes 7667720 | tf_op jit(solution)/shard_map/ppermute | solution.py:1066
  150.9 53.6 %collective-permute-start.21 = (bf16[8,192,768]{2,1,0:T(8,128)(2,1)}, bf16[8,192,768]{2,1,0:T(8,128)(2,1)}, u32[]{:S(2)}, u32[]{:S(2)}) collective-permute-start(bf16[8,192,768]{2,1,0:T(8,128)(2,1)} %assemble.6.rest_8_), channel_id=1, source_target_pairs={{0,1},{1,0},{2,3},{3,2},{4,5},{5,4},{6,7},{7,6},{8,9},{9,8},{10,11... | collective-permute-start | bytes 7077896 | tf_op jit(solution)/shard_map/ppermute | solution.py:1066
  171.2 33.2 %collective-permute-start.22 = (bf16[2,2,208,768]{3,2,1,0:T(8,128)(2,1)}, bf16[2,2,208,768]{3,2,1,0:T(8,128)(2,1)S(1)}, u32[]{:S(2)}, u32[]{:S(2)}) collective-permute-start(bf16[2,2,208,768]{3,2,1,0:T(8,128)(2,1)} %pad_maximum_fusion.1.mine), channel_id=1, source_target_pairs={{0,4},{1,5},{2,6},{3,7},{4,0},{5,1},{6,2},{7,3},{8,12},{9,13},{10,... | collective-permute-start | bytes 3833864 | tf_op jit(solution)/shard_map/ppermute | solution.py:1066
  279.5 29.4 %collective-permute-start.27 = (bf16[256,768]{1,0:T(8,128)(2,1)S(1)}, bf16[256,768]{1,0:T(8,128)(2,1)S(1)}, u32[]{:S(2)}, u32[]{:S(2)}) collective-permute-start(bf16[256,768]{1,0:T(8,128)(2,1)S(1)} %get-tuple-element.326), channel_id=1, source_target_pairs={{0,0},{2,1},{1,2},{3,3},{4,4},{6,5},{5,6},{7,7},{8,8},{10,9},{9,10... | collective-permute-start | bytes 1179656 | tf_op jit(solution)/shard_map/ppermute | solution.py:1031
  280.6 28.3 %collective-permute-start.28 = (bf16[256,768]{1,0:T(8,128)(2,1)S(1)}, bf16[256,768]{1,0:T(8,128)(2,1)S(1)}, u32[]{:S(2)}, u32[]{:S(2)}) collective-permute-start(bf16[256,768]{1,0:T(8,128)(2,1)S(1)} %get-tuple-element.327), channel_id=1, source_target_pairs={{2,0},{0,1},{3,2},{1,3},{6,4},{4,5},{7,6},{5,7},{10,8},{8,9},{11,1... | collective-permute-start | bytes 1179656 | tf_op jit(solution)/shard_map/ppermute | solution.py:1032
  375.6 19.1 %collective-permute-start.30 = (bf16[8,432,768]{2,1,0:T(8,128)(2,1)}, bf16[8,432,768]{2,1,0:T(8,128)(2,1)}, u32[]{:S(2)}, u32[]{:S(2)}) collective-permute-start(bf16[8,432,768]{2,1,0:T(8,128)(2,1)} %get-tuple-element.224), channel_id=1, source_target_pairs={{0,2},{1,3},{2,0},{3,1},{4,6},{5,7},{6,4},{7,5},{8,10},{9,11},{10,... | collective-permute-start | bytes 15925256 | tf_op jit(solution)/shard_map/ppermute | solution.py:1066
  402.3 50.9 %collective-permute-start.33 = (bf16[8,96,768]{2,1,0:T(8,128)(2,1)S(1)}, bf16[8,96,768]{2,1,0:T(8,128)(2,1)S(1)}, u32[]{:S(2)}, u32[]{:S(2)}) collective-permute-start(bf16[8,96,768]{2,1,0:T(8,128)(2,1)S(1)} %get-tuple-element.242), channel_id=1, source_target_pairs={{0,1},{1,0},{2,3},{3,2},{4,5},{5,4},{6,7},{7,6},{8,9},{9,8},{10,11... | collective-permute-start | bytes 3538952 | tf_op jit(solution)/shard_map/ppermute | solution.py:1066
  402.4 50.8 %collective-permute-start.34 = (bf16[4,240,768]{2,1,0:T(8,128)(2,1)}, bf16[4,240,768]{2,1,0:T(8,128)(2,1)S(1)}, u32[]{:S(2)}, u32[]{:S(2)}) collective-permute-start(bf16[4,240,768]{2,1,0:T(8,128)(2,1)} %get-tuple-element.244), channel_id=1, source_target_pairs={{0,4},{1,5},{2,6},{3,7},{4,0},{5,1},{6,2},{7,3},{8,12},{9,13},{10,... | collective-permute-start | bytes 4423688 | tf_op jit(solution)/shard_map/ppermute | solution.py:1066
  420.2 28.0 %collective-permute-start.32 = (bf16[8,160,768]{2,1,0:T(8,128)(2,1)}, bf16[8,160,768]{2,1,0:T(8,128)(2,1)S(1)}, u32[]{:S(2)}, u32[]{:S(2)}) collective-permute-start(bf16[8,160,768]{2,1,0:T(8,128)(2,1)} %get-tuple-element.239), channel_id=1, source_target_pairs={{0,2},{1,3},{2,0},{3,1},{4,6},{5,7},{6,4},{7,5},{8,10},{9,11},{10,... | collective-permute-start | bytes 5898248 | tf_op jit(solution)/shard_map/ppermute | solution.py:1066
  458.4 28.9 %collective-permute-start.36 = (bf16[4,96,768]{2,1,0:T(8,128)(2,1)S(1)}, bf16[4,96,768]{2,1,0:T(8,128)(2,1)S(1)}, u32[]{:S(2)}, u32[]{:S(2)}) collective-permute-start(bf16[4,96,768]{2,1,0:T(8,128)(2,1)S(1)} %get-tuple-element.255), channel_id=1, source_target_pairs={{0,4},{1,5},{2,6},{3,7},{4,0},{5,1},{6,2},{7,3},{8,12},{9,13},{10,... | collective-permute-start | bytes 1769480 | tf_op jit(solution)/shard_map/ppermute | solution.py:1066
  458.9 28.4 %collective-permute-start.37 = (bf16[2,240,768]{2,1,0:T(8,128)(2,1)S(1)}, bf16[2,240,768]{2,1,0:T(8,128)(2,1)}, u32[]{:S(2)}, u32[]{:S(2)}) collective-permute-start(bf16[2,240,768]{2,1,0:T(8,128)(2,1)S(1)} %get-tuple-element.257), channel_id=1, source_target_pairs={{0,8},{1,9},{2,10},{3,11},{4,12},{5,13},{6,14},{7,15},{8,0},{9,1},... | collective-permute-start | bytes 2211848 | tf_op jit(solution)/shard_map/ppermute | solution.py:1066
  460.6 26.7 %collective-permute-start.38 = (bf16[8,80,768]{2,1,0:T(8,128)(2,1)S(1)}, bf16[8,80,768]{2,1,0:T(8,128)(2,1)}, u32[]{:S(2)}, u32[]{:S(2)}) collective-permute-start(bf16[8,80,768]{2,1,0:T(8,128)(2,1)S(1)} %get-tuple-element.258), channel_id=1, source_target_pairs={{0,1},{1,0},{2,3},{3,2},{4,5},{5,4},{6,7},{7,6},{8,9},{9,8},{10,11... | collective-permute-start | bytes 2949128 | tf_op jit(solution)/shard_map/ppermute | solution.py:1066
  490.6 19.0 %collective-permute-start.42 = (bf16[2,96,768]{2,1,0:T(8,128)(2,1)S(1)}, bf16[2,96,768]{2,1,0:T(8,128)(2,1)S(1)}, u32[]{:S(2)}, u32[]{:S(2)}) collective-permute-start(bf16[2,96,768]{2,1,0:T(8,128)(2,1)S(1)} %get-tuple-element.268), channel_id=1, source_target_pairs={{0,8},{1,9},{2,10},{3,11},{4,12},{5,13},{6,14},{7,15},{8,0},{9,1},... | collective-permute-start | bytes 884744 | tf_op jit(solution)/shard_map/ppermute | solution.py:1066
  491.0 19.9 %collective-permute-start.43 = (bf16[1,240,768]{2,1,0:T(8,128)(2,1)S(1)}, bf16[1,240,768]{2,1,0:T(8,128)(2,1)S(1)}, u32[]{:S(2)}, u32[]{:S(2)}) collective-permute-start(bf16[1,240,768]{2,1,0:T(8,128)(2,1)S(1)} %get-tuple-element.270), channel_id=1, source_target_pairs={{0,16},{1,17},{2,18},{3,19},{4,20},{5,21},{6,22},{7,23},{8,24},{9,... | collective-permute-start | bytes 1105928 | tf_op jit(solution)/shard_map/ppermute | solution.py:1066
  494.4 16.5 %collective-permute-start.44 = (bf16[4,80,768]{2,1,0:T(8,128)(2,1)S(1)}, bf16[4,80,768]{2,1,0:T(8,128)(2,1)S(1)}, u32[]{:S(2)}, u32[]{:S(2)}) collective-permute-start(bf16[4,80,768]{2,1,0:T(8,128)(2,1)S(1)} %get-tuple-element.272), channel_id=1, source_target_pairs={{0,4},{1,5},{2,6},{3,7},{4,0},{5,1},{6,2},{7,3},{8,12},{9,13},{10,... | collective-permute-start | bytes 1474568 | tf_op jit(solution)/shard_map/ppermute | solution.py:1066
  495.9 35.8 %collective-permute-start.50 = (bf16[8,96,768]{2,1,0:T(8,128)(2,1)S(1)}, bf16[8,96,768]{2,1,0:T(8,128)(2,1)}, u32[]{:S(2)}, u32[]{:S(2)}) collective-permute-start(bf16[8,96,768]{2,1,0:T(8,128)(2,1)S(1)} %get-tuple-element.285), channel_id=1, source_target_pairs={{0,1},{1,0},{2,3},{3,2},{4,5},{5,4},{6,7},{7,6},{8,9},{9,8},{10,11... | collective-permute-start | bytes 3538952 | tf_op jit(solution)/shard_map/ppermute | solution.py:1066
  497.0 41.6 %collective-permute-start.51 = (bf16[4,240,768]{2,1,0:T(8,128)(2,1)}, bf16[4,240,768]{2,1,0:T(8,128)(2,1)S(1)}, u32[]{:S(2)}, u32[]{:S(2)}) collective-permute-start(bf16[4,240,768]{2,1,0:T(8,128)(2,1)} %get-tuple-element.287), channel_id=1, source_target_pairs={{0,4},{1,5},{2,6},{3,7},{4,0},{5,1},{6,2},{7,3},{8,12},{9,13},{10,... | collective-permute-start | bytes 4423688 | tf_op jit(solution)/shard_map/ppermute | solution.py:1066
  517.8 28.1 %collective-permute-start.52 = (bf16[8,80,768]{2,1,0:T(8,128)(2,1)S(1)}, bf16[8,80,768]{2,1,0:T(8,128)(2,1)S(1)}, u32[]{:S(2)}, u32[]{:S(2)}) collective-permute-start(bf16[8,80,768]{2,1,0:T(8,128)(2,1)S(1)} %get-tuple-element.290), channel_id=1, source_target_pairs={{0,1},{1,0},{2,3},{3,2},{4,5},{5,4},{6,7},{7,6},{8,9},{9,8},{10,11... | collective-permute-start | bytes 2949128 | tf_op jit(solution)/shard_map/ppermute | solution.py:1066
  542.6 20.1 %collective-permute-start.54 = (bf16[4,96,768]{2,1,0:T(8,128)(2,1)S(1)}, bf16[4,96,768]{2,1,0:T(8,128)(2,1)S(1)}, u32[]{:S(2)}, u32[]{:S(2)}) collective-permute-start(bf16[4,96,768]{2,1,0:T(8,128)(2,1)S(1)} %get-tuple-element.295), channel_id=1, source_target_pairs={{0,4},{1,5},{2,6},{3,7},{4,0},{5,1},{6,2},{7,3},{8,12},{9,13},{10,... | collective-permute-start | bytes 1769480 | tf_op jit(solution)/shard_map/ppermute | solution.py:1066
  544.2 19.4 %collective-permute-start.55 = (bf16[2,240,768]{2,1,0:T(8,128)(2,1)S(1)}, bf16[2,240,768]{2,1,0:T(8,128)(2,1)S(1)}, u32[]{:S(2)}, u32[]{:S(2)}) collective-permute-start(bf16[2,240,768]{2,1,0:T(8,128)(2,1)S(1)} %get-tuple-element.297), channel_id=1, source_target_pairs={{0,8},{1,9},{2,10},{3,11},{4,12},{5,13},{6,14},{7,15},{8,0},{9,1},... | collective-permute-start | bytes 2211848 | tf_op jit(solution)/shard_map/ppermute | solution.py:1066
  546.7 24.2 %collective-permute-start.57 = (bf16[4,80,768]{2,1,0:T(8,128)(2,1)S(1)}, bf16[4,80,768]{2,1,0:T(8,128)(2,1)S(1)}, u32[]{:S(2)}, u32[]{:S(2)}) collective-permute-start(bf16[4,80,768]{2,1,0:T(8,128)(2,1)S(1)} %get-tuple-element.300), channel_id=1, source_target_pairs={{0,4},{1,5},{2,6},{3,7},{4,0},{5,1},{6,2},{7,3},{8,12},{9,13},{10,... | collective-permute-start | bytes 1474568 | tf_op jit(solution)/shard_map/ppermute | solution.py:1066
  566.8 16.7 %collective-permute-start.59 = (bf16[1,240,768]{2,1,0:T(8,128)(2,1)S(1)}, bf16[1,240,768]{2,1,0:T(8,128)(2,1)S(1)}, u32[]{:S(2)}, u32[]{:S(2)}) collective-permute-start(bf16[1,240,768]{2,1,0:T(8,128)(2,1)S(1)} %get-tuple-element.306), channel_id=1, source_target_pairs={{0,16},{1,17},{2,18},{3,19},{4,20},{5,21},{6,22},{7,23},{8,24},{9,... | collective-permute-start | bytes 1105928 | tf_op jit(solution)/shard_map/ppermute | solution.py:1066
  586.0 25.4 %collective-permute-start.49 = (bf16[240,768]{1,0:T(8,128)(2,1)S(1)}, bf16[240,768]{1,0:T(8,128)(2,1)S(1)}, u32[]{:S(2)}, u32[]{:S(2)}) collective-permute-start(bf16[240,768]{1,0:T(8,128)(2,1)S(1)} %get-tuple-element.283.refs_2_), channel_id=1, source_target_pairs={{0,1},{1,0},{2,3},{3,2},{4,5},{5,4},{6,7},{7,6},{8,9},{9,8},{10,11... | collective-permute-start | bytes 1105928 | tf_op jit(solution)/shard_map/ppermute | solution.py:1066
  (94 other events, 764.1 us)
